TPU v7x, 256 devices: a whole 4x4x8 slice. The times are simulated.
256 devices in a mesh: pool: 8 (over z_hi, core), tp: 32 (over x, z_lo, y).
Axes of the slice: x: 4, y: 4, z: 8 (z_hi: 4, z_lo: 2; z = z_hi * 2 + z_lo), core: 2. Of those that a mesh axis runs over, the one named last changes fastest.
Arguments:
- hidden: bfloat16 [2048, 8192], P(('pool', 'tp'))
- norm_gain: float32 [8192], replicated, may hold values from 0.1 to 1.9
- start_positions: int32 [32], P('pool'), may hold values from 256 to 4095
- draft_lengths: int32 [32], P('pool'), may hold values from 1 to 64
- query_weight: bfloat16 [8192, 8192], P(None, 'tp'), may hold values from -0.0625 to 0.0625
- w_keyvalue: bfloat16 [32, 8192, 256], P('tp'), as said below
- output_weight: bfloat16 [8192, 8192], P('tp'), may hold values from -0.0625 to 0.0625
- kv_cache: bfloat16 [32, 256, 32, 256], P('pool', None, 'tp'), as said below
- a_query: bfloat16 [8192, 64], P(('tp', 'pool')), may hold values from -0.0625 to 0.0625
- b_query: bfloat16 [64, 8192], P(None, ('tp', 'pool')), may hold values from -0.75 to 0.75
- a_key: bfloat16 [8192, 64], P(('tp', 'pool')), may hold values from -0.0625 to 0.0625
- b_key: bfloat16 [64, 1024], P(None, ('tp', 'pool')), may hold values from -0.75 to 0.75
- a_value: bfloat16 [8192, 64], P(('tp', 'pool')), may hold values from -0.0625 to 0.0625
- b_value: bfloat16 [64, 1024], P(None, ('tp', 'pool')), may hold values from -0.75 to 0.75
- a_out: bfloat16 [8192, 64], P(('tp', 'pool')), may hold values from -0.0625 to 0.0625
- b_out: bfloat16 [64, 8192], P(None, ('tp', 'pool')), may hold values from -0.75 to 0.75
Outputs:
- updated: bfloat16 [2048, 8192], P(('pool', 'tp'))
Inputs may be any that keep to these rules, and one draw needn't show every extreme that they name: `w_keyvalue`: blocks t and u along the first dimension are equal when t // 4 == u // 4; block t holds the key columns (first 128) and value columns of key-value head t // 4. `kv_cache`: entries t and u along the third dimension are equal when t // 4 == u // 4; the first 128 entries are the key, the rest the value of key-value head t // 4.
All inputs are finite; a program needn't handle non-finite values.
Results may differ from a plain program's by a relative error of at most 0.02.
Values may be sent and summed in bfloat16 or wider, within the bound.
No kernel may reach another device: no remote copies, remote signals or barrier semaphores. Data moves between devices by JAX's collectives and lax.ppermute only.
A program may use at most 128 MiB of HBM per device.

v0:
```python
import math

import jax
import jax.numpy as jnp
from jax import lax
from jax.experimental import pallas as pl
from jax.experimental.pallas import tpu as pltpu
from jax.sharding import Mesh, PartitionSpec as P

VERIFY = 64
HEAD_DIM = 128

adapter_scale = 1.0
rope_base = 1000000.0
norm_eps = 1e-06

AXES = ("zh", "core", "x", "zl", "y")
TP = ("x", "zl", "y")
POOL = ("zh", "core")
SPOTS = [
    (zh, core, x, zl, y)
    for zh in range(4)
    for core in range(2)
    for x in range(4)
    for zl in range(2)
    for y in range(4)
]


def turns(places, width):
    half_dim = width // 2
    freqs = jnp.exp(
        jnp.arange(half_dim, dtype=jnp.float32) * (-2.0 * math.log(rope_base) / width)
    )
    angles = places.astype(jnp.float32)[:, None] * freqs[None, :]
    cosine, sine = jnp.cos(angles), jnp.sin(angles)
    return jnp.concatenate([cosine, cosine], axis=1), jnp.concatenate([-sine, sine], axis=1)


def dot32(left, right):
    return jnp.dot(left, right, preferred_element_type=jnp.float32)


def permute(block, source_to_target):
    return lax.ppermute(block, AXES, source_to_target)


def pairs(move):
    place = {spot: number for number, spot in enumerate(SPOTS)}
    return [(place[spot], place[move(*spot)]) for spot in SPOTS]


def last_shift(s):
    return pairs(
        lambda h, c, x, z, y: (h, c, (x + s) % 4, z, y) if c == 0 else (h, c, x, z, (y + s) % 4)
    )


def middle_shift(s):
    return pairs(
        lambda h, c, x, z, y: (h, c, x, z, (y + s) % 4) if c == 0 else (h, c, (x + s) % 4, z, y)
    )


def z_swap():
    return pairs(lambda h, c, x, z, y: (h, c, x, 1 - z, y))


def core_swap():
    return pairs(lambda h, c, x, z, y: (h, 1 - c, x, z, y))


def placed(blocks, here):
    count = len(blocks)
    out = jnp.zeros((count,) + blocks[0].shape, blocks[0].dtype)
    for s, block in enumerate(blocks):
        out = lax.dynamic_update_index_in_dim(out, block, (here - s) % count, 0)
    return out


def pick(blocks, index):
    return lax.dynamic_index_in_dim(blocks, index, 0, keepdims=False)


def spread(block, count, groups):
    return lax.all_to_all(
        jnp.broadcast_to(block[None], (count,) + block.shape),
        AXES,
        0,
        0,
        axis_index_groups=groups,
    )


def groups_of(key, order):
    found = {}
    for number, spot in enumerate(SPOTS):
        found.setdefault(key(*spot), []).append((order(*spot), number))
    return [[number for _, number in sorted(group)] for group in found.values()]


def pool_groups():
    return groups_of(lambda h, c, x, z, y: (x, z, y), lambda h, c, x, z, y: (h, c))


def last_groups():
    return groups_of(
        lambda h, c, x, z, y: (h, c, z, y) if c == 0 else (h, c, x, z),
        lambda h, c, x, z, y: x if c == 0 else y,
    )


def row_groups():
    return groups_of(
        lambda h, c, x, z, y: (h, c),
        lambda h, c, x, z, y: (x, z, y) if c == 0 else (y, z, x),
    )


def spec_smem():
    return pl.BlockSpec(memory_space=pltpu.SMEM)


def project_kernel(
    eight_ref, one_ref, left_ref, right_ref, three_ref, query_ref, pair_ref, out_ref, total
):
    step = pl.program_id(0)
    steps = pl.num_programs(0)

    @pl.when(step == 0)
    def _():
        total[...] = jnp.zeros_like(total)

    def add(two_ref):
        rows = jnp.concatenate(
            [eight_ref[...], one_ref[...], two_ref[...], three_ref[...]], axis=0
        )
        width = query_ref.shape[1]
        total[:, :width] += jnp.dot(rows, query_ref[...], preferred_element_type=jnp.float32)
        total[:, width:] += jnp.dot(rows, pair_ref[...], preferred_element_type=jnp.float32)

    @pl.when(step < steps // 2)
    def _():
        add(left_ref)

    @pl.when(step >= steps // 2)
    def _():
        add(right_ref)

    @pl.when(step == steps - 1)
    def _():
        out_ref[...] = total[...]


def project_rows(eight, one, left_2, right_2, three, query_weight, pair_weight):
    tile = 1024
    steps = eight.shape[1] // tile
    width = query_weight.shape[1]
    whole = pl.BlockSpec((64, tile), lambda j: (0, j))
    return pl.pallas_call(
        project_kernel,
        grid=(steps,),
        in_specs=[
            whole,
            whole,
            pl.BlockSpec((64, tile), lambda j: (0, jnp.minimum(j, steps // 2 - 1))),
            pl.BlockSpec((64, tile), lambda j: (0, jnp.maximum(j - steps // 2, 0))),
            whole,
            pl.BlockSpec((tile, width), lambda j: (j, 0)),
            pl.BlockSpec((tile, width), lambda j: (j, 0)),
        ],
        out_specs=pl.BlockSpec((256, 2 * width), lambda j: (0, 0)),
        out_shape=jax.ShapeDtypeStruct((256, 2 * width), jnp.float32),
        scratch_shapes=[pltpu.VMEM((256, 2 * width), jnp.float32)],
        compiler_params=pltpu.CompilerParams(vmem_limit_bytes=24 * 2**20),
        cost_estimate=pl.CostEstimate(
            flops=2 * 256 * 512 * 8192, bytes_accessed=12 * 2**20, transcendentals=0
        ),
    )(eight, one, left_2, right_2, three, query_weight, pair_weight)


def outer(left, right):
    return lax.dot_general(
        left, right, (((1,), (1,)), ((), ())), preferred_element_type=jnp.float32
    )


def attend_kernel(
    spot_ref,
    lengths_ref,
    frozen_ref,
    parts_ref,
    query_up_ref,
    key_up_ref,
    value_up_ref,
    cosine_ref,
    sine_ref,
    cache_ref,
    down_ref,
    ahead_ref,
    inner_ref,
    rows,
    found,
):
    half = jnp.bfloat16
    first_core = spot_ref[0] == 0
    last = spot_ref[1]
    for s in range(4):
        k = lax.rem(last - s + 4, 4)
        inner = parts_ref[k, 0].astype(jnp.float32)
        for part in range(1, 8):
            inner = inner + parts_ref[k, part].astype(jnp.float32)
        inner = inner.astype(half)
        frozen = frozen_ref[64 * s : 64 * s + 64]
        rows[k, :, :256] = frozen[:, :256] + adapter_scale * outer(inner[:, :64], query_up_ref[...])
        rows[k, :, 256:384] = frozen[:, 256:384] + adapter_scale * outer(
            inner[:, 64:128], key_up_ref[...]
        )
        rows[k, :, 384:] = frozen[:, 384:] + adapter_scale * outer(
            inner[:, 128:192], value_up_ref[...]
        )

    def place(count, axis):
        at = lax.broadcasted_iota(jnp.int32, (count, 64) if axis == 0 else (64, count), axis)
        return ((at >> 3) & 1) * 32 + ((at >> 4) & 3) * 8 + (at & 7)

    scale = 1.0 / math.sqrt(HEAD_DIM)
    for sequence in range(4):
        length = lengths_ref[sequence]
        across = jnp.concatenate(
            [rows[y, 16 * sequence : 16 * sequence + 16] for y in range(4)], axis=0
        )
        mine = jnp.where(first_core, rows[sequence], across)
        cosine = cosine_ref[64 * sequence : 64 * sequence + 64]
        sine = sine_ref[64 * sequence : 64 * sequence + 64]

        def rotated(value):
            return (value * cosine + pltpu.roll(value, 64, 1) * sine).astype(half)

        query = jnp.concatenate([rotated(mine[:, :128]), rotated(mine[:, 128:256])], axis=0)
        keys = rotated(mine[:, 256:384])
        values = mine[:, 384:].astype(half)
        cache_scores = outer(query, cache_ref[sequence, :, :128]) * scale
        draft_scores = outer(query, keys) * scale
        of_row = place(128, 0)
        of_column = lax.broadcasted_iota(jnp.int32, (128, 64), 1)
        of_column = ((of_column >> 3) & 1) * 32 + (of_column >> 4) * 8 + (of_column & 7)
        allowed = (of_column <= of_row) & (of_column < length)
        draft_scores = jnp.where(allowed, draft_scores, -1e30)
        highest = jnp.maximum(
            jnp.max(cache_scores, axis=1, keepdims=True),
            jnp.max(draft_scores, axis=1, keepdims=True),
        )
        cache_powers = jnp.exp(cache_scores - highest)
        draft_powers = jnp.exp(draft_scores - highest)
        bottom = jnp.sum(cache_powers, axis=1, keepdims=True) + jnp.sum(
            draft_powers, axis=1, keepdims=True
        )
        mixed = jnp.dot(
            (cache_powers / bottom).astype(half),
            cache_ref[sequence, :, 128:],
            preferred_element_type=jnp.float32,
        ) + jnp.dot(
            (draft_powers / bottom).astype(half), values, preferred_element_type=jnp.float32
        )
        row = lax.broadcasted_iota(jnp.int32, (128, 128), 0)
        row = ((row >> 3) & 1) * 32 + ((row >> 4) & 3) * 8 + (row & 7)
        mixed = (mixed * (row < length).astype(jnp.float32)).astype(half)
        found[sequence] = jnp.concatenate([mixed[:64], mixed[64:]], axis=1)

    for s in range(4):
        k = lax.rem(last + s, 4)
        at = pl.ds(pl.multiple_of(16 * k, 16), 16)
        across = jnp.concatenate([found[sequence, at] for sequence in range(4)], axis=0)
        block = jnp.where(first_core, found[k], across)
        ahead_ref[64 * s : 64 * s + 64] = block
        inner = jnp.dot(block, down_ref[...], preferred_element_type=jnp.float32).astype(half)
        for copy in range(8):
            inner_ref[8 * k + copy] = inner


def attend_rows(spot, lengths, frozen, parts, ups, cosine, sine, cache, down):
    operands = (frozen, parts, *ups, cosine, sine, cache, down)
    return pl.pallas_call(
        attend_kernel,
        in_specs=[spec_smem(), spec_smem()]
        + [pl.BlockSpec(memory_space=pltpu.VMEM)] * len(operands),
        out_specs=[pl.BlockSpec(memory_space=pltpu.VMEM)] * 2,
        out_shape=[
            jax.ShapeDtypeStruct((256, 256), jnp.bfloat16),
            jax.ShapeDtypeStruct((32, 64, 64), jnp.bfloat16),
        ],
        scratch_shapes=[
            pltpu.VMEM((4, 64, 512), jnp.float32),
            pltpu.VMEM((4, 64, 256), jnp.bfloat16),
        ],
        compiler_params=pltpu.CompilerParams(vmem_limit_bytes=24 * 2**20),
        cost_estimate=pl.CostEstimate(
            flops=2 * 512 * 320 * 256, bytes_accessed=4 * 2**20, transcendentals=512 * 320
        ),
    )(spot, lengths, *operands)


def sum_kernel(
    spot_ref,
    own_ref,
    plus_ref,
    minus_ref,
    left_ref,
    right_ref,
    parts_ref,
    up_ref,
    mine_ref,
    one_ref,
    two_ref,
    three_ref,
    total,
    inner,
):
    step = pl.program_id(0)
    at_left = step < pl.num_programs(0) // 2
    tile = own_ref.shape[1]

    @pl.when(step == 0)
    def _():
        found = parts_ref[0].astype(jnp.float32)
        for part in range(1, 32):
            found = found + parts_ref[part].astype(jnp.float32)
        inner[...] = found.astype(jnp.bfloat16)

    own = own_ref[...].astype(jnp.float32)

    @pl.when(at_left)
    def _():
        total[...] = own + minus_ref[...].astype(jnp.float32) + left_ref[...].astype(jnp.float32)

    @pl.when(jnp.logical_not(at_left))
    def _():
        total[...] = own + plus_ref[...].astype(jnp.float32) + right_ref[...].astype(jnp.float32)

    for k in range(4):
        column = spot_ref[1 + k] * 256

        @pl.when(column // tile == step)
        def _():
            at = pl.ds(pl.multiple_of(lax.rem(column, tile), 256), 256)
            total[:, at] += adapter_scale * outer(inner[...], up_ref[k])

    middle = spot_ref[0]
    for s, ref in enumerate((mine_ref, one_ref, two_ref, three_ref)):
        at = pl.ds(pl.multiple_of(16 * lax.rem(middle + s, 4), 16), 16)
        ref[...] = total[at, :].astype(ref.dtype)


def sum_rows(spot, own, plus, minus, left, right, parts, up_factor):
    tile = 1024
    steps = own.shape[1] // tile
    width = own.shape[1]
    last_left = steps // 2 - 1
    whole = pl.BlockSpec((64, tile), lambda j: (0, j))
    out = pl.BlockSpec((16, tile), lambda j: (0, j))
    return pl.pallas_call(
        sum_kernel,
        grid=(steps,),
        in_specs=[
            spec_smem(),
            whole,
            pl.BlockSpec((64, tile), lambda j: (0, jnp.maximum(j, steps // 2))),
            pl.BlockSpec((64, tile), lambda j: (0, jnp.minimum(j, last_left))),
            pl.BlockSpec((64, tile), lambda j: (0, jnp.minimum(j, last_left))),
            pl.BlockSpec((64, tile), lambda j: (0, jnp.maximum(j - steps // 2, 0))),
            pl.BlockSpec(parts.shape, lambda j: (0, 0, 0)),
            pl.BlockSpec(up_factor.shape, lambda j: (0, 0, 0)),
        ],
        out_specs=[out] * 4,
        out_shape=[jax.ShapeDtypeStruct((16, width), jnp.float32)]
        + [jax.ShapeDtypeStruct((16, width), jnp.bfloat16)] * 3,
        scratch_shapes=[
            pltpu.VMEM((64, tile), jnp.float32),
            pltpu.VMEM((64, 64), jnp.bfloat16),
        ],
        compiler_params=pltpu.CompilerParams(vmem_limit_bytes=16 * 2**20),
        cost_estimate=pl.CostEstimate(
            flops=2 * 64 * 64 * 1024, bytes_accessed=5 * 2**20, transcendentals=0
        ),
    )(spot, own, plus, minus, left, right, parts, up_factor)


def out_kernel(rows_ref, weight_ref, own_ref, plus_ref, minus_ref, left_ref, right_ref):
    at_left = pl.program_id(0) < pl.num_programs(0) // 2
    part = jnp.dot(rows_ref[...], weight_ref[...], preferred_element_type=jnp.float32)
    part = part.astype(jnp.bfloat16)
    own_ref[...] = part[:64]

    @pl.when(at_left)
    def _():
        left_ref[...] = part[64:128]
        plus_ref[...] = part[128:192]
        minus_ref[...] = part[192:]

    @pl.when(jnp.logical_not(at_left))
    def _():
        plus_ref[...] = part[64:128]
        minus_ref[...] = part[128:192]
        right_ref[...] = part[192:]


def out_pieces(rows, weight):
    tile = 2048
    depth, width = weight.shape
    steps = width // tile
    whole = pl.BlockSpec((64, tile), lambda j: (0, j))
    left = pl.BlockSpec((64, tile), lambda j: (0, jnp.minimum(j, steps // 2 - 1)))
    right = pl.BlockSpec((64, tile), lambda j: (0, jnp.maximum(j - steps // 2, 0)))
    return pl.pallas_call(
        out_kernel,
        grid=(steps,),
        in_specs=[
            pl.BlockSpec(rows.shape, lambda j: (0, 0)),
            pl.BlockSpec((depth, tile), lambda j: (0, j)),
        ],
        out_specs=[whole, whole, whole, left, right],
        out_shape=[jax.ShapeDtypeStruct((64, width), jnp.bfloat16)] * 3
        + [jax.ShapeDtypeStruct((64, width // 2), jnp.bfloat16)] * 2,
        compiler_params=pltpu.CompilerParams(vmem_limit_bytes=28 * 2**20),
        cost_estimate=pl.CostEstimate(
            flops=2 * 256 * 256 * 8192, bytes_accessed=8 * 2**20, transcendentals=0
        ),
    )(rows, weight)


def shards(
    hidden,
    norm_gain,
    start_positions,
    draft_lengths,
    query_weight,
    w_keyvalue,
    output_weight,
    kv_cache,
    a_query,
    b_query,
    a_key,
    b_key,
    a_value,
    b_value,
    a_out,
    b_out,
):
    zh, core, x, zl, y = (lax.axis_index(name) for name in AXES)
    first_core = core == 0
    last = jnp.where(first_core, x, y)
    middle = jnp.where(first_core, y, x)
    half = jnp.bfloat16

    def tp_index(k):
        return jnp.where(first_core, k * 8 + zl * 4 + y, x * 8 + zl * 4 + k)

    row_float = hidden.astype(jnp.float32)
    normed = (
        row_float
        * lax.rsqrt(jnp.mean(row_float * row_float, axis=-1, keepdims=True) + norm_eps)
        * norm_gain
    ).astype(half)

    packed = jnp.concatenate(
        [
            jnp.concatenate([a_query, a_key], axis=1),
            jnp.concatenate([a_value, a_out], axis=1),
            jnp.concatenate([b_query.T, b_out.T], axis=1),
            jnp.concatenate([b_key.T, b_value.T], axis=1),
            jnp.zeros((4, 128), half),
        ],
        axis=0,
    )
    packed, _ = lax.optimization_barrier((packed, normed))
    pooled = spread(packed, 8, pool_groups())
    wide = spread(pooled, 4, last_groups())
    pair = placed([normed, permute(normed, z_swap())], zl).reshape(16, 8192)
    met = [pair] + [permute(pair, middle_shift(s)) for s in (1, 2, 3)]
    eight = placed(met, middle).reshape(64, 8192)
    from_1 = permute(eight, last_shift(1))
    from_3 = permute(eight, last_shift(3))

    down_first = wide[:, :, 0:32].reshape(1024, 128)
    down_second = wide[:, :, 32:64].reshape(1024, 128)
    out_up = wide[:, :, 64:96, 64:].reshape(4, 256, 64)
    down_out = pooled[:, 32:64, 64:].reshape(256, 64)
    query_up = pooled[:, 64:96, :64].reshape(256, 64)
    narrow = wide[:, :, 96:100].reshape(128, 128)
    narrow = jnp.where(first_core, permute(narrow, core_swap()), narrow)
    key_up = narrow[:, :64]
    value_up = narrow[:, 64:]

    down = jnp.concatenate([down_first, down_second[:, :64]], axis=1).reshape(4, 256, 192)
    down_padded = jnp.zeros((8192, 192), half)
    for k in range(4):
        down_padded = lax.dynamic_update_slice_in_dim(down_padded, down[k], tp_index(k) * 256, 0)
    inner = dot32(eight, down_padded).astype(half)
    from_1, from_3, inner = lax.optimization_barrier((from_1, from_3, inner))
    left_2 = permute(from_1[:, :4096], last_shift(1))
    right_2 = permute(from_3[:, 4096:], last_shift(3))
    parts = spread(inner, 32, row_groups()).reshape(4, 8, 64, 192)
    frozen = project_rows(
        eight, from_1, left_2, right_2, from_3, query_weight, w_keyvalue.reshape(8192, 256)
    )
    draft_places = (
        jnp.arange(VERIFY, dtype=jnp.int32).reshape(2, 4, 8).transpose(1, 0, 2).reshape(VERIFY)
    )
    places = (start_positions[:, None] + draft_places[None, :]).reshape(-1)
    cosine, sine = turns(places, HEAD_DIM)
    spot = jnp.stack([core, last]).astype(jnp.int32)
    ahead, out_inner = attend_rows(
        spot,
        draft_lengths,
        frozen,
        parts,
        (query_up, key_up, value_up),
        cosine,
        sine,
        kv_cache.reshape(4, 256, 256),
        down_out,
    )

    own, plus, minus, left_1, right_3 = out_pieces(ahead, output_weight)
    got_plus = permute(plus, last_shift(1))
    got_minus = permute(minus, last_shift(3))
    out_inner, _ = lax.optimization_barrier((out_inner, plus))
    out_parts = lax.all_to_all(out_inner, AXES, 0, 0, axis_index_groups=row_groups())
    got_plus, got_minus = lax.optimization_barrier((got_plus, got_minus))
    got_left_1 = permute(left_1 + got_plus[:, :4096], last_shift(1))
    got_right_3 = permute(right_3 + got_minus[:, 4096:], last_shift(3))

    spot = jnp.stack([middle] + [tp_index(k) for k in range(4)]).astype(jnp.int32)
    total, *sent = sum_rows(
        spot, own, got_plus, got_minus, got_left_1, got_right_3, out_parts, out_up
    )
    for s, block in zip((1, 2, 3), sent):
        total = total + permute(block, middle_shift(s)).astype(jnp.float32)
    total = total.reshape(2, 8, 8192)
    branch = pick(total, zl) + permute(pick(total, 1 - zl).astype(half), z_swap()).astype(
        jnp.float32
    )
    return (row_float + branch).astype(half)


def solution(mesh):
    fine = Mesh(mesh.devices.reshape(4, 2, 4, 2, 4), AXES)
    both = ("x", "zl", "y", "zh", "core")
    in_specs = (
        P(AXES, None),
        P(),
        P(POOL),
        P(POOL),
        P(None, TP),
        P(TP, None, None),
        P(TP, None),
        P(POOL, None, TP, None),
        P(both, None),
        P(None, both),
        P(both, None),
        P(None, both),
        P(both, None),
        P(None, both),
        P(both, None),
        P(None, both),
    )
    out_specs = P(AXES, None)
    return jax.shard_map(shards, mesh=fine, in_specs=in_specs, out_specs=out_specs, check_vma=False)
```

profile of v0, /device:TPU:64, one launch (start us, length us, event | category | flops | bytes accessed | tf_op | source)
XLA Modules:
  0.0 163.0 jit_solution(11766238285609005542)
XLA Ops:
  2.2 2.0 %collective-permute-start = (bf16[8,8192]{1,0:T(8,128)(2,1)S(1)}, bf16[8,8192]{1,0:T(8,128)(2,1)S(1)}, u32[]{:S(2)}, u32[]{:S(2)}) collective-permute-start(bf16[8,8192]{1,0:T(8,128)(2,1)S(1)} %get-tuple-element.42), channel_id=1, source_target_pairs={{0,4},{1,5},{2,6},{3,7},{4,0},{5,1},{6,2},{7,3},{8,12},{9,13},{10,... | collective-permute-start | bytes 393224 | tf_op jit(solution)/shard_map/ppermute | solution.py:45
  7.3 7.2 %all-to-all-start = ((bf16[8,104,128]{2,1,0:T(8,128)(2,1)}), bf16[8,104,128]{2,1,0:T(8,128)(2,1)S(1)}, u32[]{:S(2)}, u32[]{:S(2)}) async-start(bf16[8,104,128]{2,1,0:T(8,128)(2,1)} %broadcast_in_dim.65), calls=%async_computation | async-start | bytes 425984 | tf_op jit(solution)/shard_map/all_to_all | solution.py:86
  14.7 1.7 %collective-permute-start.1 = (bf16[16,8192]{1,0:T(8,128)(2,1)S(1)}, bf16[16,8192]{1,0:T(8,128)(2,1)S(1)}, u32[]{:S(2)}, u32[]{:S(2)}) collective-permute-start(bf16[16,8192]{1,0:T(8,128)(2,1)S(1)} %bitcast.63), channel_id=1, source_target_pairs={{0,1},{1,2},{2,3},{3,0},{4,5},{5,6},{6,7},{7,4},{8,9},{9,10},{10,1... | collective-permute-start | bytes 786440 | tf_op jit(solution)/shard_map/ppermute | solution.py:45
  16.3 2.9 %collective-permute-start.2 = (bf16[16,8192]{1,0:T(8,128)(2,1)S(1)}, bf16[16,8192]{1,0:T(8,128)(2,1)S(1)}, u32[]{:S(2)}, u32[]{:S(2)}) collective-permute-start(bf16[16,8192]{1,0:T(8,128)(2,1)S(1)} %bitcast.64), channel_id=1, source_target_pairs={{0,2},{1,3},{2,0},{3,1},{4,6},{5,7},{6,4},{7,5},{8,10},{9,11},{10,... | collective-permute-start | bytes 786440 | tf_op jit(solution)/shard_map/ppermute | solution.py:45
  19.2 1.3 collective-permute-start.3
  20.7 3.2 %all-to-all-done = bf16[8,104,128]{2,1,0:T(8,128)(2,1)S(1)} async-done(((bf16[8,104,128]{2,1,0:T(8,128)(2,1)}), bf16[8,104,128]{2,1,0:T(8,128)(2,1)S(1)}, u32[]{:S(2)}, u32[]{:S(2)}) %all-to-all-start) | async-done | bytes 213024 | tf_op jit(solution)/shard_map/all_to_all | solution.py:86
  24.9 4.3 %all-to-all-start.1 = ((bf16[4,8,104,128]{3,2,1,0:T(8,128)(2,1)}), bf16[4,8,104,128]{3,2,1,0:T(8,128)(2,1)}, u32[]{:S(2)}, u32[]{:S(2)}) async-start(bf16[4,8,104,128]{3,2,1,0:T(8,128)(2,1)} %broadcast_in_dim.66), calls=%async_computation.1 | async-start | bytes 1703936 | tf_op jit(solution)/shard_map/all_to_all | solution.py:86
  29.3 2.1 %collective-permute-start.4 = (bf16[64,8192]{1,0:T(8,128)(2,1)S(1)}, bf16[64,8192]{1,0:T(8,128)(2,1)S(1)}, u32[]{:S(2)}, u32[]{:S(2)}) collective-permute-start(bf16[64,8192]{1,0:T(8,128)(2,1)S(1)} %bitcast.45), channel_id=1, source_target_pairs={{0,8},{1,9},{2,10},{3,11},{4,12},{5,13},{6,14},{7,15},{8,16},{9,17... | collective-permute-start | bytes 3145736 | tf_op jit(solution)/shard_map/ppermute | solution.py:45
  31.4 1.3 collective-permute-start.5
  32.7 6.5 %all-to-all-done.1 = bf16[4,8,104,128]{3,2,1,0:T(8,128)(2,1)} async-done(((bf16[4,8,104,128]{3,2,1,0:T(8,128)(2,1)}), bf16[4,8,104,128]{3,2,1,0:T(8,128)(2,1)}, u32[]{:S(2)}, u32[]{:S(2)}) %all-to-all-start.1) | async-done | bytes 852000 | tf_op jit(solution)/shard_map/all_to_all | solution.py:86
  41.5 8.4 %collective-permute-done.4.one_ref = bf16[64,8192]{1,0:T(8,128)(2,1)S(1)} collective-permute-done((bf16[64,8192]{1,0:T(8,128)(2,1)S(1)}, bf16[64,8192]{1,0:T(8,128)(2,1)S(1)}, u32[]{:S(2)}, u32[]{:S(2)}) %collective-permute-start.4) | collective-permute-done | bytes 1048608 | tf_op jit(solution)/shard_map/ppermute | solution.py:45
  51.3 5.8 %all-to-all-start.2 = ((bf16[32,64,192]{2,1,0:T(8,128)(2,1)}), bf16[32,64,192]{2,1,0:T(8,128)(2,1)S(1)}, u32[]{:S(2)}, u32[]{:S(2)}) async-start(bf16[32,64,192]{2,1,0:T(8,128)(2,1)} %broadcast_in_dim.67), calls=%async_computation.2 | async-start | bytes 2097152 | tf_op jit(solution)/shard_map/all_to_all | solution.py:86
  59.0 1.9 %collective-permute-start.6 = (bf16[64,4096]{1,0:T(8,128)(2,1)S(1)}, bf16[64,4096]{1,0:T(8,128)(2,1)S(1)}, u32[]{:S(2)}, u32[]{:S(2)}) collective-permute-start(bf16[64,4096]{1,0:T(8,128)(2,1)S(1)} %slice.62), channel_id=1, source_target_pairs={{0,8},{1,9},{2,10},{3,11},{4,12},{5,13},{6,14},{7,15},{8,16},{9,17... | collective-permute-start | bytes 1572872 | tf_op jit(solution)/shard_map/ppermute | solution.py:45
  62.0 1.7 %collective-permute-start.7 = (bf16[64,4096]{1,0:T(8,128)(2,1)S(1)}, bf16[64,4096]{1,0:T(8,128)(2,1)S(1)}, u32[]{:S(2)}, u32[]{:S(2)}) collective-permute-start(bf16[64,4096]{1,0:T(8,128)(2,1)S(1)} %slice.63), channel_id=1, source_target_pairs={{0,24},{1,25},{2,26},{3,27},{4,28},{5,29},{6,30},{7,31},{8,0},{9,1... | collective-permute-start | bytes 1572872 | tf_op jit(solution)/shard_map/ppermute | solution.py:45
  65.4 10.3 %collective-permute-done.6.left_ref = bf16[64,4096]{1,0:T(8,128)(2,1)S(1)} collective-permute-done((bf16[64,4096]{1,0:T(8,128)(2,1)S(1)}, bf16[64,4096]{1,0:T(8,128)(2,1)S(1)}, u32[]{:S(2)}, u32[]{:S(2)}) %collective-permute-start.6) | collective-permute-done | bytes 524320 | tf_op jit(solution)/shard_map/ppermute | solution.py:45
  75.7 2.2 %copy-done = bf16[8192,256]{1,0:T(8,128)(2,1)S(1)} copy-done((bf16[8192,256]{1,0:T(8,128)(2,1)S(1)}, bf16[8192,256]{1,0:T(8,128)(2,1)}, u32[]{:S(2)}) %copy-start) | copy-done | bytes 4194328
  77.9 2.2 %copy-done.1 = bf16[1,8192,256]{2,1,0:T(8,128)(2,1)S(1)} copy-done((bf16[1,8192,256]{2,1,0:T(8,128)(2,1)S(1)}, bf16[1,8192,256]{2,1,0:T(8,128)(2,1)}, u32[]{:S(2)}) %copy-start.1) | copy-done | bytes 4194328
  80.1 4.3 %shard_map.154.frozen_ref = f32[256,512]{1,0:T(8,128)S(1)} custom-call(bf16[64,8192]{1,0:T(8,128)(2,1)S(1)} %bitcast.48, bf16[64,8192]{1,0:T(8,128)(2,1)S(1)} %collective-permute-done.4.one_ref, bf16[64,4096]{1,0:T(8,128)(2,1)S(1)} %collective-permute-done.6.left_ref, bf16[64,4096]{1,0:T(8,128)(2,1)S(1)} %collective-permute-done.7.right_ref, ...), custom_call_target="tpu_custom_call" | custom-call | flops 2147483648 | bytes 12582912 | tf_op jit(solution)/shard_map/pallas_call | solution.py:160
  88.8 2.9 %shard_map.155 = (bf16[256,256]{1,0:T(8,128)(2,1)S(1)}, bf16[32,64,64]{2,1,0:T(8,128)(2,1)S(1)}) custom-call(s32[2]{0:T(128)S(1)} %pad_add_fusion.spot_ref, s32[4]{0:T(128)S(1)} %copy-done.15, f32[256,512]{1,0:T(8,128)S(1)} %copy-done.6, bf16[4,8,64,192]{3,2,1,0:T(8,128)(2,1)S(1)} %bitcast.50, bf16[256,64]{1,0:T(8,128)(2,1)S(1)} %bitcast.54, ...), custom_call_target="tpu_custom_call" | custom-call | flops 83886080 | bytes 4194304 | tf_op jit(solution)/shard_map/pallas_call | solution.py:284
  92.5 2.2 %copy-done.2 = bf16[256,8192]{1,0:T(8,128)(2,1)S(1)} copy-done((bf16[256,8192]{1,0:T(8,128)(2,1)S(1)}, bf16[256,8192]{1,0:T(8,128)(2,1)}, u32[]{:S(2)}) %copy-start.2) | copy-done | bytes 4194328
  94.7 2.8 %shard_map.156 = (bf16[64,8192]{1,0:T(8,128)(2,1)S(1)}, bf16[64,8192]{1,0:T(8,128)(2,1)S(1)}, bf16[64,8192]{1,0:T(8,128)(2,1)S(1)}, bf16[64,4096]{1,0:T(8,128)(2,1)S(1)}, bf16[64,4096]{1,0:T(8,128)(2,1)S(1)}) custom-call(bf16[256,256]{1,0:T(8,128)(2,1)S(1)} %get-tuple-element.27.rows_ref, bf16[256,8192]{1,0:T(8,128)(2,1)S(1)} %copy-done.2), custom_call_target="tpu_custom_call" | custom-call | flops 1073741824 | bytes 8388608 | tf_op jit(solution)/shard_map/pallas_call | solution.py:415
  100.5 12.8 %collective-permute-done.10.minus_ref = bf16[64,8192]{1,0:T(8,128)(2,1)S(1)} collective-permute-done((bf16[64,8192]{1,0:T(8,128)(2,1)S(1)}, bf16[64,8192]{1,0:T(8,128)(2,1)S(1)}, u32[]{:S(2)}, u32[]{:S(2)}) %collective-permute-start.10) | collective-permute-done | bytes 1048608 | tf_op jit(solution)/shard_map/ppermute | solution.py:45
  113.2 2.1 %collective-permute-done.9.plus_ref = bf16[64,8192]{1,0:T(8,128)(2,1)S(1)} collective-permute-done((bf16[64,8192]{1,0:T(8,128)(2,1)S(1)}, bf16[64,8192]{1,0:T(8,128)(2,1)S(1)}, u32[]{:S(2)}, u32[]{:S(2)}) %collective-permute-start.9) | collective-permute-done | bytes 1048608 | tf_op jit(solution)/shard_map/ppermute | solution.py:45
  117.1 2.0 %collective-permute-start.11 = (bf16[64,4096]{1,0:T(8,128)(2,1)}, bf16[64,4096]{1,0:T(8,128)(2,1)}, u32[]{:S(2)}, u32[]{:S(2)}) collective-permute-start(bf16[64,4096]{1,0:T(8,128)(2,1)} %slice_add_fusion.1), channel_id=1, source_target_pairs={{0,8},{1,9},{2,10},{3,11},{4,12},{5,13},{6,14},{7,15},{8,16},{9,17... | collective-permute-start | bytes 1572872 | tf_op jit(solution)/shard_map/ppermute | solution.py:45
  120.2 6.5 %all-to-all-start.3 = ((bf16[32,2,2048]{2,1,0:T(2,128)(2,1)}), bf16[32,2,2048]{2,1,0:T(2,128)(2,1)}, u32[]{:S(2)}, u32[]{:S(2)}) async-start(bf16[32,2,2048]{2,1,0:T(2,128)(2,1)} %reshape.148), calls=%async_computation.3 | async-start | bytes 524288 | tf_op jit(solution)/shard_map/all_to_all | solution.py:529
  128.0 7.9 %all-to-all-done.3 = bf16[32,2,2048]{2,1,0:T(2,128)(2,1)} async-done(((bf16[32,2,2048]{2,1,0:T(2,128)(2,1)}), bf16[32,2,2048]{2,1,0:T(2,128)(2,1)}, u32[]{:S(2)}, u32[]{:S(2)}) %all-to-all-start.3) | async-done | bytes 262176 | tf_op jit(solution)/shard_map/all_to_all | solution.py:529
  135.9 1.3 reshape.149.parts_ref
  138.5 5.3 %shard_map.157 = (f32[16,8192]{1,0:T(8,128)S(1)}, bf16[16,8192]{1,0:T(8,128)(2,1)}, bf16[16,8192]{1,0:T(8,128)(2,1)}, bf16[16,8192]{1,0:T(8,128)(2,1)}) custom-call(s32[5]{0:T(128)S(1)} %stack.32.spot_ref, bf16[64,8192]{1,0:T(8,128)(2,1)S(1)} %copy-done.8, bf16[64,8192]{1,0:T(8,128)(2,1)S(1)} %collective-permute-done.9.plus_ref, ...), custom_call_target="tpu_custom_call" | custom-call | flops 8388608 | bytes 5242880 | tf_op jit(solution)/shard_map/pallas_call | solution.py:362
  145.5 1.5 collective-permute-start.14
  147.0 1.8 %collective-permute-start.15 = (bf16[16,8192]{1,0:T(8,128)(2,1)}, bf16[16,8192]{1,0:T(8,128)(2,1)S(1)}, u32[]{:S(2)}, u32[]{:S(2)}) collective-permute-start(bf16[16,8192]{1,0:T(8,128)(2,1)} %get-tuple-element.40), channel_id=1, source_target_pairs={{0,3},{1,0},{2,1},{3,2},{4,7},{5,4},{6,5},{7,6},{8,11},{9,8},{10,9... | collective-permute-start | bytes 786440 | tf_op jit(solution)/shard_map/ppermute | solution.py:45
  148.8 6.4 %collective-permute-done.13 = bf16[16,8192]{1,0:T(8,128)(2,1)S(1)} collective-permute-done((bf16[16,8192]{1,0:T(8,128)(2,1)}, bf16[16,8192]{1,0:T(8,128)(2,1)S(1)}, u32[]{:S(2)}, u32[]{:S(2)}) %collective-permute-start.13) | collective-permute-done | bytes 262176 | tf_op jit(solution)/shard_map/ppermute | solution.py:45
  158.3 4.0 %collective-permute-done.16 = bf16[8,8192]{1,0:T(8,128)(2,1)S(1)} collective-permute-done((bf16[8,8192]{1,0:T(8,128)(2,1)S(1)}, bf16[8,8192]{1,0:T(8,128)(2,1)S(1)}, u32[]{:S(2)}, u32[]{:S(2)}) %collective-permute-start.16) | collective-permute-done | bytes 131104 | tf_op jit(solution)/shard_map/ppermute | solution.py:45
  (100 shorter events, 33.9 us)
Async XLA Ops:
  2.2 12.5 %collective-permute-start = (bf16[8,8192]{1,0:T(8,128)(2,1)S(1)}, bf16[8,8192]{1,0:T(8,128)(2,1)S(1)}, u32[]{:S(2)}, u32[]{:S(2)}) collective-permute-start(bf16[8,8192]{1,0:T(8,128)(2,1)S(1)} %get-tuple-element.42), channel_id=1, source_target_pairs={{0,4},{1,5},{2,6},{3,7},{4,0},{5,1},{6,2},{7,3},{8,12},{9,13},{10,... | collective-permute-start | bytes 393224 | tf_op jit(solution)/shard_map/ppermute | solution.py:45
  7.3 16.5 %all-to-all-start = ((bf16[8,104,128]{2,1,0:T(8,128)(2,1)}), bf16[8,104,128]{2,1,0:T(8,128)(2,1)S(1)}, u32[]{:S(2)}, u32[]{:S(2)}) async-start(bf16[8,104,128]{2,1,0:T(8,128)(2,1)} %broadcast_in_dim.65), calls=%async_computation | async-start | bytes 425984 | tf_op jit(solution)/shard_map/all_to_all | solution.py:86
  14.7 14.5 %collective-permute-start.1 = (bf16[16,8192]{1,0:T(8,128)(2,1)S(1)}, bf16[16,8192]{1,0:T(8,128)(2,1)S(1)}, u32[]{:S(2)}, u32[]{:S(2)}) collective-permute-start(bf16[16,8192]{1,0:T(8,128)(2,1)S(1)} %bitcast.63), channel_id=1, source_target_pairs={{0,1},{1,2},{2,3},{3,0},{4,5},{5,6},{6,7},{7,4},{8,9},{9,10},{10,1... | collective-permute-start | bytes 786440 | tf_op jit(solution)/shard_map/ppermute | solution.py:45
  16.3 12.9 %collective-permute-start.2 = (bf16[16,8192]{1,0:T(8,128)(2,1)S(1)}, bf16[16,8192]{1,0:T(8,128)(2,1)S(1)}, u32[]{:S(2)}, u32[]{:S(2)}) collective-permute-start(bf16[16,8192]{1,0:T(8,128)(2,1)S(1)} %bitcast.64), channel_id=1, source_target_pairs={{0,2},{1,3},{2,0},{3,1},{4,6},{5,7},{6,4},{7,5},{8,10},{9,11},{10,... | collective-permute-start | bytes 786440 | tf_op jit(solution)/shard_map/ppermute | solution.py:45
  19.2 10.0 %collective-permute-start.3 = (bf16[16,8192]{1,0:T(8,128)(2,1)S(1)}, bf16[16,8192]{1,0:T(8,128)(2,1)S(1)}, u32[]{:S(2)}, u32[]{:S(2)}) collective-permute-start(bf16[16,8192]{1,0:T(8,128)(2,1)S(1)} %bitcast.65), channel_id=1, source_target_pairs={{0,3},{1,0},{2,1},{3,2},{4,7},{5,4},{6,5},{7,6},{8,11},{9,8},{10,9... | collective-permute-start | bytes 786440 | tf_op jit(solution)/shard_map/ppermute | solution.py:45
  23.8 5.4 %copy-start.16 = (bf16[8,104,128]{2,1,0:T(8,128)(2,1)}, bf16[8,104,128]{2,1,0:T(8,128)(2,1)S(1)}, u32[]{:S(2)}) copy-start(bf16[8,104,128]{2,1,0:T(8,128)(2,1)S(1)} %all-to-all-done) | copy-start | bytes 638980
  24.9 14.3 %all-to-all-start.1 = ((bf16[4,8,104,128]{3,2,1,0:T(8,128)(2,1)}), bf16[4,8,104,128]{3,2,1,0:T(8,128)(2,1)}, u32[]{:S(2)}, u32[]{:S(2)}) async-start(bf16[4,8,104,128]{3,2,1,0:T(8,128)(2,1)} %broadcast_in_dim.66), calls=%async_computation.1 | async-start | bytes 1703936 | tf_op jit(solution)/shard_map/all_to_all | solution.py:86
  29.3 20.7 %collective-permute-start.4 = (bf16[64,8192]{1,0:T(8,128)(2,1)S(1)}, bf16[64,8192]{1,0:T(8,128)(2,1)S(1)}, u32[]{:S(2)}, u32[]{:S(2)}) collective-permute-start(bf16[64,8192]{1,0:T(8,128)(2,1)S(1)} %bitcast.45), channel_id=1, source_target_pairs={{0,8},{1,9},{2,10},{3,11},{4,12},{5,13},{6,14},{7,15},{8,16},{9,17... | collective-permute-start | bytes 3145736 | tf_op jit(solution)/shard_map/ppermute | solution.py:45
  31.4 18.6 %collective-permute-start.5 = (bf16[64,8192]{1,0:T(8,128)(2,1)S(1)}, bf16[64,8192]{1,0:T(8,128)(2,1)S(1)}, u32[]{:S(2)}, u32[]{:S(2)}) collective-permute-start(bf16[64,8192]{1,0:T(8,128)(2,1)S(1)} %bitcast.46), channel_id=1, source_target_pairs={{0,24},{1,25},{2,26},{3,27},{4,28},{5,29},{6,30},{7,31},{8,0},{9,1... | collective-permute-start | bytes 3145736 | tf_op jit(solution)/shard_map/ppermute | solution.py:45
  40.7 16.4 %copy-start.18 = (s32[4]{0:T(128)S(1)}, s32[4]{0:T(128)}, u32[]{:S(2)}) copy-start(s32[4]{0:T(128)} %param.18) | copy-start | bytes 52
  50.0 1.3 copy-start.3
  51.3 33.9 %all-to-all-start.2 = ((bf16[32,64,192]{2,1,0:T(8,128)(2,1)}), bf16[32,64,192]{2,1,0:T(8,128)(2,1)S(1)}, u32[]{:S(2)}, u32[]{:S(2)}) async-start(bf16[32,64,192]{2,1,0:T(8,128)(2,1)} %broadcast_in_dim.67), calls=%async_computation.2 | async-start | bytes 2097152 | tf_op jit(solution)/shard_map/all_to_all | solution.py:86
  57.3 18.5 %copy-start.4 = (bf16[64,8192]{1,0:T(8,128)(2,1)S(1)}, bf16[64,8192]{1,0:T(8,128)(2,1)}, u32[]{:S(2)}) copy-start(bf16[64,8192]{1,0:T(8,128)(2,1)} %copy-done.3) | copy-start | bytes 3145732
  58.9 5.8 %collective-permute-start.8 = (bf16[128,128]{1,0:T(8,128)(2,1)S(1)}, bf16[128,128]{1,0:T(8,128)(2,1)S(1)}, u32[]{:S(2)}, u32[]{:S(2)}) collective-permute-start(bf16[128,128]{1,0:T(8,128)(2,1)S(1)} %bitcast.66), channel_id=1, source_target_pairs={{0,32},{1,33},{2,34},{3,35},{4,36},{5,37},{6,38},{7,39},{8,40},{9,... | collective-permute-start | bytes 98312 | tf_op jit(solution)/shard_map/ppermute | solution.py:45
  59.0 16.7 %collective-permute-start.6 = (bf16[64,4096]{1,0:T(8,128)(2,1)S(1)}, bf16[64,4096]{1,0:T(8,128)(2,1)S(1)}, u32[]{:S(2)}, u32[]{:S(2)}) collective-permute-start(bf16[64,4096]{1,0:T(8,128)(2,1)S(1)} %slice.62), channel_id=1, source_target_pairs={{0,8},{1,9},{2,10},{3,11},{4,12},{5,13},{6,14},{7,15},{8,16},{9,17... | collective-permute-start | bytes 1572872 | tf_op jit(solution)/shard_map/ppermute | solution.py:45
  62.0 13.7 %collective-permute-start.7 = (bf16[64,4096]{1,0:T(8,128)(2,1)S(1)}, bf16[64,4096]{1,0:T(8,128)(2,1)S(1)}, u32[]{:S(2)}, u32[]{:S(2)}) collective-permute-start(bf16[64,4096]{1,0:T(8,128)(2,1)S(1)} %slice.63), channel_id=1, source_target_pairs={{0,24},{1,25},{2,26},{3,27},{4,28},{5,29},{6,30},{7,31},{8,0},{9,1... | collective-permute-start | bytes 1572872 | tf_op jit(solution)/shard_map/ppermute | solution.py:45
  75.7 2.2 %copy-start = (bf16[8192,256]{1,0:T(8,128)(2,1)S(1)}, bf16[8192,256]{1,0:T(8,128)(2,1)}, u32[]{:S(2)}) copy-start(bf16[8192,256]{1,0:T(8,128)(2,1)} %query_ref.1) | copy-start | bytes 12582916
  77.9 2.2 %copy-start.1 = (bf16[1,8192,256]{2,1,0:T(8,128)(2,1)S(1)}, bf16[1,8192,256]{2,1,0:T(8,128)(2,1)}, u32[]{:S(2)}) copy-start(bf16[1,8192,256]{2,1,0:T(8,128)(2,1)} %param.21) | copy-start | bytes 12582916
  80.1 5.1 %copy-start.15 = (s32[4]{0:T(128)S(1)}, s32[4]{0:T(128)}, u32[]{:S(2)}) copy-start(s32[4]{0:T(128)} %lengths_ref.1) | copy-start | bytes 52
  92.5 2.2 %copy-start.2 = (bf16[256,8192]{1,0:T(8,128)(2,1)S(1)}, bf16[256,8192]{1,0:T(8,128)(2,1)}, u32[]{:S(2)}) copy-start(bf16[256,8192]{1,0:T(8,128)(2,1)} %weight_ref.1) | copy-start | bytes 12582916
  94.7 24.4 %copy-start.11 = (bf16[32,64,64]{2,1,0:T(8,128)(2,1)S(1)}, bf16[32,64,64]{2,1,0:T(8,128)(2,1)}, u32[]{:S(2)}) copy-start(bf16[32,64,64]{2,1,0:T(8,128)(2,1)} %copy-done.10) | copy-start | bytes 786436
  98.4 14.8 %collective-permute-start.10 = (bf16[64,8192]{1,0:T(8,128)(2,1)S(1)}, bf16[64,8192]{1,0:T(8,128)(2,1)S(1)}, u32[]{:S(2)}, u32[]{:S(2)}) collective-permute-start(bf16[64,8192]{1,0:T(8,128)(2,1)S(1)} %get-tuple-element.30), channel_id=1, source_target_pairs={{0,24},{1,25},{2,26},{3,27},{4,28},{5,29},{6,30},{7,31},{8,0},{9,1... | collective-permute-start | bytes 3145736 | tf_op jit(solution)/shard_map/ppermute | solution.py:45
  99.4 16.0 %collective-permute-start.9 = (bf16[64,8192]{1,0:T(8,128)(2,1)S(1)}, bf16[64,8192]{1,0:T(8,128)(2,1)S(1)}, u32[]{:S(2)}, u32[]{:S(2)}) collective-permute-start(bf16[64,8192]{1,0:T(8,128)(2,1)S(1)} %get-tuple-element.29), channel_id=1, source_target_pairs={{0,8},{1,9},{2,10},{3,11},{4,12},{5,13},{6,14},{7,15},{8,16},{9,17... | collective-permute-start | bytes 3145736 | tf_op jit(solution)/shard_map/ppermute | solution.py:45
  116.2 21.0 %collective-permute-start.12 = (bf16[64,4096]{1,0:T(8,128)(2,1)}, bf16[64,4096]{1,0:T(8,128)(2,1)S(1)}, u32[]{:S(2)}, u32[]{:S(2)}) collective-permute-start(bf16[64,4096]{1,0:T(8,128)(2,1)} %slice_add_fusion), channel_id=1, source_target_pairs={{0,24},{1,25},{2,26},{3,27},{4,28},{5,29},{6,30},{7,31},{8,0},{9,1... | collective-permute-start | bytes 1572872 | tf_op jit(solution)/shard_map/ppermute | solution.py:45
  117.1 20.1 %collective-permute-start.11 = (bf16[64,4096]{1,0:T(8,128)(2,1)}, bf16[64,4096]{1,0:T(8,128)(2,1)}, u32[]{:S(2)}, u32[]{:S(2)}) collective-permute-start(bf16[64,4096]{1,0:T(8,128)(2,1)} %slice_add_fusion.1), channel_id=1, source_target_pairs={{0,8},{1,9},{2,10},{3,11},{4,12},{5,13},{6,14},{7,15},{8,16},{9,17... | collective-permute-start | bytes 1572872 | tf_op jit(solution)/shard_map/ppermute | solution.py:45
  120.2 15.7 %all-to-all-start.3 = ((bf16[32,2,2048]{2,1,0:T(2,128)(2,1)}), bf16[32,2,2048]{2,1,0:T(2,128)(2,1)}, u32[]{:S(2)}, u32[]{:S(2)}) async-start(bf16[32,2,2048]{2,1,0:T(2,128)(2,1)} %reshape.148), calls=%async_computation.3 | async-start | bytes 524288 | tf_op jit(solution)/shard_map/all_to_all | solution.py:529
  126.8 35.5 %copy-start.17 = (bf16[8,8192]{1,0:T(8,128)(2,1)S(1)}, bf16[8,8192]{1,0:T(8,128)(2,1)}, u32[]{:S(2)}) copy-start(bf16[8,8192]{1,0:T(8,128)(2,1)} %param.16) | copy-start | bytes 393220
  137.2 1.2 copy-start.8
  144.6 10.6 %collective-permute-start.13 = (bf16[16,8192]{1,0:T(8,128)(2,1)}, bf16[16,8192]{1,0:T(8,128)(2,1)S(1)}, u32[]{:S(2)}, u32[]{:S(2)}) collective-permute-start(bf16[16,8192]{1,0:T(8,128)(2,1)} %get-tuple-element.38), channel_id=1, source_target_pairs={{0,1},{1,2},{2,3},{3,0},{4,5},{5,6},{6,7},{7,4},{8,9},{9,10},{10,1... | collective-permute-start | bytes 786440 | tf_op jit(solution)/shard_map/ppermute | solution.py:45
  145.5 9.7 %collective-permute-start.14 = (bf16[16,8192]{1,0:T(8,128)(2,1)}, bf16[16,8192]{1,0:T(8,128)(2,1)S(1)}, u32[]{:S(2)}, u32[]{:S(2)}) collective-permute-start(bf16[16,8192]{1,0:T(8,128)(2,1)} %get-tuple-element.39), channel_id=1, source_target_pairs={{0,2},{1,3},{2,0},{3,1},{4,6},{5,7},{6,4},{7,5},{8,10},{9,11},{10,... | collective-permute-start | bytes 786440 | tf_op jit(solution)/shard_map/ppermute | solution.py:45
  147.0 9.1 %collective-permute-start.15 = (bf16[16,8192]{1,0:T(8,128)(2,1)}, bf16[16,8192]{1,0:T(8,128)(2,1)S(1)}, u32[]{:S(2)}, u32[]{:S(2)}) collective-permute-start(bf16[16,8192]{1,0:T(8,128)(2,1)} %get-tuple-element.40), channel_id=1, source_target_pairs={{0,3},{1,0},{2,1},{3,2},{4,7},{5,4},{6,5},{7,6},{8,11},{9,8},{10,9... | collective-permute-start | bytes 786440 | tf_op jit(solution)/shard_map/ppermute | solution.py:45
  157.3 5.1 %collective-permute-start.16 = (bf16[8,8192]{1,0:T(8,128)(2,1)S(1)}, bf16[8,8192]{1,0:T(8,128)(2,1)S(1)}, u32[]{:S(2)}, u32[]{:S(2)}) collective-permute-start(bf16[8,8192]{1,0:T(8,128)(2,1)S(1)} %fusion.4), channel_id=1, source_target_pairs={{0,4},{1,5},{2,6},{3,7},{4,0},{5,1},{6,2},{7,3},{8,12},{9,13},{10,... | collective-permute-start | bytes 393224 | tf_op jit(solution)/shard_map/ppermute | solution.py:45
  (8 other events, 7.0 us)
where the time goes:
time: 166 us; the launch traced here: 163 us
  waiting for transfers between devices  62.6 us (38%)
  starting transfers between devices  48.1 us (29%)
  local copies, waits for them, and re-layouts  26.9 us (16%)
  Pallas kernels  15.2 us (9%)
  other arithmetic  9 us (5%)
    ppermute x17, waiting for transfers between devices, permute(): return lax.ppermute(block, AXES, source_to_target)  45 us
    ppermute x17, starting transfers between devices, permute(): return lax.ppermute(block, AXES, source_to_target)  24.3 us
    unnamed x40, local copies, waits for them, and re-layouts  17.3 us
    all_to_all x3, starting transfers between devices, spread(): lax.all_to_all(jnp.broadcast_to(block[None], (count,) + block.shape), AXE...  17.3 us
    all_to_all x3, waiting for transfers between devices, spread(): lax.all_to_all(jnp.broadcast_to(block[None], (count,) + block.shape), AXE...  9.69 us
    all_to_all x1, waiting for transfers between devices, shards(): lax.all_to_all(out_inner, AXES, 0, 0, axis_index_groups=row_groups())  7.9 us
    all_to_all x1, starting transfers between devices, shards(): lax.all_to_all(out_inner, AXES, 0, 0, axis_index_groups=row_groups())  6.53 us
    pallas_call x1, Pallas kernels, sum_rows(): pl.pallas_call(sum_kernel, grid=(steps,), in_specs=[spec_smem(), whole, p...  5.34 us
  transfers between devices with their start and end apart: 21, of which 10 were waited for; matrix products, arithmetic and copies ran while one was open for 10% of the time, Pallas kernels for 3%

commit v1 on v0

--- a/solution.py
+++ b/solution.py
@@ -62,6 +62,14 @@
     )
 
 
+def pool_flip(s):
+    return pairs(lambda h, c, x, z, y: (h ^ s, c, x, z, y))
+
+
+def y_flip(s):
+    return pairs(lambda h, c, x, z, y: (h, c, x, z, y ^ s))
+
+
 def z_swap():
     return pairs(lambda h, c, x, z, y: (h, c, x, 1 - z, y))
 
@@ -78,18 +86,17 @@
     return out
 
 
+def gather4(block, shift, here):
+    return placed([block] + [permute(block, shift(s)) for s in (1, 2, 3)], here)
+
+
+def both_of(block, bit, exchange):
+    other = permute(block, exchange)
+    return jnp.stack([jnp.where(bit == 0, block, other), jnp.where(bit == 0, other, block)])
+
+
 def pick(blocks, index):
     return lax.dynamic_index_in_dim(blocks, index, 0, keepdims=False)
-
-
-def spread(block, count, groups):
-    return lax.all_to_all(
-        jnp.broadcast_to(block[None], (count,) + block.shape),
-        AXES,
-        0,
-        0,
-        axis_index_groups=groups,
-    )
 
 
 def groups_of(key, order):
@@ -97,24 +104,6 @@
     for number, spot in enumerate(SPOTS):
         found.setdefault(key(*spot), []).append((order(*spot), number))
     return [[number for _, number in sorted(group)] for group in found.values()]
-
-
-def pool_groups():
-    return groups_of(lambda h, c, x, z, y: (x, z, y), lambda h, c, x, z, y: (h, c))
-
-
-def last_groups():
-    return groups_of(
-        lambda h, c, x, z, y: (h, c, z, y) if c == 0 else (h, c, x, z),
-        lambda h, c, x, z, y: x if c == 0 else y,
-    )
-
-
-def row_groups():
-    return groups_of(
-        lambda h, c, x, z, y: (h, c),
-        lambda h, c, x, z, y: (x, z, y) if c == 0 else (y, z, x),
-    )
 
 
 def spec_smem():
@@ -172,7 +161,7 @@
         out_specs=pl.BlockSpec((256, 2 * width), lambda j: (0, 0)),
         out_shape=jax.ShapeDtypeStruct((256, 2 * width), jnp.float32),
         scratch_shapes=[pltpu.VMEM((256, 2 * width), jnp.float32)],
-        compiler_params=pltpu.CompilerParams(vmem_limit_bytes=24 * 2**20),
+        compiler_params=pltpu.CompilerParams(vmem_limit_bytes=12 * 2**20),
         cost_estimate=pl.CostEstimate(
             flops=2 * 256 * 512 * 8192, bytes_accessed=12 * 2**20, transcendentals=0
         ),
@@ -183,6 +172,66 @@
     return lax.dot_general(
         left, right, (((1,), (1,)), ((), ())), preferred_element_type=jnp.float32
     )
+
+
+def inner_kernel(spot_ref, eight_ref, one_ref, left_ref, right_ref, three_ref, *refs):
+    sides = (refs[:5], refs[5:10])
+    inner_ref, up_ref, total = refs[10:]
+    first_core = spot_ref[0] == 0
+    total[...] = jnp.zeros_like(total)
+
+    def shard(side, s, at, zl):
+        near, plus, minus, far_low, far_high = sides[side]
+        if s != 2:
+            return (near, plus, None, minus)[s][at, zl]
+        low = far_low[lax.rem(at, 2), zl]
+        high = far_high[lax.rem(at, 2), zl]
+        return jnp.where(at < 2, low, high)
+
+    for s in range(4):
+        here = lax.rem(spot_ref[1] - s + 4, 4)
+        for t in range(4):
+            there = lax.rem(spot_ref[2] - t + 4, 4)
+            x = jnp.where(first_core, here, there)
+            y = jnp.where(first_core, there, here)
+            for zl in range(2):
+                mine = shard(0, s, there, zl)
+                theirs = shard(1, t, here, zl)
+                both = jnp.stack(
+                    [jnp.where(first_core, mine, theirs), jnp.where(first_core, theirs, mine)],
+                    axis=1,
+                )
+                down = both[:, :, :32].reshape(256, 128)
+                rest = both[:, :, 32:].reshape(256, 128)
+                index = x * 8 + zl * 4 + y
+                at = pl.ds(pl.multiple_of(index * 256, 256), 256)
+                halved = pl.ds(pl.multiple_of(lax.rem(index, 16) * 256, 256), 256)
+                two = jnp.where(index < 16, left_ref[:, halved], right_ref[:, halved])
+                rows = jnp.concatenate(
+                    [eight_ref[:, at], one_ref[:, at], two, three_ref[:, at]], axis=0
+                )
+                total[:, :128] += jnp.dot(rows, down, preferred_element_type=jnp.float32)
+                total[:, 128:] += jnp.dot(rows, rest, preferred_element_type=jnp.float32)
+                up_ref[at, :] = rest
+    inner_ref[...] = total[...]
+
+
+def inner_rows(spot, blocks, bands):
+    return pl.pallas_call(
+        inner_kernel,
+        in_specs=[spec_smem()]
+        + [pl.BlockSpec(memory_space=pltpu.VMEM)] * (len(blocks) + len(bands)),
+        out_specs=[pl.BlockSpec(memory_space=pltpu.VMEM)] * 2,
+        out_shape=[
+            jax.ShapeDtypeStruct((256, 256), jnp.float32),
+            jax.ShapeDtypeStruct((8192, 128), jnp.bfloat16),
+        ],
+        scratch_shapes=[pltpu.VMEM((256, 256), jnp.float32)],
+        compiler_params=pltpu.CompilerParams(vmem_limit_bytes=24 * 2**20),
+        cost_estimate=pl.CostEstimate(
+            flops=2 * 256 * 256 * 8192, bytes_accessed=10 * 2**20, transcendentals=0
+        ),
+    )(spot, *blocks, *bands)
 
 
 def attend_kernel(
@@ -207,10 +256,7 @@
     last = spot_ref[1]
     for s in range(4):
         k = lax.rem(last - s + 4, 4)
-        inner = parts_ref[k, 0].astype(jnp.float32)
-        for part in range(1, 8):
-            inner = inner + parts_ref[k, part].astype(jnp.float32)
-        inner = inner.astype(half)
+        inner = parts_ref[64 * s : 64 * s + 64].astype(half)
         frozen = frozen_ref[64 * s : 64 * s + 64]
         rows[k, :, :256] = frozen[:, :256] + adapter_scale * outer(inner[:, :64], query_up_ref[...])
         rows[k, :, 256:384] = frozen[:, 256:384] + adapter_scale * outer(
@@ -275,8 +321,7 @@
         block = jnp.where(first_core, found[k], across)
         ahead_ref[64 * s : 64 * s + 64] = block
         inner = jnp.dot(block, down_ref[...], preferred_element_type=jnp.float32).astype(half)
-        for copy in range(8):
-            inner_ref[8 * k + copy] = inner
+        inner_ref[64 * s : 64 * s + 64] = inner
 
 
 def attend_rows(spot, lengths, frozen, parts, ups, cosine, sine, cache, down):
@@ -288,13 +333,13 @@
         out_specs=[pl.BlockSpec(memory_space=pltpu.VMEM)] * 2,
         out_shape=[
             jax.ShapeDtypeStruct((256, 256), jnp.bfloat16),
-            jax.ShapeDtypeStruct((32, 64, 64), jnp.bfloat16),
+            jax.ShapeDtypeStruct((256, 128), jnp.bfloat16),
         ],
         scratch_shapes=[
             pltpu.VMEM((4, 64, 512), jnp.float32),
             pltpu.VMEM((4, 64, 256), jnp.bfloat16),
         ],
-        compiler_params=pltpu.CompilerParams(vmem_limit_bytes=24 * 2**20),
+        compiler_params=pltpu.CompilerParams(vmem_limit_bytes=14 * 2**20),
         cost_estimate=pl.CostEstimate(
             flops=2 * 512 * 320 * 256, bytes_accessed=4 * 2**20, transcendentals=512 * 320
         ),
@@ -308,26 +353,14 @@
     minus_ref,
     left_ref,
     right_ref,
-    parts_ref,
-    up_ref,
     mine_ref,
     one_ref,
     two_ref,
     three_ref,
     total,
-    inner,
 ):
     step = pl.program_id(0)
     at_left = step < pl.num_programs(0) // 2
-    tile = own_ref.shape[1]
-
-    @pl.when(step == 0)
-    def _():
-        found = parts_ref[0].astype(jnp.float32)
-        for part in range(1, 32):
-            found = found + parts_ref[part].astype(jnp.float32)
-        inner[...] = found.astype(jnp.bfloat16)
-
     own = own_ref[...].astype(jnp.float32)
 
     @pl.when(at_left)
@@ -337,14 +370,6 @@
     @pl.when(jnp.logical_not(at_left))
     def _():
         total[...] = own + plus_ref[...].astype(jnp.float32) + right_ref[...].astype(jnp.float32)
-
-    for k in range(4):
-        column = spot_ref[1 + k] * 256
-
-        @pl.when(column // tile == step)
-        def _():
-            at = pl.ds(pl.multiple_of(lax.rem(column, tile), 256), 256)
-            total[:, at] += adapter_scale * outer(inner[...], up_ref[k])
 
     middle = spot_ref[0]
     for s, ref in enumerate((mine_ref, one_ref, two_ref, three_ref)):
@@ -352,8 +377,8 @@
         ref[...] = total[at, :].astype(ref.dtype)
 
 
-def sum_rows(spot, own, plus, minus, left, right, parts, up_factor):
-    tile = 1024
+def sum_rows(spot, own, plus, minus, left, right):
+    tile = 2048
     steps = own.shape[1] // tile
     width = own.shape[1]
     last_left = steps // 2 - 1
@@ -369,26 +394,24 @@
             pl.BlockSpec((64, tile), lambda j: (0, jnp.minimum(j, last_left))),
             pl.BlockSpec((64, tile), lambda j: (0, jnp.minimum(j, last_left))),
             pl.BlockSpec((64, tile), lambda j: (0, jnp.maximum(j - steps // 2, 0))),
-            pl.BlockSpec(parts.shape, lambda j: (0, 0, 0)),
-            pl.BlockSpec(up_factor.shape, lambda j: (0, 0, 0)),
         ],
         out_specs=[out] * 4,
         out_shape=[jax.ShapeDtypeStruct((16, width), jnp.float32)]
         + [jax.ShapeDtypeStruct((16, width), jnp.bfloat16)] * 3,
-        scratch_shapes=[
-            pltpu.VMEM((64, tile), jnp.float32),
-            pltpu.VMEM((64, 64), jnp.bfloat16),
-        ],
-        compiler_params=pltpu.CompilerParams(vmem_limit_bytes=16 * 2**20),
+        scratch_shapes=[pltpu.VMEM((64, tile), jnp.float32)],
+        compiler_params=pltpu.CompilerParams(vmem_limit_bytes=12 * 2**20),
         cost_estimate=pl.CostEstimate(
             flops=2 * 64 * 64 * 1024, bytes_accessed=5 * 2**20, transcendentals=0
         ),
-    )(spot, own, plus, minus, left, right, parts, up_factor)
-
-
-def out_kernel(rows_ref, weight_ref, own_ref, plus_ref, minus_ref, left_ref, right_ref):
+    )(spot, own, plus, minus, left, right)
+
+
+def out_kernel(
+    rows_ref, inner_ref, weight_ref, up_ref, own_ref, plus_ref, minus_ref, left_ref, right_ref
+):
     at_left = pl.program_id(0) < pl.num_programs(0) // 2
     part = jnp.dot(rows_ref[...], weight_ref[...], preferred_element_type=jnp.float32)
+    part = part + adapter_scale * outer(inner_ref[:, :64], up_ref[:, 64:])
     part = part.astype(jnp.bfloat16)
     own_ref[...] = part[:64]
 
@@ -405,7 +428,7 @@
         right_ref[...] = part[192:]
 
 
-def out_pieces(rows, weight):
+def out_pieces(rows, inner, weight, up_factor):
     tile = 2048
     depth, width = weight.shape
     steps = width // tile
@@ -417,16 +440,18 @@
         grid=(steps,),
         in_specs=[
             pl.BlockSpec(rows.shape, lambda j: (0, 0)),
+            pl.BlockSpec(inner.shape, lambda j: (0, 0)),
             pl.BlockSpec((depth, tile), lambda j: (0, j)),
+            pl.BlockSpec((tile, 128), lambda j: (j, 0)),
         ],
         out_specs=[whole, whole, whole, left, right],
         out_shape=[jax.ShapeDtypeStruct((64, width), jnp.bfloat16)] * 3
         + [jax.ShapeDtypeStruct((64, width // 2), jnp.bfloat16)] * 2,
-        compiler_params=pltpu.CompilerParams(vmem_limit_bytes=28 * 2**20),
+        compiler_params=pltpu.CompilerParams(vmem_limit_bytes=14 * 2**20),
         cost_estimate=pl.CostEstimate(
             flops=2 * 256 * 256 * 8192, bytes_accessed=8 * 2**20, transcendentals=0
         ),
-    )(rows, weight)
+    )(rows, inner, weight, up_factor)
 
 
 def shards(
@@ -453,9 +478,6 @@
     middle = jnp.where(first_core, y, x)
     half = jnp.bfloat16
 
-    def tp_index(k):
-        return jnp.where(first_core, k * 8 + zl * 4 + y, x * 8 + zl * 4 + k)
-
     row_float = hidden.astype(jnp.float32)
     normed = (
         row_float
@@ -466,50 +488,56 @@
     packed = jnp.concatenate(
         [
             jnp.concatenate([a_query, a_key], axis=1),
-            jnp.concatenate([a_value, a_out], axis=1),
-            jnp.concatenate([b_query.T, b_out.T], axis=1),
+            jnp.concatenate([a_value, b_out.T], axis=1),
+            jnp.concatenate([a_out, b_query.T], axis=1),
             jnp.concatenate([b_key.T, b_value.T], axis=1),
-            jnp.zeros((4, 128), half),
+            jnp.zeros((12, 128), half),
         ],
         axis=0,
     )
     packed, _ = lax.optimization_barrier((packed, normed))
-    pooled = spread(packed, 8, pool_groups())
-    wide = spread(pooled, 4, last_groups())
+    packed = both_of(packed, zh & 1, pool_flip(1))
     pair = placed([normed, permute(normed, z_swap())], zl).reshape(16, 8192)
+    packed, _ = lax.optimization_barrier((packed, pair))
     met = [pair] + [permute(pair, middle_shift(s)) for s in (1, 2, 3)]
     eight = placed(met, middle).reshape(64, 8192)
     from_1 = permute(eight, last_shift(1))
     from_3 = permute(eight, last_shift(3))
-
-    down_first = wide[:, :, 0:32].reshape(1024, 128)
-    down_second = wide[:, :, 32:64].reshape(1024, 128)
-    out_up = wide[:, :, 64:96, 64:].reshape(4, 256, 64)
-    down_out = pooled[:, 32:64, 64:].reshape(256, 64)
-    query_up = pooled[:, 64:96, :64].reshape(256, 64)
-    narrow = wide[:, :, 96:100].reshape(128, 128)
-    narrow = jnp.where(first_core, permute(narrow, core_swap()), narrow)
+    packed = both_of(packed, zh >> 1, pool_flip(2)).reshape(4, 112, 128)
+    packed, _ = lax.optimization_barrier((packed, eight))
+    band = packed[:, :64]
+    band = placed([band, permute(band, z_swap())], zl)
+    band = gather4(band, middle_shift, middle)
+    from_1, from_3, band = lax.optimization_barrier((from_1, from_3, band))
+    left_2 = permute(from_1[:, :4096], last_shift(1))
+    right_2 = permute(from_3[:, 4096:], last_shift(3))
+    band_1 = permute(band, last_shift(1))
+    band_3 = permute(band, last_shift(3))
+
+    own = jnp.swapaxes(both_of(packed[:, 64:], core, core_swap()), 0, 1).reshape(8, 48, 128)
+    down_out = own[:, :32].reshape(256, 128)
+    query_up = down_out[:, 64:]
+    narrow = both_of(own[:, 32:36].reshape(32, 128), y & 1, y_flip(1))
+    narrow = both_of(narrow, y >> 1, y_flip(2)).reshape(128, 128)
     key_up = narrow[:, :64]
     value_up = narrow[:, 64:]
 
-    down = jnp.concatenate([down_first, down_second[:, :64]], axis=1).reshape(4, 256, 192)
-    down_padded = jnp.zeros((8192, 192), half)
-    for k in range(4):
-        down_padded = lax.dynamic_update_slice_in_dim(down_padded, down[k], tp_index(k) * 256, 0)
-    inner = dot32(eight, down_padded).astype(half)
-    from_1, from_3, inner = lax.optimization_barrier((from_1, from_3, inner))
-    left_2 = permute(from_1[:, :4096], last_shift(1))
-    right_2 = permute(from_3[:, 4096:], last_shift(3))
-    parts = spread(inner, 32, row_groups()).reshape(4, 8, 64, 192)
+    band_1, band_3 = lax.optimization_barrier((band_1, band_3))
+    far_low = permute(band_1[:2], last_shift(1))
+    far_high = permute(band_3[2:], last_shift(3))
     frozen = project_rows(
         eight, from_1, left_2, right_2, from_3, query_weight, w_keyvalue.reshape(8192, 256)
     )
+    far_low, far_high, frozen = lax.optimization_barrier((far_low, far_high, frozen))
+    bands = (band, band_1, band_3, far_low, far_high)
+    bands = bands + tuple(permute(block, core_swap()) for block in bands)
+    spot = jnp.stack([core, last, middle]).astype(jnp.int32)
+    parts, out_up = inner_rows(spot, (eight, from_1, left_2, right_2, from_3), bands)
     draft_places = (
         jnp.arange(VERIFY, dtype=jnp.int32).reshape(2, 4, 8).transpose(1, 0, 2).reshape(VERIFY)
     )
     places = (start_positions[:, None] + draft_places[None, :]).reshape(-1)
     cosine, sine = turns(places, HEAD_DIM)
-    spot = jnp.stack([core, last]).astype(jnp.int32)
     ahead, out_inner = attend_rows(
         spot,
         draft_lengths,
@@ -522,18 +550,15 @@
         down_out,
     )
 
-    own, plus, minus, left_1, right_3 = out_pieces(ahead, output_weight)
+    own, plus, minus, left_1, right_3 = out_pieces(ahead, out_inner, output_weight, out_up)
     got_plus = permute(plus, last_shift(1))
     got_minus = permute(minus, last_shift(3))
-    out_inner, _ = lax.optimization_barrier((out_inner, plus))
-    out_parts = lax.all_to_all(out_inner, AXES, 0, 0, axis_index_groups=row_groups())
     got_plus, got_minus = lax.optimization_barrier((got_plus, got_minus))
     got_left_1 = permute(left_1 + got_plus[:, :4096], last_shift(1))
     got_right_3 = permute(right_3 + got_minus[:, 4096:], last_shift(3))
 
-    spot = jnp.stack([middle] + [tp_index(k) for k in range(4)]).astype(jnp.int32)
     total, *sent = sum_rows(
-        spot, own, got_plus, got_minus, got_left_1, got_right_3, out_parts, out_up
+        middle.reshape(1), own, got_plus, got_minus, got_left_1, got_right_3
     )
     for s, block in zip((1, 2, 3), sent):
         total = total + permute(block, middle_shift(s)).astype(jnp.float32)

time: 166 us -> 135 us (0.81); the launches traced: 163 us -> 134 us
  local copies, waits for them, and re-layouts: 26.9 us -> 13.2 us
  waiting for transfers between devices: 62.6 us -> 49.4 us
  starting transfers between devices: 48.1 us -> 44.3 us
  Pallas kernels: 15.2 us -> 18.9 us
    all_to_all x4 -> x0, starting transfers between devices: 23.8 us -> none  [the longest x3 17.3 us: spread(): lax.all_to_all(jnp.broadcast_to(block[None], (count,) + block.shape), AXE...]
    ppermute x17 -> x34, starting transfers between devices: 24.3 us -> 44.3 us  [permute(): return lax.ppermute(block, AXES, source_to_target)]
    all_to_all x4 -> x0, waiting for transfers between devices: 17.6 us -> none  [the longest x3 9.69 us: spread(): lax.all_to_all(jnp.broadcast_to(block[None], (count,) + block.shape), AXE...]
    unnamed x40 -> x18, local copies, waits for them, and re-layouts: 17.3 us -> 4.41 us
    pallas_call x0 -> x1, Pallas kernels: none -> 4.52 us  [inner_rows(): pl.pallas_call(inner_kernel, in_specs=[spec_smem()] + [pl.BlockSpec(memor...]
    ppermute x17 -> x34, waiting for transfers between devices: 45 us -> 49.4 us  [permute(): return lax.ppermute(block, AXES, source_to_target)]
    pallas_call x1, Pallas kernels: 5.34 us -> 1.11 us  [sum_rows(): pl.pallas_call(sum_kernel, grid=(steps,), in_specs=[spec_smem(), whole, p...]
    broadcast_in_dim x5 -> x1, local copies, waits for them, and re-layouts: 3.24 us -> 0.01 us  [shards(): jnp.zeros((12, 128), half)]
  transfers between devices with their start and end apart: 21 -> 34, of which waited for: 10 -> 16; matrix products, arithmetic and copies ran while one was open for 10% -> 10% of each run, Pallas kernels for 3% -> 5%
where the time goes in v1:
time: 135 us; the launch traced here: 134 us
  waiting for transfers between devices  49.4 us (37%)
  starting transfers between devices  44.3 us (33%)
  Pallas kernels  18.9 us (14%)
  local copies, waits for them, and re-layouts  13.2 us (10%)
  other arithmetic  7.72 us (6%)
    ppermute x34, waiting for transfers between devices, permute(): return lax.ppermute(block, AXES, source_to_target)  49.4 us
    ppermute x34, starting transfers between devices, permute(): return lax.ppermute(block, AXES, source_to_target)  44.3 us
    pallas_call x1, Pallas kernels, project_rows(): pl.pallas_call(project_kernel, grid=(steps,), in_specs=[whole, whole, pl....  6.32 us
    pallas_call x1, Pallas kernels, inner_rows(): pl.pallas_call(inner_kernel, in_specs=[spec_smem()] + [pl.BlockSpec(memor...  4.52 us
    unnamed x18, local copies, waits for them, and re-layouts  4.41 us
    pallas_call x1, Pallas kernels, out_pieces(): pl.pallas_call(out_kernel, grid=(steps,), in_specs=[pl.BlockSpec(rows.sha...  4.16 us
    pallas_call x1, Pallas kernels, attend_rows(): pl.pallas_call(attend_kernel, in_specs=[spec_smem(), spec_smem()] + [pl.B...  2.82 us
    dynamic_update_slice x11, local copies, waits for them, and re-layouts, placed(): out = lax.dynamic_update_index_in_dim(out, block, (here - s) % count, 0)  2.8 us
  transfers between devices with their start and end apart: 34, of which 16 were waited for; matrix products, arithmetic and copies ran while one was open for 10% of the time, Pallas kernels for 5%

profile of v1, /device:TPU:64, one launch (start us, length us, event | category | flops | bytes accessed | tf_op | source)
XLA Modules:
  0.0 134.0 jit_solution(1620457160207792093)
XLA Ops:
  2.2 2.0 %collective-permute-start = (bf16[8,8192]{1,0:T(8,128)(2,1)S(1)}, bf16[8,8192]{1,0:T(8,128)(2,1)S(1)}, u32[]{:S(2)}, u32[]{:S(2)}) collective-permute-start(bf16[8,8192]{1,0:T(8,128)(2,1)S(1)} %get-tuple-element.58), channel_id=1, source_target_pairs={{0,4},{1,5},{2,6},{3,7},{4,0},{5,1},{6,2},{7,3},{8,12},{9,13},{10,... | collective-permute-start | bytes 393224 | tf_op jit(solution)/shard_map/ppermute | solution.py:45
  9.0 2.6 %collective-permute-done.6 = bf16[112,128]{1,0:T(8,128)(2,1)S(1)} collective-permute-done((bf16[112,128]{1,0:T(8,128)(2,1)S(1)}, bf16[112,128]{1,0:T(8,128)(2,1)S(1)}, u32[]{:S(2)}, u32[]{:S(2)}) %collective-permute-start.6) | collective-permute-done | bytes 28704 | tf_op jit(solution)/shard_map/ppermute | solution.py:45
  11.6 1.7 %collective-permute-start.1 = (bf16[16,8192]{1,0:T(8,128)(2,1)S(1)}, bf16[16,8192]{1,0:T(8,128)(2,1)S(1)}, u32[]{:S(2)}, u32[]{:S(2)}) collective-permute-start(bf16[16,8192]{1,0:T(8,128)(2,1)S(1)} %bitcast.78), channel_id=1, source_target_pairs={{0,1},{1,2},{2,3},{3,0},{4,5},{5,6},{6,7},{7,4},{8,9},{9,10},{10,1... | collective-permute-start | bytes 786440 | tf_op jit(solution)/shard_map/ppermute | solution.py:45
  13.3 2.9 %collective-permute-start.2 = (bf16[16,8192]{1,0:T(8,128)(2,1)S(1)}, bf16[16,8192]{1,0:T(8,128)(2,1)S(1)}, u32[]{:S(2)}, u32[]{:S(2)}) collective-permute-start(bf16[16,8192]{1,0:T(8,128)(2,1)S(1)} %bitcast.79), channel_id=1, source_target_pairs={{0,2},{1,3},{2,0},{3,1},{4,6},{5,7},{6,4},{7,5},{8,10},{9,11},{10,... | collective-permute-start | bytes 786440 | tf_op jit(solution)/shard_map/ppermute | solution.py:45
  17.5 4.5 %collective-permute-start.7 = (bf16[2,112,128]{2,1,0:T(8,128)(2,1)S(1)}, bf16[2,112,128]{2,1,0:T(8,128)(2,1)S(1)}, u32[]{:S(2)}, u32[]{:S(2)}) collective-permute-start(bf16[2,112,128]{2,1,0:T(8,128)(2,1)S(1)} %pad_maximum_fusion.3), channel_id=1, source_target_pairs={{0,128},{1,129},{2,130},{3,131},{4,132},{5,133},{6,134},{7,135},{8... | collective-permute-start | bytes 172040 | tf_op jit(solution)/shard_map/ppermute | solution.py:45
  22.1 4.0 %collective-permute-done.7 = bf16[2,112,128]{2,1,0:T(8,128)(2,1)S(1)} collective-permute-done((bf16[2,112,128]{2,1,0:T(8,128)(2,1)S(1)}, bf16[2,112,128]{2,1,0:T(8,128)(2,1)S(1)}, u32[]{:S(2)}, u32[]{:S(2)}) %collective-permute-start.7) | collective-permute-done | bytes 57376 | tf_op jit(solution)/shard_map/ppermute | solution.py:45
  26.3 1.7 %collective-permute-start.4 = (bf16[64,8192]{1,0:T(8,128)(2,1)S(1)}, bf16[64,8192]{1,0:T(8,128)(2,1)S(1)}, u32[]{:S(2)}, u32[]{:S(2)}) collective-permute-start(bf16[64,8192]{1,0:T(8,128)(2,1)S(1)} %bitcast.70), channel_id=1, source_target_pairs={{0,8},{1,9},{2,10},{3,11},{4,12},{5,13},{6,14},{7,15},{8,16},{9,17... | collective-permute-start | bytes 3145736 | tf_op jit(solution)/shard_map/ppermute | solution.py:45
  28.0 1.6 %collective-permute-start.5 = (bf16[64,8192]{1,0:T(8,128)(2,1)S(1)}, bf16[64,8192]{1,0:T(8,128)(2,1)S(1)}, u32[]{:S(2)}, u32[]{:S(2)}) collective-permute-start(bf16[64,8192]{1,0:T(8,128)(2,1)S(1)} %bitcast.71), channel_id=1, source_target_pairs={{0,24},{1,25},{2,26},{3,27},{4,28},{5,29},{6,30},{7,31},{8,0},{9,1... | collective-permute-start | bytes 3145736 | tf_op jit(solution)/shard_map/ppermute | solution.py:45
  31.7 2.6 %collective-permute-done.8 = bf16[4,64,128]{2,1,0:T(8,128)(2,1)S(1)} collective-permute-done((bf16[4,64,128]{2,1,0:T(8,128)(2,1)S(1)}, bf16[4,64,128]{2,1,0:T(8,128)(2,1)S(1)}, u32[]{:S(2)}, u32[]{:S(2)}) %collective-permute-start.8) | collective-permute-done | bytes 65568 | tf_op jit(solution)/shard_map/ppermute | solution.py:45
  35.1 1.6 %collective-permute-start.10 = (bf16[2,4,64,128]{3,2,1,0:T(8,128)(2,1)S(1)}, bf16[2,4,64,128]{3,2,1,0:T(8,128)(2,1)S(1)}, u32[]{:S(2)}, u32[]{:S(2)}) collective-permute-start(bf16[2,4,64,128]{3,2,1,0:T(8,128)(2,1)S(1)} %bitcast_dynamic-update-slice_fusion.10), channel_id=1, source_target_pairs={{0,2},{1,3},{2,0},{3,1},{4,6},{5,7},{6,4},{7,5},{8,10},{9,11},{10,... | collective-permute-start | bytes 393224 | tf_op jit(solution)/shard_map/ppermute | solution.py:45
  38.3 2.3 %collective-permute-done.9 = bf16[2,4,64,128]{3,2,1,0:T(8,128)(2,1)S(1)} collective-permute-done((bf16[2,4,64,128]{3,2,1,0:T(8,128)(2,1)S(1)}, bf16[2,4,64,128]{3,2,1,0:T(8,128)(2,1)S(1)}, u32[]{:S(2)}, u32[]{:S(2)}) %collective-permute-start.9) | collective-permute-done | bytes 131104 | tf_op jit(solution)/shard_map/ppermute | solution.py:45
  43.9 1.6 %collective-permute-done.11 = bf16[2,4,64,128]{3,2,1,0:T(8,128)(2,1)S(1)} collective-permute-done((bf16[2,4,64,128]{3,2,1,0:T(8,128)(2,1)S(1)}, bf16[2,4,64,128]{3,2,1,0:T(8,128)(2,1)S(1)}, u32[]{:S(2)}, u32[]{:S(2)}) %collective-permute-start.11) | collective-permute-done | bytes 131104 | tf_op jit(solution)/shard_map/ppermute | solution.py:45
  46.2 1.8 %collective-permute-start.12 = (bf16[4,2,4,64,128]{4,3,2,1,0:T(8,128)(2,1)}, bf16[4,2,4,64,128]{4,3,2,1,0:T(8,128)(2,1)}, u32[]{:S(2)}, u32[]{:S(2)}) collective-permute-start(bf16[4,2,4,64,128]{4,3,2,1,0:T(8,128)(2,1)} %bitcast_dynamic-update-slice_fusion.4.refs_0_), channel_id=1, source_target_pairs={{0,8},{1,9},{2,10},{3,11},{4,12},{5,13},{6,14},{7,15},{8,16},{9,17... | collective-permute-start | bytes 1572872 | tf_op jit(solution)/shard_map/ppermute | solution.py:45
  51.8 2.6 %collective-permute-start.17 = (bf16[64,4096]{1,0:T(8,128)(2,1)}, bf16[64,4096]{1,0:T(8,128)(2,1)}, u32[]{:S(2)}, u32[]{:S(2)}) collective-permute-start(bf16[64,4096]{1,0:T(8,128)(2,1)} %slice.43), channel_id=1, source_target_pairs={{0,24},{1,25},{2,26},{3,27},{4,28},{5,29},{6,30},{7,31},{8,0},{9,1... | collective-permute-start | bytes 1572872 | tf_op jit(solution)/shard_map/ppermute | solution.py:45
  58.5 1.4 %collective-permute-start.14 = (bf16[2,2,4,64,128]{4,3,2,1,0:T(8,128)(2,1)S(1)}, bf16[2,2,4,64,128]{4,3,2,1,0:T(8,128)(2,1)S(1)}, u32[]{:S(2)}, u32[]{:S(2)}) collective-permute-start(bf16[2,2,4,64,128]{4,3,2,1,0:T(8,128)(2,1)S(1)} %slice.40), channel_id=1, source_target_pairs={{0,8},{1,9},{2,10},{3,11},{4,12},{5,13},{6,14},{7,15},{8,16},{9,17... | collective-permute-start | bytes 786440 | tf_op jit(solution)/shard_map/ppermute | solution.py:45
  60.9 1.9 %collective-permute-start.15 = (bf16[2,2,4,64,128]{4,3,2,1,0:T(8,128)(2,1)S(1)}, bf16[2,2,4,64,128]{4,3,2,1,0:T(8,128)(2,1)S(1)}, u32[]{:S(2)}, u32[]{:S(2)}) collective-permute-start(bf16[2,2,4,64,128]{4,3,2,1,0:T(8,128)(2,1)S(1)} %slice.41), channel_id=1, source_target_pairs={{0,24},{1,25},{2,26},{3,27},{4,28},{5,29},{6,30},{7,31},{8,0},{9,1... | collective-permute-start | bytes 786440 | tf_op jit(solution)/shard_map/ppermute | solution.py:45
  63.6 2.2 %copy-done = bf16[8192,256]{1,0:T(8,128)(2,1)S(1)} copy-done((bf16[8192,256]{1,0:T(8,128)(2,1)S(1)}, bf16[8192,256]{1,0:T(8,128)(2,1)}, u32[]{:S(2)}) %copy-start) | copy-done | bytes 4194328
  65.7 2.2 %copy-done.1 = bf16[1,8192,256]{2,1,0:T(8,128)(2,1)S(1)} copy-done((bf16[1,8192,256]{2,1,0:T(8,128)(2,1)S(1)}, bf16[1,8192,256]{2,1,0:T(8,128)(2,1)}, u32[]{:S(2)}) %copy-start.1) | copy-done | bytes 4194328
  67.9 6.3 %shard_map.154.frozen_ref = f32[256,512]{1,0:T(8,128)S(1)} custom-call(bf16[64,8192]{1,0:T(8,128)(2,1)S(1)} %bitcast.72, bf16[64,8192]{1,0:T(8,128)(2,1)S(1)} %collective-permute-done.4.one_ref, bf16[64,4096]{1,0:T(8,128)(2,1)} %collective-permute-done.16.left_ref, bf16[64,4096]{1,0:T(8,128)(2,1)} %collective-permute-done.17.right_ref, ...), custom_call_target="tpu_custom_call" | custom-call | flops 2147483648 | bytes 12582912 | tf_op jit(solution)/shard_map/pallas_call | solution.py:149
  76.3 4.5 %shard_map.155 = (f32[256,256]{1,0:T(8,128)S(1)}, bf16[8192,128]{1,0:T(8,128)(2,1)S(1)}) custom-call(s32[3]{0:T(128)S(1)} %pad_add_fusion.spot_ref, bf16[64,8192]{1,0:T(8,128)(2,1)S(1)} %bitcast.73, bf16[64,8192]{1,0:T(8,128)(2,1)S(1)} %collective-permute-done.4.one_ref, bf16[64,4096]{1,0:T(8,128)(2,1)} %collective-permute-done.16.left_ref, ...), custom_call_target="tpu_custom_call" | custom-call | flops 1073741824 | bytes 10485760 | tf_op jit(solution)/shard_map/pallas_call | solution.py:220
  80.9 2.8 %shard_map.156 = (bf16[256,256]{1,0:T(8,128)(2,1)S(1)}, bf16[256,128]{1,0:T(8,128)(2,1)S(1)}) custom-call(s32[3]{0:T(128)S(1)} %pad_add_fusion.spot_ref, s32[4]{0:T(128)S(1)} %copy-done.4, f32[256,512]{1,0:T(8,128)S(1)} %shard_map.154.frozen_ref, f32[256,256]{1,0:T(8,128)S(1)} %get-tuple-element.42.parts_ref, bf16[256,64]{1,0:T(8,128)(2,1)S(1)} %slice.53.query_up_ref, ...), custom_call_target="tpu_custom_call" | custom-call | flops 83886080 | bytes 4194304 | tf_op jit(solution)/shard_map/pallas_call | solution.py:329
  83.7 4.2 %shard_map.157 = (bf16[64,8192]{1,0:T(8,128)(2,1)S(1)}, bf16[64,8192]{1,0:T(8,128)(2,1)S(1)}, bf16[64,8192]{1,0:T(8,128)(2,1)S(1)}, bf16[64,4096]{1,0:T(8,128)(2,1)S(1)}, bf16[64,4096]{1,0:T(8,128)(2,1)S(1)}) custom-call(bf16[256,256]{1,0:T(8,128)(2,1)S(1)} %get-tuple-element.43.rows_ref, bf16[256,128]{1,0:T(8,128)(2,1)S(1)} %get-tuple-element.44.inner_ref, ...), custom_call_target="tpu_custom_call" | custom-call | flops 1073741824 | bytes 8388608 | tf_op jit(solution)/shard_map/pallas_call | solution.py:438
  89.0 2.2 %collective-permute-start.27 = (bf16[64,8192]{1,0:T(8,128)(2,1)S(1)}, bf16[64,8192]{1,0:T(8,128)(2,1)S(1)}, u32[]{:S(2)}, u32[]{:S(2)}) collective-permute-start(bf16[64,8192]{1,0:T(8,128)(2,1)S(1)} %get-tuple-element.48), channel_id=1, source_target_pairs={{0,24},{1,25},{2,26},{3,27},{4,28},{5,29},{6,30},{7,31},{8,0},{9,1... | collective-permute-start | bytes 3145736 | tf_op jit(solution)/shard_map/ppermute | solution.py:45
  91.2 12.8 %collective-permute-done.26.plus_ref = bf16[64,8192]{1,0:T(8,128)(2,1)S(1)} collective-permute-done((bf16[64,8192]{1,0:T(8,128)(2,1)S(1)}, bf16[64,8192]{1,0:T(8,128)(2,1)S(1)}, u32[]{:S(2)}, u32[]{:S(2)}) %collective-permute-start.26) | collective-permute-done | bytes 1048608 | tf_op jit(solution)/shard_map/ppermute | solution.py:45
  105.2 2.3 %collective-permute-start.29 = (bf16[64,4096]{1,0:T(8,128)(2,1)S(1)}, bf16[64,4096]{1,0:T(8,128)(2,1)S(1)}, u32[]{:S(2)}, u32[]{:S(2)}) collective-permute-start(bf16[64,4096]{1,0:T(8,128)(2,1)S(1)} %slice_add_fusion), channel_id=1, source_target_pairs={{0,24},{1,25},{2,26},{3,27},{4,28},{5,29},{6,30},{7,31},{8,0},{9,1... | collective-permute-start | bytes 1572872 | tf_op jit(solution)/shard_map/ppermute | solution.py:45
  107.5 7.0 %collective-permute-done.28.left_ref = bf16[64,4096]{1,0:T(8,128)(2,1)S(1)} collective-permute-done((bf16[64,4096]{1,0:T(8,128)(2,1)S(1)}, bf16[64,4096]{1,0:T(8,128)(2,1)S(1)}, u32[]{:S(2)}, u32[]{:S(2)}) %collective-permute-start.28) | collective-permute-done | bytes 524320 | tf_op jit(solution)/shard_map/ppermute | solution.py:45
  115.6 1.8 %collective-permute-start.32 = (bf16[16,8192]{1,0:T(8,128)(2,1)S(1)}, bf16[16,8192]{1,0:T(8,128)(2,1)S(1)}, u32[]{:S(2)}, u32[]{:S(2)}) collective-permute-start(bf16[16,8192]{1,0:T(8,128)(2,1)S(1)} %get-tuple-element.56), channel_id=1, source_target_pairs={{0,3},{1,0},{2,1},{3,2},{4,7},{5,4},{6,5},{7,6},{8,11},{9,8},{10,9... | collective-permute-start | bytes 786440 | tf_op jit(solution)/shard_map/ppermute | solution.py:45
  117.4 1.6 %collective-permute-start.31 = (bf16[16,8192]{1,0:T(8,128)(2,1)S(1)}, bf16[16,8192]{1,0:T(8,128)(2,1)S(1)}, u32[]{:S(2)}, u32[]{:S(2)}) collective-permute-start(bf16[16,8192]{1,0:T(8,128)(2,1)S(1)} %get-tuple-element.55), channel_id=1, source_target_pairs={{0,2},{1,3},{2,0},{3,1},{4,6},{5,7},{6,4},{7,5},{8,10},{9,11},{10,... | collective-permute-start | bytes 786440 | tf_op jit(solution)/shard_map/ppermute | solution.py:45
  119.1 3.0 %collective-permute-done.32 = bf16[16,8192]{1,0:T(8,128)(2,1)S(1)} collective-permute-done((bf16[16,8192]{1,0:T(8,128)(2,1)S(1)}, bf16[16,8192]{1,0:T(8,128)(2,1)S(1)}, u32[]{:S(2)}, u32[]{:S(2)}) %collective-permute-start.32) | collective-permute-done | bytes 262176 | tf_op jit(solution)/shard_map/ppermute | solution.py:45
  122.1 3.3 %collective-permute-done.31 = bf16[16,8192]{1,0:T(8,128)(2,1)S(1)} collective-permute-done((bf16[16,8192]{1,0:T(8,128)(2,1)S(1)}, bf16[16,8192]{1,0:T(8,128)(2,1)S(1)}, u32[]{:S(2)}, u32[]{:S(2)}) %collective-permute-start.31) | collective-permute-done | bytes 262176 | tf_op jit(solution)/shard_map/ppermute | solution.py:45
  125.4 2.7 %collective-permute-done.30 = bf16[16,8192]{1,0:T(8,128)(2,1)S(1)} collective-permute-done((bf16[16,8192]{1,0:T(8,128)(2,1)S(1)}, bf16[16,8192]{1,0:T(8,128)(2,1)S(1)}, u32[]{:S(2)}, u32[]{:S(2)}) %collective-permute-start.30) | collective-permute-done | bytes 262176 | tf_op jit(solution)/shard_map/ppermute | solution.py:45
  129.2 4.2 %collective-permute-done.33 = bf16[8,8192]{1,0:T(8,128)(2,1)S(1)} collective-permute-done((bf16[8,8192]{1,0:T(8,128)(2,1)S(1)}, bf16[8,8192]{1,0:T(8,128)(2,1)S(1)}, u32[]{:S(2)}, u32[]{:S(2)}) %collective-permute-start.33) | collective-permute-done | bytes 131104 | tf_op jit(solution)/shard_map/ppermute | solution.py:45
  (116 shorter events, 33.6 us)
Async XLA Ops:
  2.2 9.5 %collective-permute-start = (bf16[8,8192]{1,0:T(8,128)(2,1)S(1)}, bf16[8,8192]{1,0:T(8,128)(2,1)S(1)}, u32[]{:S(2)}, u32[]{:S(2)}) collective-permute-start(bf16[8,8192]{1,0:T(8,128)(2,1)S(1)} %get-tuple-element.58), channel_id=1, source_target_pairs={{0,4},{1,5},{2,6},{3,7},{4,0},{5,1},{6,2},{7,3},{8,12},{9,13},{10,... | collective-permute-start | bytes 393224 | tf_op jit(solution)/shard_map/ppermute | solution.py:45
  6.7 4.9 %collective-permute-start.6 = (bf16[112,128]{1,0:T(8,128)(2,1)S(1)}, bf16[112,128]{1,0:T(8,128)(2,1)S(1)}, u32[]{:S(2)}, u32[]{:S(2)}) collective-permute-start(bf16[112,128]{1,0:T(8,128)(2,1)S(1)} %concatenate.25), channel_id=1, source_target_pairs={{0,64},{1,65},{2,66},{3,67},{4,68},{5,69},{6,70},{7,71},{8,72},{9,... | collective-permute-start | bytes 86024 | tf_op jit(solution)/shard_map/ppermute | solution.py:45
  11.6 14.5 %collective-permute-start.1 = (bf16[16,8192]{1,0:T(8,128)(2,1)S(1)}, bf16[16,8192]{1,0:T(8,128)(2,1)S(1)}, u32[]{:S(2)}, u32[]{:S(2)}) collective-permute-start(bf16[16,8192]{1,0:T(8,128)(2,1)S(1)} %bitcast.78), channel_id=1, source_target_pairs={{0,1},{1,2},{2,3},{3,0},{4,5},{5,6},{6,7},{7,4},{8,9},{9,10},{10,1... | collective-permute-start | bytes 786440 | tf_op jit(solution)/shard_map/ppermute | solution.py:45
  13.3 12.9 %collective-permute-start.2 = (bf16[16,8192]{1,0:T(8,128)(2,1)S(1)}, bf16[16,8192]{1,0:T(8,128)(2,1)S(1)}, u32[]{:S(2)}, u32[]{:S(2)}) collective-permute-start(bf16[16,8192]{1,0:T(8,128)(2,1)S(1)} %bitcast.79), channel_id=1, source_target_pairs={{0,2},{1,3},{2,0},{3,1},{4,6},{5,7},{6,4},{7,5},{8,10},{9,11},{10,... | collective-permute-start | bytes 786440 | tf_op jit(solution)/shard_map/ppermute | solution.py:45
  16.2 10.1 %collective-permute-start.3 = (bf16[16,8192]{1,0:T(8,128)(2,1)S(1)}, bf16[16,8192]{1,0:T(8,128)(2,1)S(1)}, u32[]{:S(2)}, u32[]{:S(2)}) collective-permute-start(bf16[16,8192]{1,0:T(8,128)(2,1)S(1)} %bitcast.80), channel_id=1, source_target_pairs={{0,3},{1,0},{2,1},{3,2},{4,7},{5,4},{6,5},{7,6},{8,11},{9,8},{10,9... | collective-permute-start | bytes 786440 | tf_op jit(solution)/shard_map/ppermute | solution.py:45
  17.5 8.6 %collective-permute-start.7 = (bf16[2,112,128]{2,1,0:T(8,128)(2,1)S(1)}, bf16[2,112,128]{2,1,0:T(8,128)(2,1)S(1)}, u32[]{:S(2)}, u32[]{:S(2)}) collective-permute-start(bf16[2,112,128]{2,1,0:T(8,128)(2,1)S(1)} %pad_maximum_fusion.3), channel_id=1, source_target_pairs={{0,128},{1,129},{2,130},{3,131},{4,132},{5,133},{6,134},{7,135},{8... | collective-permute-start | bytes 172040 | tf_op jit(solution)/shard_map/ppermute | solution.py:45
  26.3 19.9 %collective-permute-start.4 = (bf16[64,8192]{1,0:T(8,128)(2,1)S(1)}, bf16[64,8192]{1,0:T(8,128)(2,1)S(1)}, u32[]{:S(2)}, u32[]{:S(2)}) collective-permute-start(bf16[64,8192]{1,0:T(8,128)(2,1)S(1)} %bitcast.70), channel_id=1, source_target_pairs={{0,8},{1,9},{2,10},{3,11},{4,12},{5,13},{6,14},{7,15},{8,16},{9,17... | collective-permute-start | bytes 3145736 | tf_op jit(solution)/shard_map/ppermute | solution.py:45
  28.0 18.2 %collective-permute-start.5 = (bf16[64,8192]{1,0:T(8,128)(2,1)S(1)}, bf16[64,8192]{1,0:T(8,128)(2,1)S(1)}, u32[]{:S(2)}, u32[]{:S(2)}) collective-permute-start(bf16[64,8192]{1,0:T(8,128)(2,1)S(1)} %bitcast.71), channel_id=1, source_target_pairs={{0,24},{1,25},{2,26},{3,27},{4,28},{5,29},{6,30},{7,31},{8,0},{9,1... | collective-permute-start | bytes 3145736 | tf_op jit(solution)/shard_map/ppermute | solution.py:45
  29.7 4.6 %collective-permute-start.8 = (bf16[4,64,128]{2,1,0:T(8,128)(2,1)S(1)}, bf16[4,64,128]{2,1,0:T(8,128)(2,1)S(1)}, u32[]{:S(2)}, u32[]{:S(2)}) collective-permute-start(bf16[4,64,128]{2,1,0:T(8,128)(2,1)S(1)} %slice.39), channel_id=1, source_target_pairs={{0,4},{1,5},{2,6},{3,7},{4,0},{5,1},{6,2},{7,3},{8,12},{9,13},{10,... | collective-permute-start | bytes 196616 | tf_op jit(solution)/shard_map/ppermute | solution.py:45
  30.9 23.6 %collective-permute-start.24 = (bf16[32,128]{1,0:T(8,128)(2,1)S(1)}, bf16[32,128]{1,0:T(8,128)(2,1)S(1)}, u32[]{:S(2)}, u32[]{:S(2)}) collective-permute-start(bf16[32,128]{1,0:T(8,128)(2,1)S(1)} %bitcast.88), channel_id=1, source_target_pairs={{0,1},{1,0},{2,3},{3,2},{4,5},{5,4},{6,7},{7,6},{8,9},{9,8},{10,11... | collective-permute-start | bytes 24584 | tf_op jit(solution)/shard_map/ppermute | solution.py:45
  34.3 6.3 %collective-permute-start.9 = (bf16[2,4,64,128]{3,2,1,0:T(8,128)(2,1)S(1)}, bf16[2,4,64,128]{3,2,1,0:T(8,128)(2,1)S(1)}, u32[]{:S(2)}, u32[]{:S(2)}) collective-permute-start(bf16[2,4,64,128]{3,2,1,0:T(8,128)(2,1)S(1)} %bitcast_dynamic-update-slice_fusion.10), channel_id=1, source_target_pairs={{0,1},{1,2},{2,3},{3,0},{4,5},{5,6},{6,7},{7,4},{8,9},{9,10},{10,1... | collective-permute-start | bytes 393224 | tf_op jit(solution)/shard_map/ppermute | solution.py:45
  35.1 8.2 %collective-permute-start.10 = (bf16[2,4,64,128]{3,2,1,0:T(8,128)(2,1)S(1)}, bf16[2,4,64,128]{3,2,1,0:T(8,128)(2,1)S(1)}, u32[]{:S(2)}, u32[]{:S(2)}) collective-permute-start(bf16[2,4,64,128]{3,2,1,0:T(8,128)(2,1)S(1)} %bitcast_dynamic-update-slice_fusion.10), channel_id=1, source_target_pairs={{0,2},{1,3},{2,0},{3,1},{4,6},{5,7},{6,4},{7,5},{8,10},{9,11},{10,... | collective-permute-start | bytes 393224 | tf_op jit(solution)/shard_map/ppermute | solution.py:45
  40.6 5.0 %collective-permute-start.11 = (bf16[2,4,64,128]{3,2,1,0:T(8,128)(2,1)S(1)}, bf16[2,4,64,128]{3,2,1,0:T(8,128)(2,1)S(1)}, u32[]{:S(2)}, u32[]{:S(2)}) collective-permute-start(bf16[2,4,64,128]{3,2,1,0:T(8,128)(2,1)S(1)} %bitcast_dynamic-update-slice_fusion.10), channel_id=1, source_target_pairs={{0,3},{1,0},{2,1},{3,2},{4,7},{5,4},{6,5},{7,6},{8,11},{9,8},{10,9... | collective-permute-start | bytes 393224 | tf_op jit(solution)/shard_map/ppermute | solution.py:45
  46.2 10.7 %collective-permute-start.12 = (bf16[4,2,4,64,128]{4,3,2,1,0:T(8,128)(2,1)}, bf16[4,2,4,64,128]{4,3,2,1,0:T(8,128)(2,1)}, u32[]{:S(2)}, u32[]{:S(2)}) collective-permute-start(bf16[4,2,4,64,128]{4,3,2,1,0:T(8,128)(2,1)} %bitcast_dynamic-update-slice_fusion.4.refs_0_), channel_id=1, source_target_pairs={{0,8},{1,9},{2,10},{3,11},{4,12},{5,13},{6,14},{7,15},{8,16},{9,17... | collective-permute-start | bytes 1572872 | tf_op jit(solution)/shard_map/ppermute | solution.py:45
  48.0 9.5 %collective-permute-start.13 = (bf16[4,2,4,64,128]{4,3,2,1,0:T(8,128)(2,1)}, bf16[4,2,4,64,128]{4,3,2,1,0:T(8,128)(2,1)}, u32[]{:S(2)}, u32[]{:S(2)}) collective-permute-start(bf16[4,2,4,64,128]{4,3,2,1,0:T(8,128)(2,1)} %bitcast_dynamic-update-slice_fusion.4.refs_0_), channel_id=1, source_target_pairs={{0,24},{1,25},{2,26},{3,27},{4,28},{5,29},{6,30},{7,31},{8,0},{9,1... | collective-permute-start | bytes 1572872 | tf_op jit(solution)/shard_map/ppermute | solution.py:45
  50.4 12.5 %collective-permute-start.16 = (bf16[64,4096]{1,0:T(8,128)(2,1)}, bf16[64,4096]{1,0:T(8,128)(2,1)}, u32[]{:S(2)}, u32[]{:S(2)}) collective-permute-start(bf16[64,4096]{1,0:T(8,128)(2,1)} %slice.42), channel_id=1, source_target_pairs={{0,8},{1,9},{2,10},{3,11},{4,12},{5,13},{6,14},{7,15},{8,16},{9,17... | collective-permute-start | bytes 1572872 | tf_op jit(solution)/shard_map/ppermute | solution.py:45
  51.8 11.6 %collective-permute-start.17 = (bf16[64,4096]{1,0:T(8,128)(2,1)}, bf16[64,4096]{1,0:T(8,128)(2,1)}, u32[]{:S(2)}, u32[]{:S(2)}) collective-permute-start(bf16[64,4096]{1,0:T(8,128)(2,1)} %slice.43), channel_id=1, source_target_pairs={{0,24},{1,25},{2,26},{3,27},{4,28},{5,29},{6,30},{7,31},{8,0},{9,1... | collective-permute-start | bytes 1572872 | tf_op jit(solution)/shard_map/ppermute | solution.py:45
  54.5 8.3 %collective-permute-start.25 = (bf16[2,32,128]{2,1,0:T(8,128)(2,1)S(1)}, bf16[2,32,128]{2,1,0:T(8,128)(2,1)S(1)}, u32[]{:S(2)}, u32[]{:S(2)}) collective-permute-start(bf16[2,32,128]{2,1,0:T(8,128)(2,1)S(1)} %pad_maximum_fusion.5), channel_id=1, source_target_pairs={{0,2},{1,3},{2,0},{3,1},{4,6},{5,7},{6,4},{7,5},{8,10},{9,11},{10,... | collective-permute-start | bytes 49160 | tf_op jit(solution)/shard_map/ppermute | solution.py:45
  58.5 15.8 %collective-permute-start.14 = (bf16[2,2,4,64,128]{4,3,2,1,0:T(8,128)(2,1)S(1)}, bf16[2,2,4,64,128]{4,3,2,1,0:T(8,128)(2,1)S(1)}, u32[]{:S(2)}, u32[]{:S(2)}) collective-permute-start(bf16[2,2,4,64,128]{4,3,2,1,0:T(8,128)(2,1)S(1)} %slice.40), channel_id=1, source_target_pairs={{0,8},{1,9},{2,10},{3,11},{4,12},{5,13},{6,14},{7,15},{8,16},{9,17... | collective-permute-start | bytes 786440 | tf_op jit(solution)/shard_map/ppermute | solution.py:45
  60.9 13.4 %collective-permute-start.15 = (bf16[2,2,4,64,128]{4,3,2,1,0:T(8,128)(2,1)S(1)}, bf16[2,2,4,64,128]{4,3,2,1,0:T(8,128)(2,1)S(1)}, u32[]{:S(2)}, u32[]{:S(2)}) collective-permute-start(bf16[2,2,4,64,128]{4,3,2,1,0:T(8,128)(2,1)S(1)} %slice.41), channel_id=1, source_target_pairs={{0,24},{1,25},{2,26},{3,27},{4,28},{5,29},{6,30},{7,31},{8,0},{9,1... | collective-permute-start | bytes 786440 | tf_op jit(solution)/shard_map/ppermute | solution.py:45
  62.8 12.4 %collective-permute-start.18 = (bf16[4,2,4,64,128]{4,3,2,1,0:T(8,128)(2,1)}, bf16[4,2,4,64,128]{4,3,2,1,0:T(8,128)(2,1)S(1)}, u32[]{:S(2)}, u32[]{:S(2)}) collective-permute-start(bf16[4,2,4,64,128]{4,3,2,1,0:T(8,128)(2,1)} %bitcast_dynamic-update-slice_fusion.4.refs_0_), channel_id=1, source_target_pairs={{0,32},{1,33},{2,34},{3,35},{4,36},{5,37},{6,38},{7,39},{8,40},{9,... | collective-permute-start | bytes 1572872 | tf_op jit(solution)/shard_map/ppermute | solution.py:45
  62.9 13.4 %collective-permute-start.19 = (bf16[4,2,4,64,128]{4,3,2,1,0:T(8,128)(2,1)}, bf16[4,2,4,64,128]{4,3,2,1,0:T(8,128)(2,1)S(1)}, u32[]{:S(2)}, u32[]{:S(2)}) collective-permute-start(bf16[4,2,4,64,128]{4,3,2,1,0:T(8,128)(2,1)} %collective-permute-done.12.refs_1_), channel_id=1, source_target_pairs={{0,32},{1,33},{2,34},{3,35},{4,36},{5,37},{6,38},{7,39},{8,40},{9,... | collective-permute-start | bytes 1572872 | tf_op jit(solution)/shard_map/ppermute | solution.py:45
  63.4 12.9 %collective-permute-start.20 = (bf16[4,2,4,64,128]{4,3,2,1,0:T(8,128)(2,1)}, bf16[4,2,4,64,128]{4,3,2,1,0:T(8,128)(2,1)S(1)}, u32[]{:S(2)}, u32[]{:S(2)}) collective-permute-start(bf16[4,2,4,64,128]{4,3,2,1,0:T(8,128)(2,1)} %collective-permute-done.13.refs_2_), channel_id=1, source_target_pairs={{0,32},{1,33},{2,34},{3,35},{4,36},{5,37},{6,38},{7,39},{8,40},{9,... | collective-permute-start | bytes 1572872 | tf_op jit(solution)/shard_map/ppermute | solution.py:45
  74.3 1.7 %collective-permute-start.21 = (bf16[2,2,4,64,128]{4,3,2,1,0:T(8,128)(2,1)S(1)}, bf16[2,2,4,64,128]{4,3,2,1,0:T(8,128)(2,1)S(1)}, u32[]{:S(2)}, u32[]{:S(2)}) collective-permute-start(bf16[2,2,4,64,128]{4,3,2,1,0:T(8,128)(2,1)S(1)} %collective-permute-done.14.refs_3_), channel_id=1, source_target_pairs={{0,32},{1,33},{2,34},{3,35},{4,36},{5,37},{6,38},{7,39},{8,40},{9,... | collective-permute-start | bytes 786440 | tf_op jit(solution)/shard_map/ppermute | solution.py:45
  87.9 16.1 %collective-permute-start.26 = (bf16[64,8192]{1,0:T(8,128)(2,1)S(1)}, bf16[64,8192]{1,0:T(8,128)(2,1)S(1)}, u32[]{:S(2)}, u32[]{:S(2)}) collective-permute-start(bf16[64,8192]{1,0:T(8,128)(2,1)S(1)} %get-tuple-element.47), channel_id=1, source_target_pairs={{0,8},{1,9},{2,10},{3,11},{4,12},{5,13},{6,14},{7,15},{8,16},{9,17... | collective-permute-start | bytes 3145736 | tf_op jit(solution)/shard_map/ppermute | solution.py:45
  89.0 15.0 %collective-permute-start.27 = (bf16[64,8192]{1,0:T(8,128)(2,1)S(1)}, bf16[64,8192]{1,0:T(8,128)(2,1)S(1)}, u32[]{:S(2)}, u32[]{:S(2)}) collective-permute-start(bf16[64,8192]{1,0:T(8,128)(2,1)S(1)} %get-tuple-element.48), channel_id=1, source_target_pairs={{0,24},{1,25},{2,26},{3,27},{4,28},{5,29},{6,30},{7,31},{8,0},{9,1... | collective-permute-start | bytes 3145736 | tf_op jit(solution)/shard_map/ppermute | solution.py:45
  104.0 10.5 %collective-permute-start.28 = (bf16[64,4096]{1,0:T(8,128)(2,1)S(1)}, bf16[64,4096]{1,0:T(8,128)(2,1)S(1)}, u32[]{:S(2)}, u32[]{:S(2)}) collective-permute-start(bf16[64,4096]{1,0:T(8,128)(2,1)S(1)} %slice_add_fusion.1), channel_id=1, source_target_pairs={{0,8},{1,9},{2,10},{3,11},{4,12},{5,13},{6,14},{7,15},{8,16},{9,17... | collective-permute-start | bytes 1572872 | tf_op jit(solution)/shard_map/ppermute | solution.py:45
  105.2 9.3 %collective-permute-start.29 = (bf16[64,4096]{1,0:T(8,128)(2,1)S(1)}, bf16[64,4096]{1,0:T(8,128)(2,1)S(1)}, u32[]{:S(2)}, u32[]{:S(2)}) collective-permute-start(bf16[64,4096]{1,0:T(8,128)(2,1)S(1)} %slice_add_fusion), channel_id=1, source_target_pairs={{0,24},{1,25},{2,26},{3,27},{4,28},{5,29},{6,30},{7,31},{8,0},{9,1... | collective-permute-start | bytes 1572872 | tf_op jit(solution)/shard_map/ppermute | solution.py:45
  115.6 6.4 %collective-permute-start.32 = (bf16[16,8192]{1,0:T(8,128)(2,1)S(1)}, bf16[16,8192]{1,0:T(8,128)(2,1)S(1)}, u32[]{:S(2)}, u32[]{:S(2)}) collective-permute-start(bf16[16,8192]{1,0:T(8,128)(2,1)S(1)} %get-tuple-element.56), channel_id=1, source_target_pairs={{0,3},{1,0},{2,1},{3,2},{4,7},{5,4},{6,5},{7,6},{8,11},{9,8},{10,9... | collective-permute-start | bytes 786440 | tf_op jit(solution)/shard_map/ppermute | solution.py:45
  117.4 8.0 %collective-permute-start.31 = (bf16[16,8192]{1,0:T(8,128)(2,1)S(1)}, bf16[16,8192]{1,0:T(8,128)(2,1)S(1)}, u32[]{:S(2)}, u32[]{:S(2)}) collective-permute-start(bf16[16,8192]{1,0:T(8,128)(2,1)S(1)} %get-tuple-element.55), channel_id=1, source_target_pairs={{0,2},{1,3},{2,0},{3,1},{4,6},{5,7},{6,4},{7,5},{8,10},{9,11},{10,... | collective-permute-start | bytes 786440 | tf_op jit(solution)/shard_map/ppermute | solution.py:45
  119.1 9.1 %collective-permute-start.30 = (bf16[16,8192]{1,0:T(8,128)(2,1)S(1)}, bf16[16,8192]{1,0:T(8,128)(2,1)S(1)}, u32[]{:S(2)}, u32[]{:S(2)}) collective-permute-start(bf16[16,8192]{1,0:T(8,128)(2,1)S(1)} %get-tuple-element.54), channel_id=1, source_target_pairs={{0,1},{1,2},{2,3},{3,0},{4,5},{5,6},{6,7},{7,4},{8,9},{9,10},{10,1... | collective-permute-start | bytes 786440 | tf_op jit(solution)/shard_map/ppermute | solution.py:45
  128.3 5.1 %collective-permute-start.33 = (bf16[8,8192]{1,0:T(8,128)(2,1)S(1)}, bf16[8,8192]{1,0:T(8,128)(2,1)S(1)}, u32[]{:S(2)}, u32[]{:S(2)}) collective-permute-start(bf16[8,8192]{1,0:T(8,128)(2,1)S(1)} %fusion.4), channel_id=1, source_target_pairs={{0,4},{1,5},{2,6},{3,7},{4,0},{5,1},{6,2},{7,3},{8,12},{9,13},{10,... | collective-permute-start | bytes 393224 | tf_op jit(solution)/shard_map/ppermute | solution.py:45
  (11 other events, 140.5 us)

commit v2 on v1

--- a/solution.py
+++ b/solution.py
@@ -108,64 +108,6 @@
 
 def spec_smem():
     return pl.BlockSpec(memory_space=pltpu.SMEM)
-
-
-def project_kernel(
-    eight_ref, one_ref, left_ref, right_ref, three_ref, query_ref, pair_ref, out_ref, total
-):
-    step = pl.program_id(0)
-    steps = pl.num_programs(0)
-
-    @pl.when(step == 0)
-    def _():
-        total[...] = jnp.zeros_like(total)
-
-    def add(two_ref):
-        rows = jnp.concatenate(
-            [eight_ref[...], one_ref[...], two_ref[...], three_ref[...]], axis=0
-        )
-        width = query_ref.shape[1]
-        total[:, :width] += jnp.dot(rows, query_ref[...], preferred_element_type=jnp.float32)
-        total[:, width:] += jnp.dot(rows, pair_ref[...], preferred_element_type=jnp.float32)
-
-    @pl.when(step < steps // 2)
-    def _():
-        add(left_ref)
-
-    @pl.when(step >= steps // 2)
-    def _():
-        add(right_ref)
-
-    @pl.when(step == steps - 1)
-    def _():
-        out_ref[...] = total[...]
-
-
-def project_rows(eight, one, left_2, right_2, three, query_weight, pair_weight):
-    tile = 1024
-    steps = eight.shape[1] // tile
-    width = query_weight.shape[1]
-    whole = pl.BlockSpec((64, tile), lambda j: (0, j))
-    return pl.pallas_call(
-        project_kernel,
-        grid=(steps,),
-        in_specs=[
-            whole,
-            whole,
-            pl.BlockSpec((64, tile), lambda j: (0, jnp.minimum(j, steps // 2 - 1))),
-            pl.BlockSpec((64, tile), lambda j: (0, jnp.maximum(j - steps // 2, 0))),
-            whole,
-            pl.BlockSpec((tile, width), lambda j: (j, 0)),
-            pl.BlockSpec((tile, width), lambda j: (j, 0)),
-        ],
-        out_specs=pl.BlockSpec((256, 2 * width), lambda j: (0, 0)),
-        out_shape=jax.ShapeDtypeStruct((256, 2 * width), jnp.float32),
-        scratch_shapes=[pltpu.VMEM((256, 2 * width), jnp.float32)],
-        compiler_params=pltpu.CompilerParams(vmem_limit_bytes=12 * 2**20),
-        cost_estimate=pl.CostEstimate(
-            flops=2 * 256 * 512 * 8192, bytes_accessed=12 * 2**20, transcendentals=0
-        ),
-    )(eight, one, left_2, right_2, three, query_weight, pair_weight)
 
 
 def outer(left, right):
@@ -237,32 +179,25 @@
 def attend_kernel(
     spot_ref,
     lengths_ref,
-    frozen_ref,
-    parts_ref,
-    query_up_ref,
-    key_up_ref,
-    value_up_ref,
-    cosine_ref,
-    sine_ref,
-    cache_ref,
-    down_ref,
-    ahead_ref,
-    inner_ref,
-    rows,
-    found,
+    *refs,
 ):
+    query_refs, pair_refs = refs[:4], refs[4:8]
+    parts_ref, query_up_ref, key_up_ref, value_up_ref = refs[8:12]
+    cosine_ref, sine_ref, cache_ref, down_ref, ahead_ref, inner_ref, rows, found = refs[12:]
     half = jnp.bfloat16
     first_core = spot_ref[0] == 0
     last = spot_ref[1]
     for s in range(4):
         k = lax.rem(last - s + 4, 4)
         inner = parts_ref[64 * s : 64 * s + 64].astype(half)
-        frozen = frozen_ref[64 * s : 64 * s + 64]
-        rows[k, :, :256] = frozen[:, :256] + adapter_scale * outer(inner[:, :64], query_up_ref[...])
-        rows[k, :, 256:384] = frozen[:, 256:384] + adapter_scale * outer(
+        pair = pair_refs[s]
+        rows[k, :, :256] = query_refs[s][...] + adapter_scale * outer(
+            inner[:, :64], query_up_ref[...]
+        )
+        rows[k, :, 256:384] = pair[:, :128] + adapter_scale * outer(
             inner[:, 64:128], key_up_ref[...]
         )
-        rows[k, :, 384:] = frozen[:, 384:] + adapter_scale * outer(
+        rows[k, :, 384:] = pair[:, 128:] + adapter_scale * outer(
             inner[:, 128:192], value_up_ref[...]
         )
 
@@ -325,7 +260,7 @@
 
 
 def attend_rows(spot, lengths, frozen, parts, ups, cosine, sine, cache, down):
-    operands = (frozen, parts, *ups, cosine, sine, cache, down)
+    operands = (*frozen, parts, *ups, cosine, sine, cache, down)
     return pl.pallas_call(
         attend_kernel,
         in_specs=[spec_smem(), spec_smem()]
@@ -346,108 +281,55 @@
     )(spot, lengths, *operands)
 
 
-def sum_kernel(
-    spot_ref,
-    own_ref,
-    plus_ref,
-    minus_ref,
-    left_ref,
-    right_ref,
-    mine_ref,
-    one_ref,
-    two_ref,
-    three_ref,
-    total,
-):
-    step = pl.program_id(0)
-    at_left = step < pl.num_programs(0) // 2
-    own = own_ref[...].astype(jnp.float32)
-
-    @pl.when(at_left)
-    def _():
-        total[...] = own + minus_ref[...].astype(jnp.float32) + left_ref[...].astype(jnp.float32)
-
-    @pl.when(jnp.logical_not(at_left))
-    def _():
-        total[...] = own + plus_ref[...].astype(jnp.float32) + right_ref[...].astype(jnp.float32)
-
-    middle = spot_ref[0]
-    for s, ref in enumerate((mine_ref, one_ref, two_ref, three_ref)):
-        at = pl.ds(pl.multiple_of(16 * lax.rem(middle + s, 4), 16), 16)
+def sum_kernel(spot_ref, *refs):
+    total = refs[8]
+    total[...] = sum(ref[...].astype(jnp.float32) for ref in refs[:4])
+    for s, ref in enumerate(refs[4:8]):
+        at = pl.ds(pl.multiple_of(16 * lax.rem(spot_ref[0] + s, 4), 16), 16)
         ref[...] = total[at, :].astype(ref.dtype)
 
 
-def sum_rows(spot, own, plus, minus, left, right):
+def sum_rows(spot, blocks):
     tile = 2048
-    steps = own.shape[1] // tile
-    width = own.shape[1]
-    last_left = steps // 2 - 1
-    whole = pl.BlockSpec((64, tile), lambda j: (0, j))
-    out = pl.BlockSpec((16, tile), lambda j: (0, j))
+    width = blocks[0].shape[1]
     return pl.pallas_call(
         sum_kernel,
-        grid=(steps,),
-        in_specs=[
-            spec_smem(),
-            whole,
-            pl.BlockSpec((64, tile), lambda j: (0, jnp.maximum(j, steps // 2))),
-            pl.BlockSpec((64, tile), lambda j: (0, jnp.minimum(j, last_left))),
-            pl.BlockSpec((64, tile), lambda j: (0, jnp.minimum(j, last_left))),
-            pl.BlockSpec((64, tile), lambda j: (0, jnp.maximum(j - steps // 2, 0))),
-        ],
-        out_specs=[out] * 4,
+        grid=(width // tile,),
+        in_specs=[spec_smem()] + [pl.BlockSpec((64, tile), lambda j: (0, j))] * 4,
+        out_specs=[pl.BlockSpec((16, tile), lambda j: (0, j))] * 4,
         out_shape=[jax.ShapeDtypeStruct((16, width), jnp.float32)]
         + [jax.ShapeDtypeStruct((16, width), jnp.bfloat16)] * 3,
         scratch_shapes=[pltpu.VMEM((64, tile), jnp.float32)],
-        compiler_params=pltpu.CompilerParams(vmem_limit_bytes=12 * 2**20),
+        compiler_params=pltpu.CompilerParams(vmem_limit_bytes=14 * 2**20),
         cost_estimate=pl.CostEstimate(
-            flops=2 * 64 * 64 * 1024, bytes_accessed=5 * 2**20, transcendentals=0
+            flops=4 * 64 * 8192, bytes_accessed=5 * 2**20, transcendentals=0
         ),
-    )(spot, own, plus, minus, left, right)
-
-
-def out_kernel(
-    rows_ref, inner_ref, weight_ref, up_ref, own_ref, plus_ref, minus_ref, left_ref, right_ref
-):
-    at_left = pl.program_id(0) < pl.num_programs(0) // 2
+    )(spot, *blocks)
+
+
+def out_kernel(rows_ref, inner_ref, weight_ref, up_ref, *out_refs):
     part = jnp.dot(rows_ref[...], weight_ref[...], preferred_element_type=jnp.float32)
     part = part + adapter_scale * outer(inner_ref[:, :64], up_ref[:, 64:])
     part = part.astype(jnp.bfloat16)
-    own_ref[...] = part[:64]
-
-    @pl.when(at_left)
-    def _():
-        left_ref[...] = part[64:128]
-        plus_ref[...] = part[128:192]
-        minus_ref[...] = part[192:]
-
-    @pl.when(jnp.logical_not(at_left))
-    def _():
-        plus_ref[...] = part[64:128]
-        minus_ref[...] = part[128:192]
-        right_ref[...] = part[192:]
+    for s in range(4):
+        out_refs[s][...] = part[64 * s : 64 * s + 64]
 
 
 def out_pieces(rows, inner, weight, up_factor):
     tile = 2048
     depth, width = weight.shape
-    steps = width // tile
-    whole = pl.BlockSpec((64, tile), lambda j: (0, j))
-    left = pl.BlockSpec((64, tile), lambda j: (0, jnp.minimum(j, steps // 2 - 1)))
-    right = pl.BlockSpec((64, tile), lambda j: (0, jnp.maximum(j - steps // 2, 0)))
     return pl.pallas_call(
         out_kernel,
-        grid=(steps,),
+        grid=(width // tile,),
         in_specs=[
             pl.BlockSpec(rows.shape, lambda j: (0, 0)),
             pl.BlockSpec(inner.shape, lambda j: (0, 0)),
             pl.BlockSpec((depth, tile), lambda j: (0, j)),
             pl.BlockSpec((tile, 128), lambda j: (j, 0)),
         ],
-        out_specs=[whole, whole, whole, left, right],
-        out_shape=[jax.ShapeDtypeStruct((64, width), jnp.bfloat16)] * 3
-        + [jax.ShapeDtypeStruct((64, width // 2), jnp.bfloat16)] * 2,
-        compiler_params=pltpu.CompilerParams(vmem_limit_bytes=14 * 2**20),
+        out_specs=[pl.BlockSpec((64, tile), lambda j: (0, j))] * 4,
+        out_shape=[jax.ShapeDtypeStruct((64, width), jnp.bfloat16)] * 4,
+        compiler_params=pltpu.CompilerParams(vmem_limit_bytes=12 * 2**20),
         cost_estimate=pl.CostEstimate(
             flops=2 * 256 * 256 * 8192, bytes_accessed=8 * 2**20, transcendentals=0
         ),
@@ -509,12 +391,13 @@
     band = placed([band, permute(band, z_swap())], zl)
     band = gather4(band, middle_shift, middle)
     from_1, from_3, band = lax.optimization_barrier((from_1, from_3, band))
+    late, _ = lax.optimization_barrier((packed[:, 64:], band))
     left_2 = permute(from_1[:, :4096], last_shift(1))
     right_2 = permute(from_3[:, 4096:], last_shift(3))
     band_1 = permute(band, last_shift(1))
     band_3 = permute(band, last_shift(3))
 
-    own = jnp.swapaxes(both_of(packed[:, 64:], core, core_swap()), 0, 1).reshape(8, 48, 128)
+    own = jnp.swapaxes(both_of(late, core, core_swap()), 0, 1).reshape(8, 48, 128)
     down_out = own[:, :32].reshape(256, 128)
     query_up = down_out[:, 64:]
     narrow = both_of(own[:, 32:36].reshape(32, 128), y & 1, y_flip(1))
@@ -525,11 +408,13 @@
     band_1, band_3 = lax.optimization_barrier((band_1, band_3))
     far_low = permute(band_1[:2], last_shift(1))
     far_high = permute(band_3[2:], last_shift(3))
-    frozen = project_rows(
-        eight, from_1, left_2, right_2, from_3, query_weight, w_keyvalue.reshape(8192, 256)
-    )
-    far_low, far_high, frozen = lax.optimization_barrier((far_low, far_high, frozen))
-    bands = (band, band_1, band_3, far_low, far_high)
+    bands, _, _ = lax.optimization_barrier(
+        ((band, band_1, band_3, far_low, far_high), left_2, right_2)
+    )
+    frozen = []
+    for weight in (query_weight, w_keyvalue[0]):
+        far = dot32(left_2, weight[:4096]) + dot32(right_2, weight[4096:])
+        frozen += [dot32(eight, weight), dot32(from_1, weight), far, dot32(from_3, weight)]
     bands = bands + tuple(permute(block, core_swap()) for block in bands)
     spot = jnp.stack([core, last, middle]).astype(jnp.int32)
     parts, out_up = inner_rows(spot, (eight, from_1, left_2, right_2, from_3), bands)
@@ -550,16 +435,9 @@
         down_out,
     )
 
-    own, plus, minus, left_1, right_3 = out_pieces(ahead, out_inner, output_weight, out_up)
-    got_plus = permute(plus, last_shift(1))
-    got_minus = permute(minus, last_shift(3))
-    got_plus, got_minus = lax.optimization_barrier((got_plus, got_minus))
-    got_left_1 = permute(left_1 + got_plus[:, :4096], last_shift(1))
-    got_right_3 = permute(right_3 + got_minus[:, 4096:], last_shift(3))
-
-    total, *sent = sum_rows(
-        middle.reshape(1), own, got_plus, got_minus, got_left_1, got_right_3
-    )
+    pieces = out_pieces(ahead, out_inner, output_weight, out_up)
+    arrived = [pieces[0]] + [permute(pieces[s], last_shift(s)) for s in (2, 1, 3)]
+    total, *sent = sum_rows(middle.reshape(1), arrived)
     for s, block in zip((1, 2, 3), sent):
         total = total + permute(block, middle_shift(s)).astype(jnp.float32)
     total = total.reshape(2, 8, 8192)

time: 135 us -> 131 us (0.970)
  local copies, waits for them, and re-layouts: 13.2 us -> 1.15 us
  waiting for transfers between devices: 49.4 us -> 58.7 us
  Pallas kernels: 18.9 us -> 11.2 us
  matrix products: 0 us -> 6.72 us
    ppermute x34 -> x33, waiting for transfers between devices: 49.4 us -> 58.7 us  [permute(): return lax.ppermute(block, AXES, source_to_target)]
    dot_general x0 -> x10, matrix products: none -> 6.72 us  [dot32(): return jnp.dot(left, right, preferred_element_type=jnp.float32)]
    pallas_call x3 -> x2, Pallas kernels: 11.6 us -> 5.14 us  [the longest x1 3.76 us: out_pieces(): pl.pallas_call(out_kernel, grid=(width // tile,), in_specs=[pl.BlockSpec(...]
    unnamed x18 -> x12, local copies, waits for them, and re-layouts: 4.41 us -> 0.04 us
    dynamic_update_slice x11, local copies, waits for them, and re-layouts: 2.8 us -> 0.23 us  [placed(): out = lax.dynamic_update_index_in_dim(out, block, (here - s) % count, 0)]
    ppermute x34 -> x33, starting transfers between devices: 44.3 us -> 44.8 us  [permute(): return lax.ppermute(block, AXES, source_to_target)]
  transfers between devices with their start and end apart: 34 -> 33, of which waited for: 16 -> 20; matrix products, arithmetic and copies ran while one was open for 10% -> 9% of each run, Pallas kernels for 5% -> 0%
where the time goes in v2:
time: 131 us; the launch traced here: 130 us
  waiting for transfers between devices  58.7 us (45%)
  starting transfers between devices  44.8 us (34%)
  Pallas kernels  11.2 us (9%)
  other arithmetic  6.91 us (5%)
  matrix products  6.72 us (5%)
    ppermute x33, waiting for transfers between devices, permute(): return lax.ppermute(block, AXES, source_to_target)  58.7 us
    ppermute x33, starting transfers between devices, permute(): return lax.ppermute(block, AXES, source_to_target)  44.8 us
    dot_general x10, matrix products, dot32(): return jnp.dot(left, right, preferred_element_type=jnp.float32)  6.72 us
    pallas_call x1, Pallas kernels, out_pieces(): pl.pallas_call(out_kernel, grid=(width // tile,), in_specs=[pl.BlockSpec(...  3.76 us
    pallas_call x1, Pallas kernels, inner_rows(): pl.pallas_call(inner_kernel, in_specs=[spec_smem()] + [pl.BlockSpec(memor...  3.2 us
    pallas_call x1, Pallas kernels, attend_rows(): pl.pallas_call(attend_kernel, in_specs=[spec_smem(), spec_smem()] + [pl.B...  2.83 us
  transfers between devices with their start and end apart: 33, of which 20 were waited for; matrix products, arithmetic and copies ran while one was open for 9% of the time, Pallas kernels for 0%

profile of v2, /device:TPU:64, one launch (start us, length us, event | category | flops | bytes accessed | tf_op | source)
XLA Modules:
  0.0 130.0 jit_solution(14104172717799166294)
XLA Ops:
  2.2 2.0 %collective-permute-start = (bf16[8,8192]{1,0:T(8,128)(2,1)S(1)}, bf16[8,8192]{1,0:T(8,128)(2,1)S(1)}, u32[]{:S(2)}, u32[]{:S(2)}) collective-permute-start(bf16[8,8192]{1,0:T(8,128)(2,1)S(1)} %get-tuple-element.58), channel_id=1, source_target_pairs={{0,4},{1,5},{2,6},{3,7},{4,0},{5,1},{6,2},{7,3},{8,12},{9,13},{10,... | collective-permute-start | bytes 393224 | tf_op jit(solution)/shard_map/ppermute | solution.py:45
  8.6 3.0 %collective-permute-done.6 = bf16[112,128]{1,0:T(8,128)(2,1)S(1)} collective-permute-done((bf16[112,128]{1,0:T(8,128)(2,1)S(1)}, bf16[112,128]{1,0:T(8,128)(2,1)S(1)}, u32[]{:S(2)}, u32[]{:S(2)}) %collective-permute-start.6) | collective-permute-done | bytes 28704 | tf_op jit(solution)/shard_map/ppermute | solution.py:45
  11.6 1.7 %collective-permute-start.1 = (bf16[16,8192]{1,0:T(8,128)(2,1)S(1)}, bf16[16,8192]{1,0:T(8,128)(2,1)S(1)}, u32[]{:S(2)}, u32[]{:S(2)}) collective-permute-start(bf16[16,8192]{1,0:T(8,128)(2,1)S(1)} %bitcast.105), channel_id=1, source_target_pairs={{0,1},{1,2},{2,3},{3,0},{4,5},{5,6},{6,7},{7,4},{8,9},{9,10},{10,1... | collective-permute-start | bytes 786440 | tf_op jit(solution)/shard_map/ppermute | solution.py:45
  13.3 2.9 %collective-permute-start.2 = (bf16[16,8192]{1,0:T(8,128)(2,1)S(1)}, bf16[16,8192]{1,0:T(8,128)(2,1)S(1)}, u32[]{:S(2)}, u32[]{:S(2)}) collective-permute-start(bf16[16,8192]{1,0:T(8,128)(2,1)S(1)} %bitcast.106), channel_id=1, source_target_pairs={{0,2},{1,3},{2,0},{3,1},{4,6},{5,7},{6,4},{7,5},{8,10},{9,11},{10,... | collective-permute-start | bytes 786440 | tf_op jit(solution)/shard_map/ppermute | solution.py:45
  17.5 4.5 %collective-permute-start.7 = (bf16[2,112,128]{2,1,0:T(8,128)(2,1)S(1)}, bf16[2,112,128]{2,1,0:T(8,128)(2,1)S(1)}, u32[]{:S(2)}, u32[]{:S(2)}) collective-permute-start(bf16[2,112,128]{2,1,0:T(8,128)(2,1)S(1)} %pad_maximum_fusion.3), channel_id=1, source_target_pairs={{0,128},{1,129},{2,130},{3,131},{4,132},{5,133},{6,134},{7,135},{8... | collective-permute-start | bytes 172040 | tf_op jit(solution)/shard_map/ppermute | solution.py:45
  22.2 3.6 %collective-permute-done.7 = bf16[2,112,128]{2,1,0:T(8,128)(2,1)S(1)} collective-permute-done((bf16[2,112,128]{2,1,0:T(8,128)(2,1)S(1)}, bf16[2,112,128]{2,1,0:T(8,128)(2,1)S(1)}, u32[]{:S(2)}, u32[]{:S(2)}) %collective-permute-start.7) | collective-permute-done | bytes 57376 | tf_op jit(solution)/shard_map/ppermute | solution.py:45
  26.0 2.0 %collective-permute-start.4 = (bf16[64,8192]{1,0:T(8,128)(2,1)S(1)}, bf16[64,8192]{1,0:T(8,128)(2,1)S(1)}, u32[]{:S(2)}, u32[]{:S(2)}) collective-permute-start(bf16[64,8192]{1,0:T(8,128)(2,1)S(1)} %bitcast.97), channel_id=1, source_target_pairs={{0,8},{1,9},{2,10},{3,11},{4,12},{5,13},{6,14},{7,15},{8,16},{9,17... | collective-permute-start | bytes 3145736 | tf_op jit(solution)/shard_map/ppermute | solution.py:45
  31.8 1.8 %collective-permute-done.8 = bf16[4,64,128]{2,1,0:T(8,128)(2,1)S(1)} collective-permute-done((bf16[4,64,128]{2,1,0:T(8,128)(2,1)S(1)}, bf16[4,64,128]{2,1,0:T(8,128)(2,1)S(1)}, u32[]{:S(2)}, u32[]{:S(2)}) %collective-permute-start.8) | collective-permute-done | bytes 65568 | tf_op jit(solution)/shard_map/ppermute | solution.py:45
  34.3 1.9 %collective-permute-start.10 = (bf16[2,4,64,128]{3,2,1,0:T(8,128)(2,1)S(1)}, bf16[2,4,64,128]{3,2,1,0:T(8,128)(2,1)S(1)}, u32[]{:S(2)}, u32[]{:S(2)}) collective-permute-start(bf16[2,4,64,128]{3,2,1,0:T(8,128)(2,1)S(1)} %bitcast_dynamic-update-slice_fusion.10), channel_id=1, source_target_pairs={{0,2},{1,3},{2,0},{3,1},{4,6},{5,7},{6,4},{7,5},{8,10},{9,11},{10,... | collective-permute-start | bytes 393224 | tf_op jit(solution)/shard_map/ppermute | solution.py:45
  37.7 3.1 %collective-permute-done.9 = bf16[2,4,64,128]{3,2,1,0:T(8,128)(2,1)S(1)} collective-permute-done((bf16[2,4,64,128]{3,2,1,0:T(8,128)(2,1)S(1)}, bf16[2,4,64,128]{3,2,1,0:T(8,128)(2,1)S(1)}, u32[]{:S(2)}, u32[]{:S(2)}) %collective-permute-start.9) | collective-permute-done | bytes 131104 | tf_op jit(solution)/shard_map/ppermute | solution.py:45
  40.8 2.5 %collective-permute-done.10 = bf16[2,4,64,128]{3,2,1,0:T(8,128)(2,1)S(1)} collective-permute-done((bf16[2,4,64,128]{3,2,1,0:T(8,128)(2,1)S(1)}, bf16[2,4,64,128]{3,2,1,0:T(8,128)(2,1)S(1)}, u32[]{:S(2)}, u32[]{:S(2)}) %collective-permute-start.10) | collective-permute-done | bytes 131104 | tf_op jit(solution)/shard_map/ppermute | solution.py:45
  43.4 1.5 %collective-permute-done.4.one_ref = bf16[64,8192]{1,0:T(8,128)(2,1)S(1)} collective-permute-done((bf16[64,8192]{1,0:T(8,128)(2,1)S(1)}, bf16[64,8192]{1,0:T(8,128)(2,1)S(1)}, u32[]{:S(2)}, u32[]{:S(2)}) %collective-permute-start.4) | collective-permute-done | bytes 1048608 | tf_op jit(solution)/shard_map/ppermute | solution.py:45
  46.6 2.2 %collective-permute-start.15 = (bf16[4,2,4,64,128]{4,3,2,1,0:T(8,128)(2,1)S(1)}, bf16[4,2,4,64,128]{4,3,2,1,0:T(8,128)(2,1)S(1)}, u32[]{:S(2)}, u32[]{:S(2)}) collective-permute-start(bf16[4,2,4,64,128]{4,3,2,1,0:T(8,128)(2,1)S(1)} %bitcast_dynamic-update-slice_fusion.4.refs_0_), channel_id=1, source_target_pairs={{0,24},{1,25},{2,26},{3,27},{4,28},{5,29},{6,30},{7,31},{8,0},{9,1... | collective-permute-start | bytes 1572872 | tf_op jit(solution)/shard_map/ppermute | solution.py:45
  51.7 2.6 %collective-permute-done.24 = bf16[32,128]{1,0:T(8,128)(2,1)S(1)} collective-permute-done((bf16[32,128]{1,0:T(8,128)(2,1)S(1)}, bf16[32,128]{1,0:T(8,128)(2,1)S(1)}, u32[]{:S(2)}, u32[]{:S(2)}) %collective-permute-start.24) | collective-permute-done | bytes 8224 | tf_op jit(solution)/shard_map/ppermute | solution.py:45
  56.0 3.2 %collective-permute-start.13 = (bf16[64,4096]{1,0:T(8,128)(2,1)S(1)}, bf16[64,4096]{1,0:T(8,128)(2,1)S(1)}, u32[]{:S(2)}, u32[]{:S(2)}) collective-permute-start(bf16[64,4096]{1,0:T(8,128)(2,1)S(1)} %slice.54), channel_id=1, source_target_pairs={{0,24},{1,25},{2,26},{3,27},{4,28},{5,29},{6,30},{7,31},{8,0},{9,1... | collective-permute-start | bytes 1572872 | tf_op jit(solution)/shard_map/ppermute | solution.py:45
  60.0 3.3 %collective-permute-start.17 = (bf16[2,2,4,64,128]{4,3,2,1,0:T(8,128)(2,1)S(1)}, bf16[2,2,4,64,128]{4,3,2,1,0:T(8,128)(2,1)S(1)}, u32[]{:S(2)}, u32[]{:S(2)}) collective-permute-start(bf16[2,2,4,64,128]{4,3,2,1,0:T(8,128)(2,1)S(1)} %slice.61), channel_id=1, source_target_pairs={{0,24},{1,25},{2,26},{3,27},{4,28},{5,29},{6,30},{7,31},{8,0},{9,1... | collective-permute-start | bytes 786440 | tf_op jit(solution)/shard_map/ppermute | solution.py:45
  63.3 2.6 %collective-permute-done.13.right_ref = bf16[64,4096]{1,0:T(8,128)(2,1)S(1)} collective-permute-done((bf16[64,4096]{1,0:T(8,128)(2,1)S(1)}, bf16[64,4096]{1,0:T(8,128)(2,1)S(1)}, u32[]{:S(2)}, u32[]{:S(2)}) %collective-permute-start.13) | collective-permute-done | bytes 524320 | tf_op jit(solution)/shard_map/ppermute | solution.py:45
  66.8 2.3 %collective-permute-done.16.refs_3_ = bf16[2,2,4,64,128]{4,3,2,1,0:T(8,128)(2,1)S(1)} collective-permute-done((bf16[2,2,4,64,128]{4,3,2,1,0:T(8,128)(2,1)S(1)}, bf16[2,2,4,64,128]{4,3,2,1,0:T(8,128)(2,1)S(1)}, u32[]{:S(2)}, u32[]{:S(2)}) %collective-permute-start.16) | collective-permute-done | bytes 262176 | tf_op jit(solution)/shard_map/ppermute | solution.py:45
  73.3 3.2 %shard_map.154 = (f32[256,256]{1,0:T(8,128)S(1)}, bf16[8192,128]{1,0:T(8,128)(2,1)S(1)}) custom-call(s32[3]{0:T(128)S(1)} %pad_add_fusion.spot_ref, bf16[64,8192]{1,0:T(8,128)(2,1)S(1)} %bitcast.101, bf16[64,8192]{1,0:T(8,128)(2,1)S(1)} %collective-permute-done.4.one_ref, bf16[64,4096]{1,0:T(8,128)(2,1)S(1)} %collective-permute-done.12.left_ref, ...), custom_call_target="tpu_custom_call" | custom-call | flops 1073741824 | bytes 10485760 | tf_op jit(solution)/shard_map/pallas_call | solution.py:162
  76.6 2.8 %shard_map.155 = (bf16[256,256]{1,0:T(8,128)(2,1)S(1)}, bf16[256,128]{1,0:T(8,128)(2,1)S(1)}) custom-call(s32[3]{0:T(128)S(1)} %pad_add_fusion.spot_ref, s32[4]{0:T(128)S(1)} %copy-done.2, f32[64,256]{1,0:T(8,128)S(1)} %fusion.30.refs_0_, f32[64,256]{1,0:T(8,128)S(1)} %fusion.31.refs_1_, f32[64,256]{1,0:T(8,128)S(1)} %fusion.16.refs_2_, ...), custom_call_target="tpu_custom_call" | custom-call | flops 83886080 | bytes 4194304 | tf_op jit(solution)/shard_map/pallas_call | solution.py:264
  79.4 3.8 %shard_map.156 = (bf16[64,8192]{1,0:T(8,128)(2,1)S(1)}, bf16[64,8192]{1,0:T(8,128)(2,1)S(1)}, bf16[64,8192]{1,0:T(8,128)(2,1)S(1)}, bf16[64,8192]{1,0:T(8,128)(2,1)S(1)}) custom-call(bf16[256,256]{1,0:T(8,128)(2,1)S(1)} %get-tuple-element.46.rows_ref, bf16[256,128]{1,0:T(8,128)(2,1)S(1)} %get-tuple-element.47.inner_ref, bf16[256,8192]{1,0:T(8,128)(2,1)S(1)} %copy-done, ...), custom_call_target="tpu_custom_call" | custom-call | flops 1073741824 | bytes 8388608 | tf_op jit(solution)/shard_map/pallas_call | solution.py:321
  83.2 2.4 %collective-permute-start.26 = (bf16[64,8192]{1,0:T(8,128)(2,1)S(1)}, bf16[64,8192]{1,0:T(8,128)(2,1)S(1)}, u32[]{:S(2)}, u32[]{:S(2)}) collective-permute-start(bf16[64,8192]{1,0:T(8,128)(2,1)S(1)} %get-tuple-element.50), channel_id=1, source_target_pairs={{0,16},{1,17},{2,18},{3,19},{4,20},{5,21},{6,22},{7,23},{8,24},{9,... | collective-permute-start | bytes 3145736 | tf_op jit(solution)/shard_map/ppermute | solution.py:45
  85.6 1.8 %collective-permute-start.27 = (bf16[64,8192]{1,0:T(8,128)(2,1)S(1)}, bf16[64,8192]{1,0:T(8,128)(2,1)S(1)}, u32[]{:S(2)}, u32[]{:S(2)}) collective-permute-start(bf16[64,8192]{1,0:T(8,128)(2,1)S(1)} %get-tuple-element.51), channel_id=1, source_target_pairs={{0,8},{1,9},{2,10},{3,11},{4,12},{5,13},{6,14},{7,15},{8,16},{9,17... | collective-permute-start | bytes 3145736 | tf_op jit(solution)/shard_map/ppermute | solution.py:45
  87.4 1.4 %collective-permute-start.28 = (bf16[64,8192]{1,0:T(8,128)(2,1)S(1)}, bf16[64,8192]{1,0:T(8,128)(2,1)S(1)}, u32[]{:S(2)}, u32[]{:S(2)}) collective-permute-start(bf16[64,8192]{1,0:T(8,128)(2,1)S(1)} %get-tuple-element.52), channel_id=1, source_target_pairs={{0,24},{1,25},{2,26},{3,27},{4,28},{5,29},{6,30},{7,31},{8,0},{9,1... | collective-permute-start | bytes 3145736 | tf_op jit(solution)/shard_map/ppermute | solution.py:45
  88.8 10.9 %collective-permute-done.26.refs_1_ = bf16[64,8192]{1,0:T(8,128)(2,1)S(1)} collective-permute-done((bf16[64,8192]{1,0:T(8,128)(2,1)S(1)}, bf16[64,8192]{1,0:T(8,128)(2,1)S(1)}, u32[]{:S(2)}, u32[]{:S(2)}) %collective-permute-start.26) | collective-permute-done | bytes 1048608 | tf_op jit(solution)/shard_map/ppermute | solution.py:45
  99.7 11.1 %collective-permute-done.27.refs_2_ = bf16[64,8192]{1,0:T(8,128)(2,1)S(1)} collective-permute-done((bf16[64,8192]{1,0:T(8,128)(2,1)S(1)}, bf16[64,8192]{1,0:T(8,128)(2,1)S(1)}, u32[]{:S(2)}, u32[]{:S(2)}) %collective-permute-start.27) | collective-permute-done | bytes 1048608 | tf_op jit(solution)/shard_map/ppermute | solution.py:45
  111.4 1.4 %shard_map.157 = (f32[16,8192]{1,0:T(8,128)S(1)}, bf16[16,8192]{1,0:T(8,128)(2,1)S(1)}, bf16[16,8192]{1,0:T(8,128)(2,1)S(1)}, bf16[16,8192]{1,0:T(8,128)(2,1)S(1)}) custom-call(s32[1]{0:T(128)} %bitcast.spot_ref, bf16[64,8192]{1,0:T(8,128)(2,1)S(1)} %get-tuple-element.49.refs_0_, bf16[64,8192]{1,0:T(8,128)(2,1)S(1)} %collective-permute-done.26.refs_1_, ...), custom_call_target="tpu_custom_call" | custom-call | flops 2097152 | bytes 5242880 | tf_op jit(solution)/shard_map/pallas_call | solution.py:295
  113.6 3.1 %collective-permute-start.30 = (bf16[16,8192]{1,0:T(8,128)(2,1)S(1)}, bf16[16,8192]{1,0:T(8,128)(2,1)S(1)}, u32[]{:S(2)}, u32[]{:S(2)}) collective-permute-start(bf16[16,8192]{1,0:T(8,128)(2,1)S(1)} %get-tuple-element.55), channel_id=1, source_target_pairs={{0,2},{1,3},{2,0},{3,1},{4,6},{5,7},{6,4},{7,5},{8,10},{9,11},{10,... | collective-permute-start | bytes 786440 | tf_op jit(solution)/shard_map/ppermute | solution.py:45
  116.7 1.8 %collective-permute-start.31 = (bf16[16,8192]{1,0:T(8,128)(2,1)S(1)}, bf16[16,8192]{1,0:T(8,128)(2,1)S(1)}, u32[]{:S(2)}, u32[]{:S(2)}) collective-permute-start(bf16[16,8192]{1,0:T(8,128)(2,1)S(1)} %get-tuple-element.56), channel_id=1, source_target_pairs={{0,3},{1,0},{2,1},{3,2},{4,7},{5,4},{6,5},{7,6},{8,11},{9,8},{10,9... | collective-permute-start | bytes 786440 | tf_op jit(solution)/shard_map/ppermute | solution.py:45
  118.4 2.0 %collective-permute-done.29 = bf16[16,8192]{1,0:T(8,128)(2,1)S(1)} collective-permute-done((bf16[16,8192]{1,0:T(8,128)(2,1)S(1)}, bf16[16,8192]{1,0:T(8,128)(2,1)S(1)}, u32[]{:S(2)}, u32[]{:S(2)}) %collective-permute-start.29) | collective-permute-done | bytes 262176 | tf_op jit(solution)/shard_map/ppermute | solution.py:45
  120.5 3.3 %collective-permute-done.30 = bf16[16,8192]{1,0:T(8,128)(2,1)S(1)} collective-permute-done((bf16[16,8192]{1,0:T(8,128)(2,1)S(1)}, bf16[16,8192]{1,0:T(8,128)(2,1)S(1)}, u32[]{:S(2)}, u32[]{:S(2)}) %collective-permute-start.30) | collective-permute-done | bytes 262176 | tf_op jit(solution)/shard_map/ppermute | solution.py:45
  124.9 4.5 %collective-permute-done.32 = bf16[8,8192]{1,0:T(8,128)(2,1)S(1)} collective-permute-done((bf16[8,8192]{1,0:T(8,128)(2,1)S(1)}, bf16[8,8192]{1,0:T(8,128)(2,1)S(1)}, u32[]{:S(2)}, u32[]{:S(2)}) %collective-permute-start.32) | collective-permute-done | bytes 131104 | tf_op jit(solution)/shard_map/ppermute | solution.py:45
  (115 shorter events, 29.2 us)
Async XLA Ops:
  2.2 9.5 %collective-permute-start = (bf16[8,8192]{1,0:T(8,128)(2,1)S(1)}, bf16[8,8192]{1,0:T(8,128)(2,1)S(1)}, u32[]{:S(2)}, u32[]{:S(2)}) collective-permute-start(bf16[8,8192]{1,0:T(8,128)(2,1)S(1)} %get-tuple-element.58), channel_id=1, source_target_pairs={{0,4},{1,5},{2,6},{3,7},{4,0},{5,1},{6,2},{7,3},{8,12},{9,13},{10,... | collective-permute-start | bytes 393224 | tf_op jit(solution)/shard_map/ppermute | solution.py:45
  6.7 4.9 %collective-permute-start.6 = (bf16[112,128]{1,0:T(8,128)(2,1)S(1)}, bf16[112,128]{1,0:T(8,128)(2,1)S(1)}, u32[]{:S(2)}, u32[]{:S(2)}) collective-permute-start(bf16[112,128]{1,0:T(8,128)(2,1)S(1)} %concatenate.25), channel_id=1, source_target_pairs={{0,64},{1,65},{2,66},{3,67},{4,68},{5,69},{6,70},{7,71},{8,72},{9,... | collective-permute-start | bytes 86024 | tf_op jit(solution)/shard_map/ppermute | solution.py:45
  11.6 14.2 %collective-permute-start.1 = (bf16[16,8192]{1,0:T(8,128)(2,1)S(1)}, bf16[16,8192]{1,0:T(8,128)(2,1)S(1)}, u32[]{:S(2)}, u32[]{:S(2)}) collective-permute-start(bf16[16,8192]{1,0:T(8,128)(2,1)S(1)} %bitcast.105), channel_id=1, source_target_pairs={{0,1},{1,2},{2,3},{3,0},{4,5},{5,6},{6,7},{7,4},{8,9},{9,10},{10,1... | collective-permute-start | bytes 786440 | tf_op jit(solution)/shard_map/ppermute | solution.py:45
  13.3 12.6 %collective-permute-start.2 = (bf16[16,8192]{1,0:T(8,128)(2,1)S(1)}, bf16[16,8192]{1,0:T(8,128)(2,1)S(1)}, u32[]{:S(2)}, u32[]{:S(2)}) collective-permute-start(bf16[16,8192]{1,0:T(8,128)(2,1)S(1)} %bitcast.106), channel_id=1, source_target_pairs={{0,2},{1,3},{2,0},{3,1},{4,6},{5,7},{6,4},{7,5},{8,10},{9,11},{10,... | collective-permute-start | bytes 786440 | tf_op jit(solution)/shard_map/ppermute | solution.py:45
  16.2 9.7 %collective-permute-start.3 = (bf16[16,8192]{1,0:T(8,128)(2,1)S(1)}, bf16[16,8192]{1,0:T(8,128)(2,1)S(1)}, u32[]{:S(2)}, u32[]{:S(2)}) collective-permute-start(bf16[16,8192]{1,0:T(8,128)(2,1)S(1)} %bitcast.107), channel_id=1, source_target_pairs={{0,3},{1,0},{2,1},{3,2},{4,7},{5,4},{6,5},{7,6},{8,11},{9,8},{10,9... | collective-permute-start | bytes 786440 | tf_op jit(solution)/shard_map/ppermute | solution.py:45
  17.5 8.3 %collective-permute-start.7 = (bf16[2,112,128]{2,1,0:T(8,128)(2,1)S(1)}, bf16[2,112,128]{2,1,0:T(8,128)(2,1)S(1)}, u32[]{:S(2)}, u32[]{:S(2)}) collective-permute-start(bf16[2,112,128]{2,1,0:T(8,128)(2,1)S(1)} %pad_maximum_fusion.3), channel_id=1, source_target_pairs={{0,128},{1,129},{2,130},{3,131},{4,132},{5,133},{6,134},{7,135},{8... | collective-permute-start | bytes 172040 | tf_op jit(solution)/shard_map/ppermute | solution.py:45
  26.0 18.9 %collective-permute-start.4 = (bf16[64,8192]{1,0:T(8,128)(2,1)S(1)}, bf16[64,8192]{1,0:T(8,128)(2,1)S(1)}, u32[]{:S(2)}, u32[]{:S(2)}) collective-permute-start(bf16[64,8192]{1,0:T(8,128)(2,1)S(1)} %bitcast.97), channel_id=1, source_target_pairs={{0,8},{1,9},{2,10},{3,11},{4,12},{5,13},{6,14},{7,15},{8,16},{9,17... | collective-permute-start | bytes 3145736 | tf_op jit(solution)/shard_map/ppermute | solution.py:45
  28.0 17.6 %collective-permute-start.5 = (bf16[64,8192]{1,0:T(8,128)(2,1)S(1)}, bf16[64,8192]{1,0:T(8,128)(2,1)S(1)}, u32[]{:S(2)}, u32[]{:S(2)}) collective-permute-start(bf16[64,8192]{1,0:T(8,128)(2,1)S(1)} %bitcast.98), channel_id=1, source_target_pairs={{0,24},{1,25},{2,26},{3,27},{4,28},{5,29},{6,30},{7,31},{8,0},{9,1... | collective-permute-start | bytes 3145736 | tf_op jit(solution)/shard_map/ppermute | solution.py:45
  29.3 4.3 %collective-permute-start.8 = (bf16[4,64,128]{2,1,0:T(8,128)(2,1)S(1)}, bf16[4,64,128]{2,1,0:T(8,128)(2,1)S(1)}, u32[]{:S(2)}, u32[]{:S(2)}) collective-permute-start(bf16[4,64,128]{2,1,0:T(8,128)(2,1)S(1)} %slice.51), channel_id=1, source_target_pairs={{0,4},{1,5},{2,6},{3,7},{4,0},{5,1},{6,2},{7,3},{8,12},{9,13},{10,... | collective-permute-start | bytes 196616 | tf_op jit(solution)/shard_map/ppermute | solution.py:45
  33.6 7.2 %collective-permute-start.9 = (bf16[2,4,64,128]{3,2,1,0:T(8,128)(2,1)S(1)}, bf16[2,4,64,128]{3,2,1,0:T(8,128)(2,1)S(1)}, u32[]{:S(2)}, u32[]{:S(2)}) collective-permute-start(bf16[2,4,64,128]{3,2,1,0:T(8,128)(2,1)S(1)} %bitcast_dynamic-update-slice_fusion.10), channel_id=1, source_target_pairs={{0,1},{1,2},{2,3},{3,0},{4,5},{5,6},{6,7},{7,4},{8,9},{9,10},{10,1... | collective-permute-start | bytes 393224 | tf_op jit(solution)/shard_map/ppermute | solution.py:45
  34.3 9.0 %collective-permute-start.10 = (bf16[2,4,64,128]{3,2,1,0:T(8,128)(2,1)S(1)}, bf16[2,4,64,128]{3,2,1,0:T(8,128)(2,1)S(1)}, u32[]{:S(2)}, u32[]{:S(2)}) collective-permute-start(bf16[2,4,64,128]{3,2,1,0:T(8,128)(2,1)S(1)} %bitcast_dynamic-update-slice_fusion.10), channel_id=1, source_target_pairs={{0,2},{1,3},{2,0},{3,1},{4,6},{5,7},{6,4},{7,5},{8,10},{9,11},{10,... | collective-permute-start | bytes 393224 | tf_op jit(solution)/shard_map/ppermute | solution.py:45
  36.3 7.1 %collective-permute-start.11 = (bf16[2,4,64,128]{3,2,1,0:T(8,128)(2,1)S(1)}, bf16[2,4,64,128]{3,2,1,0:T(8,128)(2,1)S(1)}, u32[]{:S(2)}, u32[]{:S(2)}) collective-permute-start(bf16[2,4,64,128]{3,2,1,0:T(8,128)(2,1)S(1)} %bitcast_dynamic-update-slice_fusion.10), channel_id=1, source_target_pairs={{0,3},{1,0},{2,1},{3,2},{4,7},{5,4},{6,5},{7,6},{8,11},{9,8},{10,9... | collective-permute-start | bytes 393224 | tf_op jit(solution)/shard_map/ppermute | solution.py:45
  45.6 14.2 %collective-permute-start.14 = (bf16[4,2,4,64,128]{4,3,2,1,0:T(8,128)(2,1)S(1)}, bf16[4,2,4,64,128]{4,3,2,1,0:T(8,128)(2,1)S(1)}, u32[]{:S(2)}, u32[]{:S(2)}) collective-permute-start(bf16[4,2,4,64,128]{4,3,2,1,0:T(8,128)(2,1)S(1)} %bitcast_dynamic-update-slice_fusion.4.refs_0_), channel_id=1, source_target_pairs={{0,8},{1,9},{2,10},{3,11},{4,12},{5,13},{6,14},{7,15},{8,16},{9,17... | collective-permute-start | bytes 1572872 | tf_op jit(solution)/shard_map/ppermute | solution.py:45
  46.6 13.2 %collective-permute-start.15 = (bf16[4,2,4,64,128]{4,3,2,1,0:T(8,128)(2,1)S(1)}, bf16[4,2,4,64,128]{4,3,2,1,0:T(8,128)(2,1)S(1)}, u32[]{:S(2)}, u32[]{:S(2)}) collective-permute-start(bf16[4,2,4,64,128]{4,3,2,1,0:T(8,128)(2,1)S(1)} %bitcast_dynamic-update-slice_fusion.4.refs_0_), channel_id=1, source_target_pairs={{0,24},{1,25},{2,26},{3,27},{4,28},{5,29},{6,30},{7,31},{8,0},{9,1... | collective-permute-start | bytes 1572872 | tf_op jit(solution)/shard_map/ppermute | solution.py:45
  50.5 3.7 %collective-permute-start.24 = (bf16[32,128]{1,0:T(8,128)(2,1)S(1)}, bf16[32,128]{1,0:T(8,128)(2,1)S(1)}, u32[]{:S(2)}, u32[]{:S(2)}) collective-permute-start(bf16[32,128]{1,0:T(8,128)(2,1)S(1)} %bitcast.114), channel_id=1, source_target_pairs={{0,1},{1,0},{2,3},{3,2},{4,5},{5,4},{6,7},{7,6},{8,9},{9,8},{10,11... | collective-permute-start | bytes 24584 | tf_op jit(solution)/shard_map/ppermute | solution.py:45
  54.3 5.4 %collective-permute-start.25 = (bf16[2,32,128]{2,1,0:T(8,128)(2,1)S(1)}, bf16[2,32,128]{2,1,0:T(8,128)(2,1)S(1)}, u32[]{:S(2)}, u32[]{:S(2)}) collective-permute-start(bf16[2,32,128]{2,1,0:T(8,128)(2,1)S(1)} %pad_maximum_fusion.5), channel_id=1, source_target_pairs={{0,2},{1,3},{2,0},{3,1},{4,6},{5,7},{6,4},{7,5},{8,10},{9,11},{10,... | collective-permute-start | bytes 49160 | tf_op jit(solution)/shard_map/ppermute | solution.py:45
  55.9 10.5 %collective-permute-start.12 = (bf16[64,4096]{1,0:T(8,128)(2,1)S(1)}, bf16[64,4096]{1,0:T(8,128)(2,1)S(1)}, u32[]{:S(2)}, u32[]{:S(2)}) collective-permute-start(bf16[64,4096]{1,0:T(8,128)(2,1)S(1)} %slice.52), channel_id=1, source_target_pairs={{0,8},{1,9},{2,10},{3,11},{4,12},{5,13},{6,14},{7,15},{8,16},{9,17... | collective-permute-start | bytes 1572872 | tf_op jit(solution)/shard_map/ppermute | solution.py:45
  56.0 9.9 %collective-permute-start.13 = (bf16[64,4096]{1,0:T(8,128)(2,1)S(1)}, bf16[64,4096]{1,0:T(8,128)(2,1)S(1)}, u32[]{:S(2)}, u32[]{:S(2)}) collective-permute-start(bf16[64,4096]{1,0:T(8,128)(2,1)S(1)} %slice.54), channel_id=1, source_target_pairs={{0,24},{1,25},{2,26},{3,27},{4,28},{5,29},{6,30},{7,31},{8,0},{9,1... | collective-permute-start | bytes 1572872 | tf_op jit(solution)/shard_map/ppermute | solution.py:45
  59.9 9.3 %collective-permute-start.16 = (bf16[2,2,4,64,128]{4,3,2,1,0:T(8,128)(2,1)S(1)}, bf16[2,2,4,64,128]{4,3,2,1,0:T(8,128)(2,1)S(1)}, u32[]{:S(2)}, u32[]{:S(2)}) collective-permute-start(bf16[2,2,4,64,128]{4,3,2,1,0:T(8,128)(2,1)S(1)} %slice.60), channel_id=1, source_target_pairs={{0,8},{1,9},{2,10},{3,11},{4,12},{5,13},{6,14},{7,15},{8,16},{9,17... | collective-permute-start | bytes 786440 | tf_op jit(solution)/shard_map/ppermute | solution.py:45
  60.0 9.2 %collective-permute-start.17 = (bf16[2,2,4,64,128]{4,3,2,1,0:T(8,128)(2,1)S(1)}, bf16[2,2,4,64,128]{4,3,2,1,0:T(8,128)(2,1)S(1)}, u32[]{:S(2)}, u32[]{:S(2)}) collective-permute-start(bf16[2,2,4,64,128]{4,3,2,1,0:T(8,128)(2,1)S(1)} %slice.61), channel_id=1, source_target_pairs={{0,24},{1,25},{2,26},{3,27},{4,28},{5,29},{6,30},{7,31},{8,0},{9,1... | collective-permute-start | bytes 786440 | tf_op jit(solution)/shard_map/ppermute | solution.py:45
  69.2 4.2 %collective-permute-start.18 = (bf16[4,2,4,64,128]{4,3,2,1,0:T(8,128)(2,1)S(1)}, bf16[4,2,4,64,128]{4,3,2,1,0:T(8,128)(2,1)S(1)}, u32[]{:S(2)}, u32[]{:S(2)}) collective-permute-start(bf16[4,2,4,64,128]{4,3,2,1,0:T(8,128)(2,1)S(1)} %bitcast_dynamic-update-slice_fusion.4.refs_0_), channel_id=1, source_target_pairs={{0,32},{1,33},{2,34},{3,35},{4,36},{5,37},{6,38},{7,39},{8,40},{9,... | collective-permute-start | bytes 1572872 | tf_op jit(solution)/shard_map/ppermute | solution.py:45
  69.2 4.2 %collective-permute-start.19 = (bf16[4,2,4,64,128]{4,3,2,1,0:T(8,128)(2,1)S(1)}, bf16[4,2,4,64,128]{4,3,2,1,0:T(8,128)(2,1)S(1)}, u32[]{:S(2)}, u32[]{:S(2)}) collective-permute-start(bf16[4,2,4,64,128]{4,3,2,1,0:T(8,128)(2,1)S(1)} %collective-permute-done.14.refs_1_), channel_id=1, source_target_pairs={{0,32},{1,33},{2,34},{3,35},{4,36},{5,37},{6,38},{7,39},{8,40},{9,... | collective-permute-start | bytes 1572872 | tf_op jit(solution)/shard_map/ppermute | solution.py:45
  69.7 3.7 %collective-permute-start.20 = (bf16[4,2,4,64,128]{4,3,2,1,0:T(8,128)(2,1)S(1)}, bf16[4,2,4,64,128]{4,3,2,1,0:T(8,128)(2,1)S(1)}, u32[]{:S(2)}, u32[]{:S(2)}) collective-permute-start(bf16[4,2,4,64,128]{4,3,2,1,0:T(8,128)(2,1)S(1)} %collective-permute-done.15.refs_2_), channel_id=1, source_target_pairs={{0,32},{1,33},{2,34},{3,35},{4,36},{5,37},{6,38},{7,39},{8,40},{9,... | collective-permute-start | bytes 1572872 | tf_op jit(solution)/shard_map/ppermute | solution.py:45
  70.2 2.8 %collective-permute-start.21 = (bf16[2,2,4,64,128]{4,3,2,1,0:T(8,128)(2,1)S(1)}, bf16[2,2,4,64,128]{4,3,2,1,0:T(8,128)(2,1)S(1)}, u32[]{:S(2)}, u32[]{:S(2)}) collective-permute-start(bf16[2,2,4,64,128]{4,3,2,1,0:T(8,128)(2,1)S(1)} %collective-permute-done.16.refs_3_), channel_id=1, source_target_pairs={{0,32},{1,33},{2,34},{3,35},{4,36},{5,37},{6,38},{7,39},{8,40},{9,... | collective-permute-start | bytes 786440 | tf_op jit(solution)/shard_map/ppermute | solution.py:45
  70.8 2.6 %collective-permute-start.22 = (bf16[2,2,4,64,128]{4,3,2,1,0:T(8,128)(2,1)S(1)}, bf16[2,2,4,64,128]{4,3,2,1,0:T(8,128)(2,1)S(1)}, u32[]{:S(2)}, u32[]{:S(2)}) collective-permute-start(bf16[2,2,4,64,128]{4,3,2,1,0:T(8,128)(2,1)S(1)} %collective-permute-done.17.refs_4_), channel_id=1, source_target_pairs={{0,32},{1,33},{2,34},{3,35},{4,36},{5,37},{6,38},{7,39},{8,40},{9,... | collective-permute-start | bytes 786440 | tf_op jit(solution)/shard_map/ppermute | solution.py:45
  83.2 16.5 %collective-permute-start.26 = (bf16[64,8192]{1,0:T(8,128)(2,1)S(1)}, bf16[64,8192]{1,0:T(8,128)(2,1)S(1)}, u32[]{:S(2)}, u32[]{:S(2)}) collective-permute-start(bf16[64,8192]{1,0:T(8,128)(2,1)S(1)} %get-tuple-element.50), channel_id=1, source_target_pairs={{0,16},{1,17},{2,18},{3,19},{4,20},{5,21},{6,22},{7,23},{8,24},{9,... | collective-permute-start | bytes 3145736 | tf_op jit(solution)/shard_map/ppermute | solution.py:45
  85.6 25.3 %collective-permute-start.27 = (bf16[64,8192]{1,0:T(8,128)(2,1)S(1)}, bf16[64,8192]{1,0:T(8,128)(2,1)S(1)}, u32[]{:S(2)}, u32[]{:S(2)}) collective-permute-start(bf16[64,8192]{1,0:T(8,128)(2,1)S(1)} %get-tuple-element.51), channel_id=1, source_target_pairs={{0,8},{1,9},{2,10},{3,11},{4,12},{5,13},{6,14},{7,15},{8,16},{9,17... | collective-permute-start | bytes 3145736 | tf_op jit(solution)/shard_map/ppermute | solution.py:45
  87.4 24.1 %collective-permute-start.28 = (bf16[64,8192]{1,0:T(8,128)(2,1)S(1)}, bf16[64,8192]{1,0:T(8,128)(2,1)S(1)}, u32[]{:S(2)}, u32[]{:S(2)}) collective-permute-start(bf16[64,8192]{1,0:T(8,128)(2,1)S(1)} %get-tuple-element.52), channel_id=1, source_target_pairs={{0,24},{1,25},{2,26},{3,27},{4,28},{5,29},{6,30},{7,31},{8,0},{9,1... | collective-permute-start | bytes 3145736 | tf_op jit(solution)/shard_map/ppermute | solution.py:45
  112.8 7.7 %collective-permute-start.29 = (bf16[16,8192]{1,0:T(8,128)(2,1)S(1)}, bf16[16,8192]{1,0:T(8,128)(2,1)S(1)}, u32[]{:S(2)}, u32[]{:S(2)}) collective-permute-start(bf16[16,8192]{1,0:T(8,128)(2,1)S(1)} %get-tuple-element.54), channel_id=1, source_target_pairs={{0,1},{1,2},{2,3},{3,0},{4,5},{5,6},{6,7},{7,4},{8,9},{9,10},{10,1... | collective-permute-start | bytes 786440 | tf_op jit(solution)/shard_map/ppermute | solution.py:45
  113.6 10.3 %collective-permute-start.30 = (bf16[16,8192]{1,0:T(8,128)(2,1)S(1)}, bf16[16,8192]{1,0:T(8,128)(2,1)S(1)}, u32[]{:S(2)}, u32[]{:S(2)}) collective-permute-start(bf16[16,8192]{1,0:T(8,128)(2,1)S(1)} %get-tuple-element.55), channel_id=1, source_target_pairs={{0,2},{1,3},{2,0},{3,1},{4,6},{5,7},{6,4},{7,5},{8,10},{9,11},{10,... | collective-permute-start | bytes 786440 | tf_op jit(solution)/shard_map/ppermute | solution.py:45
  116.7 7.5 %collective-permute-start.31 = (bf16[16,8192]{1,0:T(8,128)(2,1)S(1)}, bf16[16,8192]{1,0:T(8,128)(2,1)S(1)}, u32[]{:S(2)}, u32[]{:S(2)}) collective-permute-start(bf16[16,8192]{1,0:T(8,128)(2,1)S(1)} %get-tuple-element.56), channel_id=1, source_target_pairs={{0,3},{1,0},{2,1},{3,2},{4,7},{5,4},{6,5},{7,6},{8,11},{9,8},{10,9... | collective-permute-start | bytes 786440 | tf_op jit(solution)/shard_map/ppermute | solution.py:45
  124.3 5.1 %collective-permute-start.32 = (bf16[8,8192]{1,0:T(8,128)(2,1)S(1)}, bf16[8,8192]{1,0:T(8,128)(2,1)S(1)}, u32[]{:S(2)}, u32[]{:S(2)}) collective-permute-start(bf16[8,8192]{1,0:T(8,128)(2,1)S(1)} %fusion.26), channel_id=1, source_target_pairs={{0,4},{1,5},{2,6},{3,7},{4,0},{5,1},{6,2},{7,3},{8,12},{9,13},{10,... | collective-permute-start | bytes 393224 | tf_op jit(solution)/shard_map/ppermute | solution.py:45
  (7 other events, 95.9 us)

commit v3 on v2

--- a/solution.py
+++ b/solution.py
@@ -283,23 +283,24 @@
 
 def sum_kernel(spot_ref, *refs):
     total = refs[8]
-    total[...] = sum(ref[...].astype(jnp.float32) for ref in refs[:4])
-    for s, ref in enumerate(refs[4:8]):
-        at = pl.ds(pl.multiple_of(16 * lax.rem(spot_ref[0] + s, 4), 16), 16)
-        ref[...] = total[at, :].astype(ref.dtype)
+    tile = total.shape[1]
+    for j in range(refs[0].shape[1] // tile):
+        along = slice(tile * j, tile * j + tile)
+        total[...] = sum(ref[:, along].astype(jnp.float32) for ref in refs[:4])
+        for s, ref in enumerate(refs[4:8]):
+            at = pl.ds(pl.multiple_of(16 * lax.rem(spot_ref[0] + s, 4), 16), 16)
+            ref[:, along] = total[at, :].astype(ref.dtype)
 
 
 def sum_rows(spot, blocks):
-    tile = 2048
     width = blocks[0].shape[1]
     return pl.pallas_call(
         sum_kernel,
-        grid=(width // tile,),
-        in_specs=[spec_smem()] + [pl.BlockSpec((64, tile), lambda j: (0, j))] * 4,
-        out_specs=[pl.BlockSpec((16, tile), lambda j: (0, j))] * 4,
+        in_specs=[spec_smem()] + [pl.BlockSpec(memory_space=pltpu.VMEM)] * 4,
+        out_specs=[pl.BlockSpec(memory_space=pltpu.VMEM)] * 4,
         out_shape=[jax.ShapeDtypeStruct((16, width), jnp.float32)]
         + [jax.ShapeDtypeStruct((16, width), jnp.bfloat16)] * 3,
-        scratch_shapes=[pltpu.VMEM((64, tile), jnp.float32)],
+        scratch_shapes=[pltpu.VMEM((64, 2048), jnp.float32)],
         compiler_params=pltpu.CompilerParams(vmem_limit_bytes=14 * 2**20),
         cost_estimate=pl.CostEstimate(
             flops=4 * 64 * 8192, bytes_accessed=5 * 2**20, transcendentals=0
@@ -308,28 +309,23 @@
 
 
 def out_kernel(rows_ref, inner_ref, weight_ref, up_ref, *out_refs):
-    part = jnp.dot(rows_ref[...], weight_ref[...], preferred_element_type=jnp.float32)
-    part = part + adapter_scale * outer(inner_ref[:, :64], up_ref[:, 64:])
-    part = part.astype(jnp.bfloat16)
-    for s in range(4):
-        out_refs[s][...] = part[64 * s : 64 * s + 64]
+    tile = 2048
+    for j in range(weight_ref.shape[1] // tile):
+        at = slice(tile * j, tile * j + tile)
+        part = jnp.dot(rows_ref[...], weight_ref[:, at], preferred_element_type=jnp.float32)
+        part = part + adapter_scale * outer(inner_ref[:, :64], up_ref[at, 64:])
+        part = part.astype(jnp.bfloat16)
+        for s in range(4):
+            out_refs[s][:, at] = part[64 * s : 64 * s + 64]
 
 
 def out_pieces(rows, inner, weight, up_factor):
-    tile = 2048
-    depth, width = weight.shape
     return pl.pallas_call(
         out_kernel,
-        grid=(width // tile,),
-        in_specs=[
-            pl.BlockSpec(rows.shape, lambda j: (0, 0)),
-            pl.BlockSpec(inner.shape, lambda j: (0, 0)),
-            pl.BlockSpec((depth, tile), lambda j: (0, j)),
-            pl.BlockSpec((tile, 128), lambda j: (j, 0)),
-        ],
-        out_specs=[pl.BlockSpec((64, tile), lambda j: (0, j))] * 4,
-        out_shape=[jax.ShapeDtypeStruct((64, width), jnp.bfloat16)] * 4,
-        compiler_params=pltpu.CompilerParams(vmem_limit_bytes=12 * 2**20),
+        in_specs=[pl.BlockSpec(memory_space=pltpu.VMEM)] * 4,
+        out_specs=[pl.BlockSpec(memory_space=pltpu.VMEM)] * 4,
+        out_shape=[jax.ShapeDtypeStruct((64, weight.shape[1]), jnp.bfloat16)] * 4,
+        compiler_params=pltpu.CompilerParams(vmem_limit_bytes=20 * 2**20),
         cost_estimate=pl.CostEstimate(
             flops=2 * 256 * 256 * 8192, bytes_accessed=8 * 2**20, transcendentals=0
         ),

time: 131 us -> 129 us (0.985)
  Pallas kernels: 11.2 us -> 9.38 us
    pallas_call x2, Pallas kernels: 5.14 us -> 3.35 us  [the longest x1 2.41 us: out_pieces(): pl.pallas_call(out_kernel, in_specs=[pl.BlockSpec(memory_space=pltpu.VMEM...]
where the time goes in v3:
time: 129 us; the launch traced here: 128 us
  waiting for transfers between devices  58.7 us (46%)
  starting transfers between devices  44.8 us (35%)
  Pallas kernels  9.38 us (7%)
  other arithmetic  6.91 us (5%)
  matrix products  6.72 us (5%)
    ppermute x33, waiting for transfers between devices, permute(): return lax.ppermute(block, AXES, source_to_target)  58.7 us
    ppermute x33, starting transfers between devices, permute(): return lax.ppermute(block, AXES, source_to_target)  44.8 us
    dot_general x10, matrix products, dot32(): return jnp.dot(left, right, preferred_element_type=jnp.float32)  6.72 us
    pallas_call x1, Pallas kernels, inner_rows(): pl.pallas_call(inner_kernel, in_specs=[spec_smem()] + [pl.BlockSpec(memor...  3.2 us
    pallas_call x1, Pallas kernels, attend_rows(): pl.pallas_call(attend_kernel, in_specs=[spec_smem(), spec_smem()] + [pl.B...  2.83 us
  transfers between devices with their start and end apart: 33, of which 20 were waited for; matrix products, arithmetic and copies ran while one was open for 9% of the time, Pallas kernels for 0%

profile of v3, /device:TPU:64, one launch (start us, length us, event | category | flops | bytes accessed | tf_op | source)
XLA Modules:
  0.0 128.3 jit_solution(8448500872077680033)
XLA Ops:
  2.2 2.0 %collective-permute-start = (bf16[8,8192]{1,0:T(8,128)(2,1)S(1)}, bf16[8,8192]{1,0:T(8,128)(2,1)S(1)}, u32[]{:S(2)}, u32[]{:S(2)}) collective-permute-start(bf16[8,8192]{1,0:T(8,128)(2,1)S(1)} %get-tuple-element.58), channel_id=1, source_target_pairs={{0,4},{1,5},{2,6},{3,7},{4,0},{5,1},{6,2},{7,3},{8,12},{9,13},{10,... | collective-permute-start | bytes 393224 | tf_op jit(solution)/shard_map/ppermute | solution.py:45
  8.6 3.0 %collective-permute-done.6 = bf16[112,128]{1,0:T(8,128)(2,1)S(1)} collective-permute-done((bf16[112,128]{1,0:T(8,128)(2,1)S(1)}, bf16[112,128]{1,0:T(8,128)(2,1)S(1)}, u32[]{:S(2)}, u32[]{:S(2)}) %collective-permute-start.6) | collective-permute-done | bytes 28704 | tf_op jit(solution)/shard_map/ppermute | solution.py:45
  11.6 1.7 %collective-permute-start.1 = (bf16[16,8192]{1,0:T(8,128)(2,1)S(1)}, bf16[16,8192]{1,0:T(8,128)(2,1)S(1)}, u32[]{:S(2)}, u32[]{:S(2)}) collective-permute-start(bf16[16,8192]{1,0:T(8,128)(2,1)S(1)} %bitcast.105), channel_id=1, source_target_pairs={{0,1},{1,2},{2,3},{3,0},{4,5},{5,6},{6,7},{7,4},{8,9},{9,10},{10,1... | collective-permute-start | bytes 786440 | tf_op jit(solution)/shard_map/ppermute | solution.py:45
  13.3 2.9 %collective-permute-start.2 = (bf16[16,8192]{1,0:T(8,128)(2,1)S(1)}, bf16[16,8192]{1,0:T(8,128)(2,1)S(1)}, u32[]{:S(2)}, u32[]{:S(2)}) collective-permute-start(bf16[16,8192]{1,0:T(8,128)(2,1)S(1)} %bitcast.106), channel_id=1, source_target_pairs={{0,2},{1,3},{2,0},{3,1},{4,6},{5,7},{6,4},{7,5},{8,10},{9,11},{10,... | collective-permute-start | bytes 786440 | tf_op jit(solution)/shard_map/ppermute | solution.py:45
  17.5 4.5 %collective-permute-start.7 = (bf16[2,112,128]{2,1,0:T(8,128)(2,1)S(1)}, bf16[2,112,128]{2,1,0:T(8,128)(2,1)S(1)}, u32[]{:S(2)}, u32[]{:S(2)}) collective-permute-start(bf16[2,112,128]{2,1,0:T(8,128)(2,1)S(1)} %pad_maximum_fusion.3), channel_id=1, source_target_pairs={{0,128},{1,129},{2,130},{3,131},{4,132},{5,133},{6,134},{7,135},{8... | collective-permute-start | bytes 172040 | tf_op jit(solution)/shard_map/ppermute | solution.py:45
  22.2 3.6 %collective-permute-done.7 = bf16[2,112,128]{2,1,0:T(8,128)(2,1)S(1)} collective-permute-done((bf16[2,112,128]{2,1,0:T(8,128)(2,1)S(1)}, bf16[2,112,128]{2,1,0:T(8,128)(2,1)S(1)}, u32[]{:S(2)}, u32[]{:S(2)}) %collective-permute-start.7) | collective-permute-done | bytes 57376 | tf_op jit(solution)/shard_map/ppermute | solution.py:45
  26.0 2.0 %collective-permute-start.4 = (bf16[64,8192]{1,0:T(8,128)(2,1)S(1)}, bf16[64,8192]{1,0:T(8,128)(2,1)S(1)}, u32[]{:S(2)}, u32[]{:S(2)}) collective-permute-start(bf16[64,8192]{1,0:T(8,128)(2,1)S(1)} %bitcast.97), channel_id=1, source_target_pairs={{0,8},{1,9},{2,10},{3,11},{4,12},{5,13},{6,14},{7,15},{8,16},{9,17... | collective-permute-start | bytes 3145736 | tf_op jit(solution)/shard_map/ppermute | solution.py:45
  31.8 1.8 %collective-permute-done.8 = bf16[4,64,128]{2,1,0:T(8,128)(2,1)S(1)} collective-permute-done((bf16[4,64,128]{2,1,0:T(8,128)(2,1)S(1)}, bf16[4,64,128]{2,1,0:T(8,128)(2,1)S(1)}, u32[]{:S(2)}, u32[]{:S(2)}) %collective-permute-start.8) | collective-permute-done | bytes 65568 | tf_op jit(solution)/shard_map/ppermute | solution.py:45
  34.3 1.9 %collective-permute-start.10 = (bf16[2,4,64,128]{3,2,1,0:T(8,128)(2,1)S(1)}, bf16[2,4,64,128]{3,2,1,0:T(8,128)(2,1)S(1)}, u32[]{:S(2)}, u32[]{:S(2)}) collective-permute-start(bf16[2,4,64,128]{3,2,1,0:T(8,128)(2,1)S(1)} %bitcast_dynamic-update-slice_fusion.10), channel_id=1, source_target_pairs={{0,2},{1,3},{2,0},{3,1},{4,6},{5,7},{6,4},{7,5},{8,10},{9,11},{10,... | collective-permute-start | bytes 393224 | tf_op jit(solution)/shard_map/ppermute | solution.py:45
  37.7 3.1 %collective-permute-done.9 = bf16[2,4,64,128]{3,2,1,0:T(8,128)(2,1)S(1)} collective-permute-done((bf16[2,4,64,128]{3,2,1,0:T(8,128)(2,1)S(1)}, bf16[2,4,64,128]{3,2,1,0:T(8,128)(2,1)S(1)}, u32[]{:S(2)}, u32[]{:S(2)}) %collective-permute-start.9) | collective-permute-done | bytes 131104 | tf_op jit(solution)/shard_map/ppermute | solution.py:45
  40.8 2.5 %collective-permute-done.10 = bf16[2,4,64,128]{3,2,1,0:T(8,128)(2,1)S(1)} collective-permute-done((bf16[2,4,64,128]{3,2,1,0:T(8,128)(2,1)S(1)}, bf16[2,4,64,128]{3,2,1,0:T(8,128)(2,1)S(1)}, u32[]{:S(2)}, u32[]{:S(2)}) %collective-permute-start.10) | collective-permute-done | bytes 131104 | tf_op jit(solution)/shard_map/ppermute | solution.py:45
  43.4 1.5 %collective-permute-done.4.one_ref = bf16[64,8192]{1,0:T(8,128)(2,1)S(1)} collective-permute-done((bf16[64,8192]{1,0:T(8,128)(2,1)S(1)}, bf16[64,8192]{1,0:T(8,128)(2,1)S(1)}, u32[]{:S(2)}, u32[]{:S(2)}) %collective-permute-start.4) | collective-permute-done | bytes 1048608 | tf_op jit(solution)/shard_map/ppermute | solution.py:45
  46.6 2.2 %collective-permute-start.15 = (bf16[4,2,4,64,128]{4,3,2,1,0:T(8,128)(2,1)S(1)}, bf16[4,2,4,64,128]{4,3,2,1,0:T(8,128)(2,1)S(1)}, u32[]{:S(2)}, u32[]{:S(2)}) collective-permute-start(bf16[4,2,4,64,128]{4,3,2,1,0:T(8,128)(2,1)S(1)} %bitcast_dynamic-update-slice_fusion.4.refs_0_), channel_id=1, source_target_pairs={{0,24},{1,25},{2,26},{3,27},{4,28},{5,29},{6,30},{7,31},{8,0},{9,1... | collective-permute-start | bytes 1572872 | tf_op jit(solution)/shard_map/ppermute | solution.py:45
  51.7 2.6 %collective-permute-done.24 = bf16[32,128]{1,0:T(8,128)(2,1)S(1)} collective-permute-done((bf16[32,128]{1,0:T(8,128)(2,1)S(1)}, bf16[32,128]{1,0:T(8,128)(2,1)S(1)}, u32[]{:S(2)}, u32[]{:S(2)}) %collective-permute-start.24) | collective-permute-done | bytes 8224 | tf_op jit(solution)/shard_map/ppermute | solution.py:45
  56.0 3.2 %collective-permute-start.13 = (bf16[64,4096]{1,0:T(8,128)(2,1)S(1)}, bf16[64,4096]{1,0:T(8,128)(2,1)S(1)}, u32[]{:S(2)}, u32[]{:S(2)}) collective-permute-start(bf16[64,4096]{1,0:T(8,128)(2,1)S(1)} %slice.54), channel_id=1, source_target_pairs={{0,24},{1,25},{2,26},{3,27},{4,28},{5,29},{6,30},{7,31},{8,0},{9,1... | collective-permute-start | bytes 1572872 | tf_op jit(solution)/shard_map/ppermute | solution.py:45
  60.0 3.3 %collective-permute-start.17 = (bf16[2,2,4,64,128]{4,3,2,1,0:T(8,128)(2,1)S(1)}, bf16[2,2,4,64,128]{4,3,2,1,0:T(8,128)(2,1)S(1)}, u32[]{:S(2)}, u32[]{:S(2)}) collective-permute-start(bf16[2,2,4,64,128]{4,3,2,1,0:T(8,128)(2,1)S(1)} %slice.61), channel_id=1, source_target_pairs={{0,24},{1,25},{2,26},{3,27},{4,28},{5,29},{6,30},{7,31},{8,0},{9,1... | collective-permute-start | bytes 786440 | tf_op jit(solution)/shard_map/ppermute | solution.py:45
  63.3 2.6 %collective-permute-done.13.right_ref = bf16[64,4096]{1,0:T(8,128)(2,1)S(1)} collective-permute-done((bf16[64,4096]{1,0:T(8,128)(2,1)S(1)}, bf16[64,4096]{1,0:T(8,128)(2,1)S(1)}, u32[]{:S(2)}, u32[]{:S(2)}) %collective-permute-start.13) | collective-permute-done | bytes 524320 | tf_op jit(solution)/shard_map/ppermute | solution.py:45
  66.8 2.3 %collective-permute-done.16.refs_3_ = bf16[2,2,4,64,128]{4,3,2,1,0:T(8,128)(2,1)S(1)} collective-permute-done((bf16[2,2,4,64,128]{4,3,2,1,0:T(8,128)(2,1)S(1)}, bf16[2,2,4,64,128]{4,3,2,1,0:T(8,128)(2,1)S(1)}, u32[]{:S(2)}, u32[]{:S(2)}) %collective-permute-start.16) | collective-permute-done | bytes 262176 | tf_op jit(solution)/shard_map/ppermute | solution.py:45
  71.6 1.4 %collective-permute-done.21.refs_8_ = bf16[2,2,4,64,128]{4,3,2,1,0:T(8,128)(2,1)S(1)} collective-permute-done((bf16[2,2,4,64,128]{4,3,2,1,0:T(8,128)(2,1)S(1)}, bf16[2,2,4,64,128]{4,3,2,1,0:T(8,128)(2,1)S(1)}, u32[]{:S(2)}, u32[]{:S(2)}) %collective-permute-start.21) | collective-permute-done | bytes 262176 | tf_op jit(solution)/shard_map/ppermute | solution.py:45
  73.3 3.2 %shard_map.154 = (f32[256,256]{1,0:T(8,128)S(1)}, bf16[8192,128]{1,0:T(8,128)(2,1)S(1)}) custom-call(s32[3]{0:T(128)S(1)} %pad_add_fusion.spot_ref, bf16[64,8192]{1,0:T(8,128)(2,1)S(1)} %bitcast.101, bf16[64,8192]{1,0:T(8,128)(2,1)S(1)} %collective-permute-done.4.one_ref, bf16[64,4096]{1,0:T(8,128)(2,1)S(1)} %collective-permute-done.12.left_ref, ...), custom_call_target="tpu_custom_call" | custom-call | flops 1073741824 | bytes 10485760 | tf_op jit(solution)/shard_map/pallas_call | solution.py:162
  76.6 2.8 %shard_map.155 = (bf16[256,256]{1,0:T(8,128)(2,1)S(1)}, bf16[256,128]{1,0:T(8,128)(2,1)S(1)}) custom-call(s32[3]{0:T(128)S(1)} %pad_add_fusion.spot_ref, s32[4]{0:T(128)S(1)} %copy-done.2, f32[64,256]{1,0:T(8,128)S(1)} %fusion.30.refs_0_, f32[64,256]{1,0:T(8,128)S(1)} %fusion.31.refs_1_, f32[64,256]{1,0:T(8,128)S(1)} %fusion.16.refs_2_, ...), custom_call_target="tpu_custom_call" | custom-call | flops 83886080 | bytes 4194304 | tf_op jit(solution)/shard_map/pallas_call | solution.py:264
  79.4 2.4 %shard_map.156 = (bf16[64,8192]{1,0:T(8,128)(2,1)S(1)}, bf16[64,8192]{1,0:T(8,128)(2,1)S(1)}, bf16[64,8192]{1,0:T(8,128)(2,1)S(1)}, bf16[64,8192]{1,0:T(8,128)(2,1)S(1)}) custom-call(bf16[256,256]{1,0:T(8,128)(2,1)S(1)} %get-tuple-element.46.rows_ref, bf16[256,128]{1,0:T(8,128)(2,1)S(1)} %get-tuple-element.47.inner_ref, bf16[256,8192]{1,0:T(8,128)(2,1)S(1)} %copy-done, ...), custom_call_target="tpu_custom_call" | custom-call | flops 1073741824 | bytes 8388608 | tf_op jit(solution)/shard_map/pallas_call | solution.py:323
  81.9 2.4 %collective-permute-start.26 = (bf16[64,8192]{1,0:T(8,128)(2,1)S(1)}, bf16[64,8192]{1,0:T(8,128)(2,1)S(1)}, u32[]{:S(2)}, u32[]{:S(2)}) collective-permute-start(bf16[64,8192]{1,0:T(8,128)(2,1)S(1)} %get-tuple-element.50), channel_id=1, source_target_pairs={{0,16},{1,17},{2,18},{3,19},{4,20},{5,21},{6,22},{7,23},{8,24},{9,... | collective-permute-start | bytes 3145736 | tf_op jit(solution)/shard_map/ppermute | solution.py:45
  84.2 1.8 %collective-permute-start.27 = (bf16[64,8192]{1,0:T(8,128)(2,1)S(1)}, bf16[64,8192]{1,0:T(8,128)(2,1)S(1)}, u32[]{:S(2)}, u32[]{:S(2)}) collective-permute-start(bf16[64,8192]{1,0:T(8,128)(2,1)S(1)} %get-tuple-element.51), channel_id=1, source_target_pairs={{0,8},{1,9},{2,10},{3,11},{4,12},{5,13},{6,14},{7,15},{8,16},{9,17... | collective-permute-start | bytes 3145736 | tf_op jit(solution)/shard_map/ppermute | solution.py:45
  86.0 1.4 %collective-permute-start.28 = (bf16[64,8192]{1,0:T(8,128)(2,1)S(1)}, bf16[64,8192]{1,0:T(8,128)(2,1)S(1)}, u32[]{:S(2)}, u32[]{:S(2)}) collective-permute-start(bf16[64,8192]{1,0:T(8,128)(2,1)S(1)} %get-tuple-element.52), channel_id=1, source_target_pairs={{0,24},{1,25},{2,26},{3,27},{4,28},{5,29},{6,30},{7,31},{8,0},{9,1... | collective-permute-start | bytes 3145736 | tf_op jit(solution)/shard_map/ppermute | solution.py:45
  87.4 10.9 %collective-permute-done.26.refs_1_ = bf16[64,8192]{1,0:T(8,128)(2,1)S(1)} collective-permute-done((bf16[64,8192]{1,0:T(8,128)(2,1)S(1)}, bf16[64,8192]{1,0:T(8,128)(2,1)S(1)}, u32[]{:S(2)}, u32[]{:S(2)}) %collective-permute-start.26) | collective-permute-done | bytes 1048608 | tf_op jit(solution)/shard_map/ppermute | solution.py:45
  98.3 11.1 %collective-permute-done.27.refs_2_ = bf16[64,8192]{1,0:T(8,128)(2,1)S(1)} collective-permute-done((bf16[64,8192]{1,0:T(8,128)(2,1)S(1)}, bf16[64,8192]{1,0:T(8,128)(2,1)S(1)}, u32[]{:S(2)}, u32[]{:S(2)}) %collective-permute-start.27) | collective-permute-done | bytes 1048608 | tf_op jit(solution)/shard_map/ppermute | solution.py:45
  111.8 3.1 %collective-permute-start.30 = (bf16[16,8192]{1,0:T(8,128)(2,1)S(1)}, bf16[16,8192]{1,0:T(8,128)(2,1)S(1)}, u32[]{:S(2)}, u32[]{:S(2)}) collective-permute-start(bf16[16,8192]{1,0:T(8,128)(2,1)S(1)} %get-tuple-element.55), channel_id=1, source_target_pairs={{0,2},{1,3},{2,0},{3,1},{4,6},{5,7},{6,4},{7,5},{8,10},{9,11},{10,... | collective-permute-start | bytes 786440 | tf_op jit(solution)/shard_map/ppermute | solution.py:45
  114.9 1.8 %collective-permute-start.31 = (bf16[16,8192]{1,0:T(8,128)(2,1)S(1)}, bf16[16,8192]{1,0:T(8,128)(2,1)S(1)}, u32[]{:S(2)}, u32[]{:S(2)}) collective-permute-start(bf16[16,8192]{1,0:T(8,128)(2,1)S(1)} %get-tuple-element.56), channel_id=1, source_target_pairs={{0,3},{1,0},{2,1},{3,2},{4,7},{5,4},{6,5},{7,6},{8,11},{9,8},{10,9... | collective-permute-start | bytes 786440 | tf_op jit(solution)/shard_map/ppermute | solution.py:45
  116.7 2.0 %collective-permute-done.29 = bf16[16,8192]{1,0:T(8,128)(2,1)S(1)} collective-permute-done((bf16[16,8192]{1,0:T(8,128)(2,1)S(1)}, bf16[16,8192]{1,0:T(8,128)(2,1)S(1)}, u32[]{:S(2)}, u32[]{:S(2)}) %collective-permute-start.29) | collective-permute-done | bytes 262176 | tf_op jit(solution)/shard_map/ppermute | solution.py:45
  118.7 3.4 %collective-permute-done.30 = bf16[16,8192]{1,0:T(8,128)(2,1)S(1)} collective-permute-done((bf16[16,8192]{1,0:T(8,128)(2,1)S(1)}, bf16[16,8192]{1,0:T(8,128)(2,1)S(1)}, u32[]{:S(2)}, u32[]{:S(2)}) %collective-permute-start.30) | collective-permute-done | bytes 262176 | tf_op jit(solution)/shard_map/ppermute | solution.py:45
  123.1 4.5 %collective-permute-done.32 = bf16[8,8192]{1,0:T(8,128)(2,1)S(1)} collective-permute-done((bf16[8,8192]{1,0:T(8,128)(2,1)S(1)}, bf16[8,8192]{1,0:T(8,128)(2,1)S(1)}, u32[]{:S(2)}, u32[]{:S(2)}) %collective-permute-start.32) | collective-permute-done | bytes 131104 | tf_op jit(solution)/shard_map/ppermute | solution.py:45
  (115 shorter events, 28.8 us)
Async XLA Ops:
  2.2 9.5 %collective-permute-start = (bf16[8,8192]{1,0:T(8,128)(2,1)S(1)}, bf16[8,8192]{1,0:T(8,128)(2,1)S(1)}, u32[]{:S(2)}, u32[]{:S(2)}) collective-permute-start(bf16[8,8192]{1,0:T(8,128)(2,1)S(1)} %get-tuple-element.58), channel_id=1, source_target_pairs={{0,4},{1,5},{2,6},{3,7},{4,0},{5,1},{6,2},{7,3},{8,12},{9,13},{10,... | collective-permute-start | bytes 393224 | tf_op jit(solution)/shard_map/ppermute | solution.py:45
  6.7 4.9 %collective-permute-start.6 = (bf16[112,128]{1,0:T(8,128)(2,1)S(1)}, bf16[112,128]{1,0:T(8,128)(2,1)S(1)}, u32[]{:S(2)}, u32[]{:S(2)}) collective-permute-start(bf16[112,128]{1,0:T(8,128)(2,1)S(1)} %concatenate.25), channel_id=1, source_target_pairs={{0,64},{1,65},{2,66},{3,67},{4,68},{5,69},{6,70},{7,71},{8,72},{9,... | collective-permute-start | bytes 86024 | tf_op jit(solution)/shard_map/ppermute | solution.py:45
  11.6 14.2 %collective-permute-start.1 = (bf16[16,8192]{1,0:T(8,128)(2,1)S(1)}, bf16[16,8192]{1,0:T(8,128)(2,1)S(1)}, u32[]{:S(2)}, u32[]{:S(2)}) collective-permute-start(bf16[16,8192]{1,0:T(8,128)(2,1)S(1)} %bitcast.105), channel_id=1, source_target_pairs={{0,1},{1,2},{2,3},{3,0},{4,5},{5,6},{6,7},{7,4},{8,9},{9,10},{10,1... | collective-permute-start | bytes 786440 | tf_op jit(solution)/shard_map/ppermute | solution.py:45
  13.3 12.6 %collective-permute-start.2 = (bf16[16,8192]{1,0:T(8,128)(2,1)S(1)}, bf16[16,8192]{1,0:T(8,128)(2,1)S(1)}, u32[]{:S(2)}, u32[]{:S(2)}) collective-permute-start(bf16[16,8192]{1,0:T(8,128)(2,1)S(1)} %bitcast.106), channel_id=1, source_target_pairs={{0,2},{1,3},{2,0},{3,1},{4,6},{5,7},{6,4},{7,5},{8,10},{9,11},{10,... | collective-permute-start | bytes 786440 | tf_op jit(solution)/shard_map/ppermute | solution.py:45
  16.2 9.7 %collective-permute-start.3 = (bf16[16,8192]{1,0:T(8,128)(2,1)S(1)}, bf16[16,8192]{1,0:T(8,128)(2,1)S(1)}, u32[]{:S(2)}, u32[]{:S(2)}) collective-permute-start(bf16[16,8192]{1,0:T(8,128)(2,1)S(1)} %bitcast.107), channel_id=1, source_target_pairs={{0,3},{1,0},{2,1},{3,2},{4,7},{5,4},{6,5},{7,6},{8,11},{9,8},{10,9... | collective-permute-start | bytes 786440 | tf_op jit(solution)/shard_map/ppermute | solution.py:45
  17.5 8.3 %collective-permute-start.7 = (bf16[2,112,128]{2,1,0:T(8,128)(2,1)S(1)}, bf16[2,112,128]{2,1,0:T(8,128)(2,1)S(1)}, u32[]{:S(2)}, u32[]{:S(2)}) collective-permute-start(bf16[2,112,128]{2,1,0:T(8,128)(2,1)S(1)} %pad_maximum_fusion.3), channel_id=1, source_target_pairs={{0,128},{1,129},{2,130},{3,131},{4,132},{5,133},{6,134},{7,135},{8... | collective-permute-start | bytes 172040 | tf_op jit(solution)/shard_map/ppermute | solution.py:45
  26.0 18.9 %collective-permute-start.4 = (bf16[64,8192]{1,0:T(8,128)(2,1)S(1)}, bf16[64,8192]{1,0:T(8,128)(2,1)S(1)}, u32[]{:S(2)}, u32[]{:S(2)}) collective-permute-start(bf16[64,8192]{1,0:T(8,128)(2,1)S(1)} %bitcast.97), channel_id=1, source_target_pairs={{0,8},{1,9},{2,10},{3,11},{4,12},{5,13},{6,14},{7,15},{8,16},{9,17... | collective-permute-start | bytes 3145736 | tf_op jit(solution)/shard_map/ppermute | solution.py:45
  28.0 17.6 %collective-permute-start.5 = (bf16[64,8192]{1,0:T(8,128)(2,1)S(1)}, bf16[64,8192]{1,0:T(8,128)(2,1)S(1)}, u32[]{:S(2)}, u32[]{:S(2)}) collective-permute-start(bf16[64,8192]{1,0:T(8,128)(2,1)S(1)} %bitcast.98), channel_id=1, source_target_pairs={{0,24},{1,25},{2,26},{3,27},{4,28},{5,29},{6,30},{7,31},{8,0},{9,1... | collective-permute-start | bytes 3145736 | tf_op jit(solution)/shard_map/ppermute | solution.py:45
  29.3 4.3 %collective-permute-start.8 = (bf16[4,64,128]{2,1,0:T(8,128)(2,1)S(1)}, bf16[4,64,128]{2,1,0:T(8,128)(2,1)S(1)}, u32[]{:S(2)}, u32[]{:S(2)}) collective-permute-start(bf16[4,64,128]{2,1,0:T(8,128)(2,1)S(1)} %slice.51), channel_id=1, source_target_pairs={{0,4},{1,5},{2,6},{3,7},{4,0},{5,1},{6,2},{7,3},{8,12},{9,13},{10,... | collective-permute-start | bytes 196616 | tf_op jit(solution)/shard_map/ppermute | solution.py:45
  33.6 7.2 %collective-permute-start.9 = (bf16[2,4,64,128]{3,2,1,0:T(8,128)(2,1)S(1)}, bf16[2,4,64,128]{3,2,1,0:T(8,128)(2,1)S(1)}, u32[]{:S(2)}, u32[]{:S(2)}) collective-permute-start(bf16[2,4,64,128]{3,2,1,0:T(8,128)(2,1)S(1)} %bitcast_dynamic-update-slice_fusion.10), channel_id=1, source_target_pairs={{0,1},{1,2},{2,3},{3,0},{4,5},{5,6},{6,7},{7,4},{8,9},{9,10},{10,1... | collective-permute-start | bytes 393224 | tf_op jit(solution)/shard_map/ppermute | solution.py:45
  34.3 9.0 %collective-permute-start.10 = (bf16[2,4,64,128]{3,2,1,0:T(8,128)(2,1)S(1)}, bf16[2,4,64,128]{3,2,1,0:T(8,128)(2,1)S(1)}, u32[]{:S(2)}, u32[]{:S(2)}) collective-permute-start(bf16[2,4,64,128]{3,2,1,0:T(8,128)(2,1)S(1)} %bitcast_dynamic-update-slice_fusion.10), channel_id=1, source_target_pairs={{0,2},{1,3},{2,0},{3,1},{4,6},{5,7},{6,4},{7,5},{8,10},{9,11},{10,... | collective-permute-start | bytes 393224 | tf_op jit(solution)/shard_map/ppermute | solution.py:45
  36.3 7.1 %collective-permute-start.11 = (bf16[2,4,64,128]{3,2,1,0:T(8,128)(2,1)S(1)}, bf16[2,4,64,128]{3,2,1,0:T(8,128)(2,1)S(1)}, u32[]{:S(2)}, u32[]{:S(2)}) collective-permute-start(bf16[2,4,64,128]{3,2,1,0:T(8,128)(2,1)S(1)} %bitcast_dynamic-update-slice_fusion.10), channel_id=1, source_target_pairs={{0,3},{1,0},{2,1},{3,2},{4,7},{5,4},{6,5},{7,6},{8,11},{9,8},{10,9... | collective-permute-start | bytes 393224 | tf_op jit(solution)/shard_map/ppermute | solution.py:45
  45.6 14.2 %collective-permute-start.14 = (bf16[4,2,4,64,128]{4,3,2,1,0:T(8,128)(2,1)S(1)}, bf16[4,2,4,64,128]{4,3,2,1,0:T(8,128)(2,1)S(1)}, u32[]{:S(2)}, u32[]{:S(2)}) collective-permute-start(bf16[4,2,4,64,128]{4,3,2,1,0:T(8,128)(2,1)S(1)} %bitcast_dynamic-update-slice_fusion.4.refs_0_), channel_id=1, source_target_pairs={{0,8},{1,9},{2,10},{3,11},{4,12},{5,13},{6,14},{7,15},{8,16},{9,17... | collective-permute-start | bytes 1572872 | tf_op jit(solution)/shard_map/ppermute | solution.py:45
  46.6 13.2 %collective-permute-start.15 = (bf16[4,2,4,64,128]{4,3,2,1,0:T(8,128)(2,1)S(1)}, bf16[4,2,4,64,128]{4,3,2,1,0:T(8,128)(2,1)S(1)}, u32[]{:S(2)}, u32[]{:S(2)}) collective-permute-start(bf16[4,2,4,64,128]{4,3,2,1,0:T(8,128)(2,1)S(1)} %bitcast_dynamic-update-slice_fusion.4.refs_0_), channel_id=1, source_target_pairs={{0,24},{1,25},{2,26},{3,27},{4,28},{5,29},{6,30},{7,31},{8,0},{9,1... | collective-permute-start | bytes 1572872 | tf_op jit(solution)/shard_map/ppermute | solution.py:45
  50.5 3.7 %collective-permute-start.24 = (bf16[32,128]{1,0:T(8,128)(2,1)S(1)}, bf16[32,128]{1,0:T(8,128)(2,1)S(1)}, u32[]{:S(2)}, u32[]{:S(2)}) collective-permute-start(bf16[32,128]{1,0:T(8,128)(2,1)S(1)} %bitcast.114), channel_id=1, source_target_pairs={{0,1},{1,0},{2,3},{3,2},{4,5},{5,4},{6,7},{7,6},{8,9},{9,8},{10,11... | collective-permute-start | bytes 24584 | tf_op jit(solution)/shard_map/ppermute | solution.py:45
  54.3 5.4 %collective-permute-start.25 = (bf16[2,32,128]{2,1,0:T(8,128)(2,1)S(1)}, bf16[2,32,128]{2,1,0:T(8,128)(2,1)S(1)}, u32[]{:S(2)}, u32[]{:S(2)}) collective-permute-start(bf16[2,32,128]{2,1,0:T(8,128)(2,1)S(1)} %pad_maximum_fusion.5), channel_id=1, source_target_pairs={{0,2},{1,3},{2,0},{3,1},{4,6},{5,7},{6,4},{7,5},{8,10},{9,11},{10,... | collective-permute-start | bytes 49160 | tf_op jit(solution)/shard_map/ppermute | solution.py:45
  55.9 10.5 %collective-permute-start.12 = (bf16[64,4096]{1,0:T(8,128)(2,1)S(1)}, bf16[64,4096]{1,0:T(8,128)(2,1)S(1)}, u32[]{:S(2)}, u32[]{:S(2)}) collective-permute-start(bf16[64,4096]{1,0:T(8,128)(2,1)S(1)} %slice.52), channel_id=1, source_target_pairs={{0,8},{1,9},{2,10},{3,11},{4,12},{5,13},{6,14},{7,15},{8,16},{9,17... | collective-permute-start | bytes 1572872 | tf_op jit(solution)/shard_map/ppermute | solution.py:45
  56.0 9.9 %collective-permute-start.13 = (bf16[64,4096]{1,0:T(8,128)(2,1)S(1)}, bf16[64,4096]{1,0:T(8,128)(2,1)S(1)}, u32[]{:S(2)}, u32[]{:S(2)}) collective-permute-start(bf16[64,4096]{1,0:T(8,128)(2,1)S(1)} %slice.54), channel_id=1, source_target_pairs={{0,24},{1,25},{2,26},{3,27},{4,28},{5,29},{6,30},{7,31},{8,0},{9,1... | collective-permute-start | bytes 1572872 | tf_op jit(solution)/shard_map/ppermute | solution.py:45
  59.9 9.3 %collective-permute-start.16 = (bf16[2,2,4,64,128]{4,3,2,1,0:T(8,128)(2,1)S(1)}, bf16[2,2,4,64,128]{4,3,2,1,0:T(8,128)(2,1)S(1)}, u32[]{:S(2)}, u32[]{:S(2)}) collective-permute-start(bf16[2,2,4,64,128]{4,3,2,1,0:T(8,128)(2,1)S(1)} %slice.60), channel_id=1, source_target_pairs={{0,8},{1,9},{2,10},{3,11},{4,12},{5,13},{6,14},{7,15},{8,16},{9,17... | collective-permute-start | bytes 786440 | tf_op jit(solution)/shard_map/ppermute | solution.py:45
  60.0 9.2 %collective-permute-start.17 = (bf16[2,2,4,64,128]{4,3,2,1,0:T(8,128)(2,1)S(1)}, bf16[2,2,4,64,128]{4,3,2,1,0:T(8,128)(2,1)S(1)}, u32[]{:S(2)}, u32[]{:S(2)}) collective-permute-start(bf16[2,2,4,64,128]{4,3,2,1,0:T(8,128)(2,1)S(1)} %slice.61), channel_id=1, source_target_pairs={{0,24},{1,25},{2,26},{3,27},{4,28},{5,29},{6,30},{7,31},{8,0},{9,1... | collective-permute-start | bytes 786440 | tf_op jit(solution)/shard_map/ppermute | solution.py:45
  69.2 4.2 %collective-permute-start.18 = (bf16[4,2,4,64,128]{4,3,2,1,0:T(8,128)(2,1)S(1)}, bf16[4,2,4,64,128]{4,3,2,1,0:T(8,128)(2,1)S(1)}, u32[]{:S(2)}, u32[]{:S(2)}) collective-permute-start(bf16[4,2,4,64,128]{4,3,2,1,0:T(8,128)(2,1)S(1)} %bitcast_dynamic-update-slice_fusion.4.refs_0_), channel_id=1, source_target_pairs={{0,32},{1,33},{2,34},{3,35},{4,36},{5,37},{6,38},{7,39},{8,40},{9,... | collective-permute-start | bytes 1572872 | tf_op jit(solution)/shard_map/ppermute | solution.py:45
  69.2 4.2 %collective-permute-start.19 = (bf16[4,2,4,64,128]{4,3,2,1,0:T(8,128)(2,1)S(1)}, bf16[4,2,4,64,128]{4,3,2,1,0:T(8,128)(2,1)S(1)}, u32[]{:S(2)}, u32[]{:S(2)}) collective-permute-start(bf16[4,2,4,64,128]{4,3,2,1,0:T(8,128)(2,1)S(1)} %collective-permute-done.14.refs_1_), channel_id=1, source_target_pairs={{0,32},{1,33},{2,34},{3,35},{4,36},{5,37},{6,38},{7,39},{8,40},{9,... | collective-permute-start | bytes 1572872 | tf_op jit(solution)/shard_map/ppermute | solution.py:45
  69.7 3.7 %collective-permute-start.20 = (bf16[4,2,4,64,128]{4,3,2,1,0:T(8,128)(2,1)S(1)}, bf16[4,2,4,64,128]{4,3,2,1,0:T(8,128)(2,1)S(1)}, u32[]{:S(2)}, u32[]{:S(2)}) collective-permute-start(bf16[4,2,4,64,128]{4,3,2,1,0:T(8,128)(2,1)S(1)} %collective-permute-done.15.refs_2_), channel_id=1, source_target_pairs={{0,32},{1,33},{2,34},{3,35},{4,36},{5,37},{6,38},{7,39},{8,40},{9,... | collective-permute-start | bytes 1572872 | tf_op jit(solution)/shard_map/ppermute | solution.py:45
  70.2 2.8 %collective-permute-start.21 = (bf16[2,2,4,64,128]{4,3,2,1,0:T(8,128)(2,1)S(1)}, bf16[2,2,4,64,128]{4,3,2,1,0:T(8,128)(2,1)S(1)}, u32[]{:S(2)}, u32[]{:S(2)}) collective-permute-start(bf16[2,2,4,64,128]{4,3,2,1,0:T(8,128)(2,1)S(1)} %collective-permute-done.16.refs_3_), channel_id=1, source_target_pairs={{0,32},{1,33},{2,34},{3,35},{4,36},{5,37},{6,38},{7,39},{8,40},{9,... | collective-permute-start | bytes 786440 | tf_op jit(solution)/shard_map/ppermute | solution.py:45
  70.8 2.6 %collective-permute-start.22 = (bf16[2,2,4,64,128]{4,3,2,1,0:T(8,128)(2,1)S(1)}, bf16[2,2,4,64,128]{4,3,2,1,0:T(8,128)(2,1)S(1)}, u32[]{:S(2)}, u32[]{:S(2)}) collective-permute-start(bf16[2,2,4,64,128]{4,3,2,1,0:T(8,128)(2,1)S(1)} %collective-permute-done.17.refs_4_), channel_id=1, source_target_pairs={{0,32},{1,33},{2,34},{3,35},{4,36},{5,37},{6,38},{7,39},{8,40},{9,... | collective-permute-start | bytes 786440 | tf_op jit(solution)/shard_map/ppermute | solution.py:45
  81.9 16.5 %collective-permute-start.26 = (bf16[64,8192]{1,0:T(8,128)(2,1)S(1)}, bf16[64,8192]{1,0:T(8,128)(2,1)S(1)}, u32[]{:S(2)}, u32[]{:S(2)}) collective-permute-start(bf16[64,8192]{1,0:T(8,128)(2,1)S(1)} %get-tuple-element.50), channel_id=1, source_target_pairs={{0,16},{1,17},{2,18},{3,19},{4,20},{5,21},{6,22},{7,23},{8,24},{9,... | collective-permute-start | bytes 3145736 | tf_op jit(solution)/shard_map/ppermute | solution.py:45
  84.2 25.3 %collective-permute-start.27 = (bf16[64,8192]{1,0:T(8,128)(2,1)S(1)}, bf16[64,8192]{1,0:T(8,128)(2,1)S(1)}, u32[]{:S(2)}, u32[]{:S(2)}) collective-permute-start(bf16[64,8192]{1,0:T(8,128)(2,1)S(1)} %get-tuple-element.51), channel_id=1, source_target_pairs={{0,8},{1,9},{2,10},{3,11},{4,12},{5,13},{6,14},{7,15},{8,16},{9,17... | collective-permute-start | bytes 3145736 | tf_op jit(solution)/shard_map/ppermute | solution.py:45
  86.0 24.1 %collective-permute-start.28 = (bf16[64,8192]{1,0:T(8,128)(2,1)S(1)}, bf16[64,8192]{1,0:T(8,128)(2,1)S(1)}, u32[]{:S(2)}, u32[]{:S(2)}) collective-permute-start(bf16[64,8192]{1,0:T(8,128)(2,1)S(1)} %get-tuple-element.52), channel_id=1, source_target_pairs={{0,24},{1,25},{2,26},{3,27},{4,28},{5,29},{6,30},{7,31},{8,0},{9,1... | collective-permute-start | bytes 3145736 | tf_op jit(solution)/shard_map/ppermute | solution.py:45
  111.0 7.7 %collective-permute-start.29 = (bf16[16,8192]{1,0:T(8,128)(2,1)S(1)}, bf16[16,8192]{1,0:T(8,128)(2,1)S(1)}, u32[]{:S(2)}, u32[]{:S(2)}) collective-permute-start(bf16[16,8192]{1,0:T(8,128)(2,1)S(1)} %get-tuple-element.54), channel_id=1, source_target_pairs={{0,1},{1,2},{2,3},{3,0},{4,5},{5,6},{6,7},{7,4},{8,9},{9,10},{10,1... | collective-permute-start | bytes 786440 | tf_op jit(solution)/shard_map/ppermute | solution.py:45
  111.8 10.3 %collective-permute-start.30 = (bf16[16,8192]{1,0:T(8,128)(2,1)S(1)}, bf16[16,8192]{1,0:T(8,128)(2,1)S(1)}, u32[]{:S(2)}, u32[]{:S(2)}) collective-permute-start(bf16[16,8192]{1,0:T(8,128)(2,1)S(1)} %get-tuple-element.55), channel_id=1, source_target_pairs={{0,2},{1,3},{2,0},{3,1},{4,6},{5,7},{6,4},{7,5},{8,10},{9,11},{10,... | collective-permute-start | bytes 786440 | tf_op jit(solution)/shard_map/ppermute | solution.py:45
  114.9 7.5 %collective-permute-start.31 = (bf16[16,8192]{1,0:T(8,128)(2,1)S(1)}, bf16[16,8192]{1,0:T(8,128)(2,1)S(1)}, u32[]{:S(2)}, u32[]{:S(2)}) collective-permute-start(bf16[16,8192]{1,0:T(8,128)(2,1)S(1)} %get-tuple-element.56), channel_id=1, source_target_pairs={{0,3},{1,0},{2,1},{3,2},{4,7},{5,4},{6,5},{7,6},{8,11},{9,8},{10,9... | collective-permute-start | bytes 786440 | tf_op jit(solution)/shard_map/ppermute | solution.py:45
  122.5 5.1 %collective-permute-start.32 = (bf16[8,8192]{1,0:T(8,128)(2,1)S(1)}, bf16[8,8192]{1,0:T(8,128)(2,1)S(1)}, u32[]{:S(2)}, u32[]{:S(2)}) collective-permute-start(bf16[8,8192]{1,0:T(8,128)(2,1)S(1)} %fusion.26), channel_id=1, source_target_pairs={{0,4},{1,5},{2,6},{3,7},{4,0},{5,1},{6,2},{7,3},{8,12},{9,13},{10,... | collective-permute-start | bytes 393224 | tf_op jit(solution)/shard_map/ppermute | solution.py:45
  (7 other events, 95.5 us)

commit v4 on v3

--- a/solution.py
+++ b/solution.py
@@ -136,6 +136,7 @@
             there = lax.rem(spot_ref[2] - t + 4, 4)
             x = jnp.where(first_core, here, there)
             y = jnp.where(first_core, there, here)
+            rows, factors = [], []
             for zl in range(2):
                 mine = shard(0, s, there, zl)
                 theirs = shard(1, t, here, zl)
@@ -143,18 +144,21 @@
                     [jnp.where(first_core, mine, theirs), jnp.where(first_core, theirs, mine)],
                     axis=1,
                 )
-                down = both[:, :, :32].reshape(256, 128)
                 rest = both[:, :, 32:].reshape(256, 128)
+                factors.append(jnp.concatenate([both[:, :, :32].reshape(256, 128), rest], axis=1))
                 index = x * 8 + zl * 4 + y
                 at = pl.ds(pl.multiple_of(index * 256, 256), 256)
                 halved = pl.ds(pl.multiple_of(lax.rem(index, 16) * 256, 256), 256)
                 two = jnp.where(index < 16, left_ref[:, halved], right_ref[:, halved])
-                rows = jnp.concatenate(
-                    [eight_ref[:, at], one_ref[:, at], two, three_ref[:, at]], axis=0
+                rows.append(
+                    jnp.concatenate([eight_ref[:, at], one_ref[:, at], two, three_ref[:, at]], axis=0)
                 )
-                total[:, :128] += jnp.dot(rows, down, preferred_element_type=jnp.float32)
-                total[:, 128:] += jnp.dot(rows, rest, preferred_element_type=jnp.float32)
                 up_ref[at, :] = rest
+            total[...] += jnp.dot(
+                jnp.concatenate(rows, axis=1),
+                jnp.concatenate(factors, axis=0),
+                preferred_element_type=jnp.float32,
+            )
     inner_ref[...] = total[...]
 
 

time: 129 us -> 128 us (level)
  no operation moved by 1% of the time
where the time goes in v4:
time: 128 us; the launch traced here: 127 us
  waiting for transfers between devices  58.7 us (46%)
  starting transfers between devices  44.8 us (35%)
  Pallas kernels  8.46 us (7%)
  other arithmetic  6.91 us (5%)
  matrix products  6.72 us (5%)
    ppermute x33, waiting for transfers between devices, permute(): return lax.ppermute(block, AXES, source_to_target)  58.7 us
    ppermute x33, starting transfers between devices, permute(): return lax.ppermute(block, AXES, source_to_target)  44.8 us
    dot_general x10, matrix products, dot32(): return jnp.dot(left, right, preferred_element_type=jnp.float32)  6.72 us
    pallas_call x1, Pallas kernels, attend_rows(): pl.pallas_call(attend_kernel, in_specs=[spec_smem(), spec_smem()] + [pl.B...  2.83 us
  transfers between devices with their start and end apart: 33, of which 20 were waited for; matrix products, arithmetic and copies ran while one was open for 9% of the time, Pallas kernels for 0%

profile of v4, /device:TPU:64, one launch (start us, length us, event | category | flops | bytes accessed | tf_op | source)
XLA Modules:
  0.0 127.3 jit_solution(8669029221324095871)
XLA Ops:
  2.2 2.0 %collective-permute-start = (bf16[8,8192]{1,0:T(8,128)(2,1)S(1)}, bf16[8,8192]{1,0:T(8,128)(2,1)S(1)}, u32[]{:S(2)}, u32[]{:S(2)}) collective-permute-start(bf16[8,8192]{1,0:T(8,128)(2,1)S(1)} %get-tuple-element.58), channel_id=1, source_target_pairs={{0,4},{1,5},{2,6},{3,7},{4,0},{5,1},{6,2},{7,3},{8,12},{9,13},{10,... | collective-permute-start | bytes 393224 | tf_op jit(solution)/shard_map/ppermute | solution.py:45
  8.6 3.0 %collective-permute-done.6 = bf16[112,128]{1,0:T(8,128)(2,1)S(1)} collective-permute-done((bf16[112,128]{1,0:T(8,128)(2,1)S(1)}, bf16[112,128]{1,0:T(8,128)(2,1)S(1)}, u32[]{:S(2)}, u32[]{:S(2)}) %collective-permute-start.6) | collective-permute-done | bytes 28704 | tf_op jit(solution)/shard_map/ppermute | solution.py:45
  11.6 1.7 %collective-permute-start.1 = (bf16[16,8192]{1,0:T(8,128)(2,1)S(1)}, bf16[16,8192]{1,0:T(8,128)(2,1)S(1)}, u32[]{:S(2)}, u32[]{:S(2)}) collective-permute-start(bf16[16,8192]{1,0:T(8,128)(2,1)S(1)} %bitcast.105), channel_id=1, source_target_pairs={{0,1},{1,2},{2,3},{3,0},{4,5},{5,6},{6,7},{7,4},{8,9},{9,10},{10,1... | collective-permute-start | bytes 786440 | tf_op jit(solution)/shard_map/ppermute | solution.py:45
  13.3 2.9 %collective-permute-start.2 = (bf16[16,8192]{1,0:T(8,128)(2,1)S(1)}, bf16[16,8192]{1,0:T(8,128)(2,1)S(1)}, u32[]{:S(2)}, u32[]{:S(2)}) collective-permute-start(bf16[16,8192]{1,0:T(8,128)(2,1)S(1)} %bitcast.106), channel_id=1, source_target_pairs={{0,2},{1,3},{2,0},{3,1},{4,6},{5,7},{6,4},{7,5},{8,10},{9,11},{10,... | collective-permute-start | bytes 786440 | tf_op jit(solution)/shard_map/ppermute | solution.py:45
  17.5 4.5 %collective-permute-start.7 = (bf16[2,112,128]{2,1,0:T(8,128)(2,1)S(1)}, bf16[2,112,128]{2,1,0:T(8,128)(2,1)S(1)}, u32[]{:S(2)}, u32[]{:S(2)}) collective-permute-start(bf16[2,112,128]{2,1,0:T(8,128)(2,1)S(1)} %pad_maximum_fusion.3), channel_id=1, source_target_pairs={{0,128},{1,129},{2,130},{3,131},{4,132},{5,133},{6,134},{7,135},{8... | collective-permute-start | bytes 172040 | tf_op jit(solution)/shard_map/ppermute | solution.py:45
  22.2 3.6 %collective-permute-done.7 = bf16[2,112,128]{2,1,0:T(8,128)(2,1)S(1)} collective-permute-done((bf16[2,112,128]{2,1,0:T(8,128)(2,1)S(1)}, bf16[2,112,128]{2,1,0:T(8,128)(2,1)S(1)}, u32[]{:S(2)}, u32[]{:S(2)}) %collective-permute-start.7) | collective-permute-done | bytes 57376 | tf_op jit(solution)/shard_map/ppermute | solution.py:45
  26.0 2.0 %collective-permute-start.4 = (bf16[64,8192]{1,0:T(8,128)(2,1)S(1)}, bf16[64,8192]{1,0:T(8,128)(2,1)S(1)}, u32[]{:S(2)}, u32[]{:S(2)}) collective-permute-start(bf16[64,8192]{1,0:T(8,128)(2,1)S(1)} %bitcast.97), channel_id=1, source_target_pairs={{0,8},{1,9},{2,10},{3,11},{4,12},{5,13},{6,14},{7,15},{8,16},{9,17... | collective-permute-start | bytes 3145736 | tf_op jit(solution)/shard_map/ppermute | solution.py:45
  31.8 1.8 %collective-permute-done.8 = bf16[4,64,128]{2,1,0:T(8,128)(2,1)S(1)} collective-permute-done((bf16[4,64,128]{2,1,0:T(8,128)(2,1)S(1)}, bf16[4,64,128]{2,1,0:T(8,128)(2,1)S(1)}, u32[]{:S(2)}, u32[]{:S(2)}) %collective-permute-start.8) | collective-permute-done | bytes 65568 | tf_op jit(solution)/shard_map/ppermute | solution.py:45
  34.3 1.9 %collective-permute-start.10 = (bf16[2,4,64,128]{3,2,1,0:T(8,128)(2,1)S(1)}, bf16[2,4,64,128]{3,2,1,0:T(8,128)(2,1)S(1)}, u32[]{:S(2)}, u32[]{:S(2)}) collective-permute-start(bf16[2,4,64,128]{3,2,1,0:T(8,128)(2,1)S(1)} %bitcast_dynamic-update-slice_fusion.10), channel_id=1, source_target_pairs={{0,2},{1,3},{2,0},{3,1},{4,6},{5,7},{6,4},{7,5},{8,10},{9,11},{10,... | collective-permute-start | bytes 393224 | tf_op jit(solution)/shard_map/ppermute | solution.py:45
  37.7 3.1 %collective-permute-done.9 = bf16[2,4,64,128]{3,2,1,0:T(8,128)(2,1)S(1)} collective-permute-done((bf16[2,4,64,128]{3,2,1,0:T(8,128)(2,1)S(1)}, bf16[2,4,64,128]{3,2,1,0:T(8,128)(2,1)S(1)}, u32[]{:S(2)}, u32[]{:S(2)}) %collective-permute-start.9) | collective-permute-done | bytes 131104 | tf_op jit(solution)/shard_map/ppermute | solution.py:45
  40.8 2.5 %collective-permute-done.10 = bf16[2,4,64,128]{3,2,1,0:T(8,128)(2,1)S(1)} collective-permute-done((bf16[2,4,64,128]{3,2,1,0:T(8,128)(2,1)S(1)}, bf16[2,4,64,128]{3,2,1,0:T(8,128)(2,1)S(1)}, u32[]{:S(2)}, u32[]{:S(2)}) %collective-permute-start.10) | collective-permute-done | bytes 131104 | tf_op jit(solution)/shard_map/ppermute | solution.py:45
  43.4 1.5 %collective-permute-done.4.one_ref = bf16[64,8192]{1,0:T(8,128)(2,1)S(1)} collective-permute-done((bf16[64,8192]{1,0:T(8,128)(2,1)S(1)}, bf16[64,8192]{1,0:T(8,128)(2,1)S(1)}, u32[]{:S(2)}, u32[]{:S(2)}) %collective-permute-start.4) | collective-permute-done | bytes 1048608 | tf_op jit(solution)/shard_map/ppermute | solution.py:45
  46.6 2.2 %collective-permute-start.15 = (bf16[4,2,4,64,128]{4,3,2,1,0:T(8,128)(2,1)S(1)}, bf16[4,2,4,64,128]{4,3,2,1,0:T(8,128)(2,1)S(1)}, u32[]{:S(2)}, u32[]{:S(2)}) collective-permute-start(bf16[4,2,4,64,128]{4,3,2,1,0:T(8,128)(2,1)S(1)} %bitcast_dynamic-update-slice_fusion.4.refs_0_), channel_id=1, source_target_pairs={{0,24},{1,25},{2,26},{3,27},{4,28},{5,29},{6,30},{7,31},{8,0},{9,1... | collective-permute-start | bytes 1572872 | tf_op jit(solution)/shard_map/ppermute | solution.py:45
  51.7 2.6 %collective-permute-done.24 = bf16[32,128]{1,0:T(8,128)(2,1)S(1)} collective-permute-done((bf16[32,128]{1,0:T(8,128)(2,1)S(1)}, bf16[32,128]{1,0:T(8,128)(2,1)S(1)}, u32[]{:S(2)}, u32[]{:S(2)}) %collective-permute-start.24) | collective-permute-done | bytes 8224 | tf_op jit(solution)/shard_map/ppermute | solution.py:45
  56.0 3.2 %collective-permute-start.13 = (bf16[64,4096]{1,0:T(8,128)(2,1)S(1)}, bf16[64,4096]{1,0:T(8,128)(2,1)S(1)}, u32[]{:S(2)}, u32[]{:S(2)}) collective-permute-start(bf16[64,4096]{1,0:T(8,128)(2,1)S(1)} %slice.54), channel_id=1, source_target_pairs={{0,24},{1,25},{2,26},{3,27},{4,28},{5,29},{6,30},{7,31},{8,0},{9,1... | collective-permute-start | bytes 1572872 | tf_op jit(solution)/shard_map/ppermute | solution.py:45
  60.0 3.3 %collective-permute-start.17 = (bf16[2,2,4,64,128]{4,3,2,1,0:T(8,128)(2,1)S(1)}, bf16[2,2,4,64,128]{4,3,2,1,0:T(8,128)(2,1)S(1)}, u32[]{:S(2)}, u32[]{:S(2)}) collective-permute-start(bf16[2,2,4,64,128]{4,3,2,1,0:T(8,128)(2,1)S(1)} %slice.61), channel_id=1, source_target_pairs={{0,24},{1,25},{2,26},{3,27},{4,28},{5,29},{6,30},{7,31},{8,0},{9,1... | collective-permute-start | bytes 786440 | tf_op jit(solution)/shard_map/ppermute | solution.py:45
  63.3 2.6 %collective-permute-done.13.right_ref = bf16[64,4096]{1,0:T(8,128)(2,1)S(1)} collective-permute-done((bf16[64,4096]{1,0:T(8,128)(2,1)S(1)}, bf16[64,4096]{1,0:T(8,128)(2,1)S(1)}, u32[]{:S(2)}, u32[]{:S(2)}) %collective-permute-start.13) | collective-permute-done | bytes 524320 | tf_op jit(solution)/shard_map/ppermute | solution.py:45
  66.8 2.3 %collective-permute-done.16.refs_3_ = bf16[2,2,4,64,128]{4,3,2,1,0:T(8,128)(2,1)S(1)} collective-permute-done((bf16[2,2,4,64,128]{4,3,2,1,0:T(8,128)(2,1)S(1)}, bf16[2,2,4,64,128]{4,3,2,1,0:T(8,128)(2,1)S(1)}, u32[]{:S(2)}, u32[]{:S(2)}) %collective-permute-start.16) | collective-permute-done | bytes 262176 | tf_op jit(solution)/shard_map/ppermute | solution.py:45
  71.6 1.4 %collective-permute-done.21.refs_8_ = bf16[2,2,4,64,128]{4,3,2,1,0:T(8,128)(2,1)S(1)} collective-permute-done((bf16[2,2,4,64,128]{4,3,2,1,0:T(8,128)(2,1)S(1)}, bf16[2,2,4,64,128]{4,3,2,1,0:T(8,128)(2,1)S(1)}, u32[]{:S(2)}, u32[]{:S(2)}) %collective-permute-start.21) | collective-permute-done | bytes 262176 | tf_op jit(solution)/shard_map/ppermute | solution.py:45
  73.3 2.3 %shard_map.154 = (f32[256,256]{1,0:T(8,128)S(1)}, bf16[8192,128]{1,0:T(8,128)(2,1)S(1)}) custom-call(s32[3]{0:T(128)S(1)} %pad_add_fusion.spot_ref, bf16[64,8192]{1,0:T(8,128)(2,1)S(1)} %bitcast.101, bf16[64,8192]{1,0:T(8,128)(2,1)S(1)} %collective-permute-done.4.one_ref, bf16[64,4096]{1,0:T(8,128)(2,1)S(1)} %collective-permute-done.12.left_ref, ...), custom_call_target="tpu_custom_call" | custom-call | flops 1073741824 | bytes 10485760 | tf_op jit(solution)/shard_map/pallas_call | solution.py:166
  75.7 2.8 %shard_map.155 = (bf16[256,256]{1,0:T(8,128)(2,1)S(1)}, bf16[256,128]{1,0:T(8,128)(2,1)S(1)}) custom-call(s32[3]{0:T(128)S(1)} %pad_add_fusion.spot_ref, s32[4]{0:T(128)S(1)} %copy-done.2, f32[64,256]{1,0:T(8,128)S(1)} %fusion.30.refs_0_, f32[64,256]{1,0:T(8,128)S(1)} %fusion.31.refs_1_, f32[64,256]{1,0:T(8,128)S(1)} %fusion.16.refs_2_, ...), custom_call_target="tpu_custom_call" | custom-call | flops 83886080 | bytes 4194304 | tf_op jit(solution)/shard_map/pallas_call | solution.py:268
  78.5 2.4 %shard_map.156 = (bf16[64,8192]{1,0:T(8,128)(2,1)S(1)}, bf16[64,8192]{1,0:T(8,128)(2,1)S(1)}, bf16[64,8192]{1,0:T(8,128)(2,1)S(1)}, bf16[64,8192]{1,0:T(8,128)(2,1)S(1)}) custom-call(bf16[256,256]{1,0:T(8,128)(2,1)S(1)} %get-tuple-element.46.rows_ref, bf16[256,128]{1,0:T(8,128)(2,1)S(1)} %get-tuple-element.47.inner_ref, bf16[256,8192]{1,0:T(8,128)(2,1)S(1)} %copy-done, ...), custom_call_target="tpu_custom_call" | custom-call | flops 1073741824 | bytes 8388608 | tf_op jit(solution)/shard_map/pallas_call | solution.py:327
  80.9 2.4 %collective-permute-start.26 = (bf16[64,8192]{1,0:T(8,128)(2,1)S(1)}, bf16[64,8192]{1,0:T(8,128)(2,1)S(1)}, u32[]{:S(2)}, u32[]{:S(2)}) collective-permute-start(bf16[64,8192]{1,0:T(8,128)(2,1)S(1)} %get-tuple-element.50), channel_id=1, source_target_pairs={{0,16},{1,17},{2,18},{3,19},{4,20},{5,21},{6,22},{7,23},{8,24},{9,... | collective-permute-start | bytes 3145736 | tf_op jit(solution)/shard_map/ppermute | solution.py:45
  83.3 1.8 %collective-permute-start.27 = (bf16[64,8192]{1,0:T(8,128)(2,1)S(1)}, bf16[64,8192]{1,0:T(8,128)(2,1)S(1)}, u32[]{:S(2)}, u32[]{:S(2)}) collective-permute-start(bf16[64,8192]{1,0:T(8,128)(2,1)S(1)} %get-tuple-element.51), channel_id=1, source_target_pairs={{0,8},{1,9},{2,10},{3,11},{4,12},{5,13},{6,14},{7,15},{8,16},{9,17... | collective-permute-start | bytes 3145736 | tf_op jit(solution)/shard_map/ppermute | solution.py:45
  85.1 1.4 %collective-permute-start.28 = (bf16[64,8192]{1,0:T(8,128)(2,1)S(1)}, bf16[64,8192]{1,0:T(8,128)(2,1)S(1)}, u32[]{:S(2)}, u32[]{:S(2)}) collective-permute-start(bf16[64,8192]{1,0:T(8,128)(2,1)S(1)} %get-tuple-element.52), channel_id=1, source_target_pairs={{0,24},{1,25},{2,26},{3,27},{4,28},{5,29},{6,30},{7,31},{8,0},{9,1... | collective-permute-start | bytes 3145736 | tf_op jit(solution)/shard_map/ppermute | solution.py:45
  86.5 10.9 %collective-permute-done.26.refs_1_ = bf16[64,8192]{1,0:T(8,128)(2,1)S(1)} collective-permute-done((bf16[64,8192]{1,0:T(8,128)(2,1)S(1)}, bf16[64,8192]{1,0:T(8,128)(2,1)S(1)}, u32[]{:S(2)}, u32[]{:S(2)}) %collective-permute-start.26) | collective-permute-done | bytes 1048608 | tf_op jit(solution)/shard_map/ppermute | solution.py:45
  97.4 11.1 %collective-permute-done.27.refs_2_ = bf16[64,8192]{1,0:T(8,128)(2,1)S(1)} collective-permute-done((bf16[64,8192]{1,0:T(8,128)(2,1)S(1)}, bf16[64,8192]{1,0:T(8,128)(2,1)S(1)}, u32[]{:S(2)}, u32[]{:S(2)}) %collective-permute-start.27) | collective-permute-done | bytes 1048608 | tf_op jit(solution)/shard_map/ppermute | solution.py:45
  110.8 3.1 %collective-permute-start.30 = (bf16[16,8192]{1,0:T(8,128)(2,1)S(1)}, bf16[16,8192]{1,0:T(8,128)(2,1)S(1)}, u32[]{:S(2)}, u32[]{:S(2)}) collective-permute-start(bf16[16,8192]{1,0:T(8,128)(2,1)S(1)} %get-tuple-element.55), channel_id=1, source_target_pairs={{0,2},{1,3},{2,0},{3,1},{4,6},{5,7},{6,4},{7,5},{8,10},{9,11},{10,... | collective-permute-start | bytes 786440 | tf_op jit(solution)/shard_map/ppermute | solution.py:45
  114.0 1.8 %collective-permute-start.31 = (bf16[16,8192]{1,0:T(8,128)(2,1)S(1)}, bf16[16,8192]{1,0:T(8,128)(2,1)S(1)}, u32[]{:S(2)}, u32[]{:S(2)}) collective-permute-start(bf16[16,8192]{1,0:T(8,128)(2,1)S(1)} %get-tuple-element.56), channel_id=1, source_target_pairs={{0,3},{1,0},{2,1},{3,2},{4,7},{5,4},{6,5},{7,6},{8,11},{9,8},{10,9... | collective-permute-start | bytes 786440 | tf_op jit(solution)/shard_map/ppermute | solution.py:45
  115.7 2.0 %collective-permute-done.29 = bf16[16,8192]{1,0:T(8,128)(2,1)S(1)} collective-permute-done((bf16[16,8192]{1,0:T(8,128)(2,1)S(1)}, bf16[16,8192]{1,0:T(8,128)(2,1)S(1)}, u32[]{:S(2)}, u32[]{:S(2)}) %collective-permute-start.29) | collective-permute-done | bytes 262176 | tf_op jit(solution)/shard_map/ppermute | solution.py:45
  117.8 3.4 %collective-permute-done.30 = bf16[16,8192]{1,0:T(8,128)(2,1)S(1)} collective-permute-done((bf16[16,8192]{1,0:T(8,128)(2,1)S(1)}, bf16[16,8192]{1,0:T(8,128)(2,1)S(1)}, u32[]{:S(2)}, u32[]{:S(2)}) %collective-permute-start.30) | collective-permute-done | bytes 262176 | tf_op jit(solution)/shard_map/ppermute | solution.py:45
  122.1 4.5 %collective-permute-done.32 = bf16[8,8192]{1,0:T(8,128)(2,1)S(1)} collective-permute-done((bf16[8,8192]{1,0:T(8,128)(2,1)S(1)}, bf16[8,8192]{1,0:T(8,128)(2,1)S(1)}, u32[]{:S(2)}, u32[]{:S(2)}) %collective-permute-start.32) | collective-permute-done | bytes 131104 | tf_op jit(solution)/shard_map/ppermute | solution.py:45
  (115 shorter events, 28.8 us)
Async XLA Ops:
  2.2 9.5 %collective-permute-start = (bf16[8,8192]{1,0:T(8,128)(2,1)S(1)}, bf16[8,8192]{1,0:T(8,128)(2,1)S(1)}, u32[]{:S(2)}, u32[]{:S(2)}) collective-permute-start(bf16[8,8192]{1,0:T(8,128)(2,1)S(1)} %get-tuple-element.58), channel_id=1, source_target_pairs={{0,4},{1,5},{2,6},{3,7},{4,0},{5,1},{6,2},{7,3},{8,12},{9,13},{10,... | collective-permute-start | bytes 393224 | tf_op jit(solution)/shard_map/ppermute | solution.py:45
  6.7 4.9 %collective-permute-start.6 = (bf16[112,128]{1,0:T(8,128)(2,1)S(1)}, bf16[112,128]{1,0:T(8,128)(2,1)S(1)}, u32[]{:S(2)}, u32[]{:S(2)}) collective-permute-start(bf16[112,128]{1,0:T(8,128)(2,1)S(1)} %concatenate.25), channel_id=1, source_target_pairs={{0,64},{1,65},{2,66},{3,67},{4,68},{5,69},{6,70},{7,71},{8,72},{9,... | collective-permute-start | bytes 86024 | tf_op jit(solution)/shard_map/ppermute | solution.py:45
  11.6 14.2 %collective-permute-start.1 = (bf16[16,8192]{1,0:T(8,128)(2,1)S(1)}, bf16[16,8192]{1,0:T(8,128)(2,1)S(1)}, u32[]{:S(2)}, u32[]{:S(2)}) collective-permute-start(bf16[16,8192]{1,0:T(8,128)(2,1)S(1)} %bitcast.105), channel_id=1, source_target_pairs={{0,1},{1,2},{2,3},{3,0},{4,5},{5,6},{6,7},{7,4},{8,9},{9,10},{10,1... | collective-permute-start | bytes 786440 | tf_op jit(solution)/shard_map/ppermute | solution.py:45
  13.3 12.6 %collective-permute-start.2 = (bf16[16,8192]{1,0:T(8,128)(2,1)S(1)}, bf16[16,8192]{1,0:T(8,128)(2,1)S(1)}, u32[]{:S(2)}, u32[]{:S(2)}) collective-permute-start(bf16[16,8192]{1,0:T(8,128)(2,1)S(1)} %bitcast.106), channel_id=1, source_target_pairs={{0,2},{1,3},{2,0},{3,1},{4,6},{5,7},{6,4},{7,5},{8,10},{9,11},{10,... | collective-permute-start | bytes 786440 | tf_op jit(solution)/shard_map/ppermute | solution.py:45
  16.2 9.7 %collective-permute-start.3 = (bf16[16,8192]{1,0:T(8,128)(2,1)S(1)}, bf16[16,8192]{1,0:T(8,128)(2,1)S(1)}, u32[]{:S(2)}, u32[]{:S(2)}) collective-permute-start(bf16[16,8192]{1,0:T(8,128)(2,1)S(1)} %bitcast.107), channel_id=1, source_target_pairs={{0,3},{1,0},{2,1},{3,2},{4,7},{5,4},{6,5},{7,6},{8,11},{9,8},{10,9... | collective-permute-start | bytes 786440 | tf_op jit(solution)/shard_map/ppermute | solution.py:45
  17.5 8.3 %collective-permute-start.7 = (bf16[2,112,128]{2,1,0:T(8,128)(2,1)S(1)}, bf16[2,112,128]{2,1,0:T(8,128)(2,1)S(1)}, u32[]{:S(2)}, u32[]{:S(2)}) collective-permute-start(bf16[2,112,128]{2,1,0:T(8,128)(2,1)S(1)} %pad_maximum_fusion.3), channel_id=1, source_target_pairs={{0,128},{1,129},{2,130},{3,131},{4,132},{5,133},{6,134},{7,135},{8... | collective-permute-start | bytes 172040 | tf_op jit(solution)/shard_map/ppermute | solution.py:45
  26.0 18.9 %collective-permute-start.4 = (bf16[64,8192]{1,0:T(8,128)(2,1)S(1)}, bf16[64,8192]{1,0:T(8,128)(2,1)S(1)}, u32[]{:S(2)}, u32[]{:S(2)}) collective-permute-start(bf16[64,8192]{1,0:T(8,128)(2,1)S(1)} %bitcast.97), channel_id=1, source_target_pairs={{0,8},{1,9},{2,10},{3,11},{4,12},{5,13},{6,14},{7,15},{8,16},{9,17... | collective-permute-start | bytes 3145736 | tf_op jit(solution)/shard_map/ppermute | solution.py:45
  28.0 17.6 %collective-permute-start.5 = (bf16[64,8192]{1,0:T(8,128)(2,1)S(1)}, bf16[64,8192]{1,0:T(8,128)(2,1)S(1)}, u32[]{:S(2)}, u32[]{:S(2)}) collective-permute-start(bf16[64,8192]{1,0:T(8,128)(2,1)S(1)} %bitcast.98), channel_id=1, source_target_pairs={{0,24},{1,25},{2,26},{3,27},{4,28},{5,29},{6,30},{7,31},{8,0},{9,1... | collective-permute-start | bytes 3145736 | tf_op jit(solution)/shard_map/ppermute | solution.py:45
  29.3 4.3 %collective-permute-start.8 = (bf16[4,64,128]{2,1,0:T(8,128)(2,1)S(1)}, bf16[4,64,128]{2,1,0:T(8,128)(2,1)S(1)}, u32[]{:S(2)}, u32[]{:S(2)}) collective-permute-start(bf16[4,64,128]{2,1,0:T(8,128)(2,1)S(1)} %slice.51), channel_id=1, source_target_pairs={{0,4},{1,5},{2,6},{3,7},{4,0},{5,1},{6,2},{7,3},{8,12},{9,13},{10,... | collective-permute-start | bytes 196616 | tf_op jit(solution)/shard_map/ppermute | solution.py:45
  33.6 7.2 %collective-permute-start.9 = (bf16[2,4,64,128]{3,2,1,0:T(8,128)(2,1)S(1)}, bf16[2,4,64,128]{3,2,1,0:T(8,128)(2,1)S(1)}, u32[]{:S(2)}, u32[]{:S(2)}) collective-permute-start(bf16[2,4,64,128]{3,2,1,0:T(8,128)(2,1)S(1)} %bitcast_dynamic-update-slice_fusion.10), channel_id=1, source_target_pairs={{0,1},{1,2},{2,3},{3,0},{4,5},{5,6},{6,7},{7,4},{8,9},{9,10},{10,1... | collective-permute-start | bytes 393224 | tf_op jit(solution)/shard_map/ppermute | solution.py:45
  34.3 9.0 %collective-permute-start.10 = (bf16[2,4,64,128]{3,2,1,0:T(8,128)(2,1)S(1)}, bf16[2,4,64,128]{3,2,1,0:T(8,128)(2,1)S(1)}, u32[]{:S(2)}, u32[]{:S(2)}) collective-permute-start(bf16[2,4,64,128]{3,2,1,0:T(8,128)(2,1)S(1)} %bitcast_dynamic-update-slice_fusion.10), channel_id=1, source_target_pairs={{0,2},{1,3},{2,0},{3,1},{4,6},{5,7},{6,4},{7,5},{8,10},{9,11},{10,... | collective-permute-start | bytes 393224 | tf_op jit(solution)/shard_map/ppermute | solution.py:45
  36.3 7.1 %collective-permute-start.11 = (bf16[2,4,64,128]{3,2,1,0:T(8,128)(2,1)S(1)}, bf16[2,4,64,128]{3,2,1,0:T(8,128)(2,1)S(1)}, u32[]{:S(2)}, u32[]{:S(2)}) collective-permute-start(bf16[2,4,64,128]{3,2,1,0:T(8,128)(2,1)S(1)} %bitcast_dynamic-update-slice_fusion.10), channel_id=1, source_target_pairs={{0,3},{1,0},{2,1},{3,2},{4,7},{5,4},{6,5},{7,6},{8,11},{9,8},{10,9... | collective-permute-start | bytes 393224 | tf_op jit(solution)/shard_map/ppermute | solution.py:45
  45.6 14.2 %collective-permute-start.14 = (bf16[4,2,4,64,128]{4,3,2,1,0:T(8,128)(2,1)S(1)}, bf16[4,2,4,64,128]{4,3,2,1,0:T(8,128)(2,1)S(1)}, u32[]{:S(2)}, u32[]{:S(2)}) collective-permute-start(bf16[4,2,4,64,128]{4,3,2,1,0:T(8,128)(2,1)S(1)} %bitcast_dynamic-update-slice_fusion.4.refs_0_), channel_id=1, source_target_pairs={{0,8},{1,9},{2,10},{3,11},{4,12},{5,13},{6,14},{7,15},{8,16},{9,17... | collective-permute-start | bytes 1572872 | tf_op jit(solution)/shard_map/ppermute | solution.py:45
  46.6 13.2 %collective-permute-start.15 = (bf16[4,2,4,64,128]{4,3,2,1,0:T(8,128)(2,1)S(1)}, bf16[4,2,4,64,128]{4,3,2,1,0:T(8,128)(2,1)S(1)}, u32[]{:S(2)}, u32[]{:S(2)}) collective-permute-start(bf16[4,2,4,64,128]{4,3,2,1,0:T(8,128)(2,1)S(1)} %bitcast_dynamic-update-slice_fusion.4.refs_0_), channel_id=1, source_target_pairs={{0,24},{1,25},{2,26},{3,27},{4,28},{5,29},{6,30},{7,31},{8,0},{9,1... | collective-permute-start | bytes 1572872 | tf_op jit(solution)/shard_map/ppermute | solution.py:45
  50.5 3.7 %collective-permute-start.24 = (bf16[32,128]{1,0:T(8,128)(2,1)S(1)}, bf16[32,128]{1,0:T(8,128)(2,1)S(1)}, u32[]{:S(2)}, u32[]{:S(2)}) collective-permute-start(bf16[32,128]{1,0:T(8,128)(2,1)S(1)} %bitcast.114), channel_id=1, source_target_pairs={{0,1},{1,0},{2,3},{3,2},{4,5},{5,4},{6,7},{7,6},{8,9},{9,8},{10,11... | collective-permute-start | bytes 24584 | tf_op jit(solution)/shard_map/ppermute | solution.py:45
  54.3 5.4 %collective-permute-start.25 = (bf16[2,32,128]{2,1,0:T(8,128)(2,1)S(1)}, bf16[2,32,128]{2,1,0:T(8,128)(2,1)S(1)}, u32[]{:S(2)}, u32[]{:S(2)}) collective-permute-start(bf16[2,32,128]{2,1,0:T(8,128)(2,1)S(1)} %pad_maximum_fusion.5), channel_id=1, source_target_pairs={{0,2},{1,3},{2,0},{3,1},{4,6},{5,7},{6,4},{7,5},{8,10},{9,11},{10,... | collective-permute-start | bytes 49160 | tf_op jit(solution)/shard_map/ppermute | solution.py:45
  55.9 10.5 %collective-permute-start.12 = (bf16[64,4096]{1,0:T(8,128)(2,1)S(1)}, bf16[64,4096]{1,0:T(8,128)(2,1)S(1)}, u32[]{:S(2)}, u32[]{:S(2)}) collective-permute-start(bf16[64,4096]{1,0:T(8,128)(2,1)S(1)} %slice.52), channel_id=1, source_target_pairs={{0,8},{1,9},{2,10},{3,11},{4,12},{5,13},{6,14},{7,15},{8,16},{9,17... | collective-permute-start | bytes 1572872 | tf_op jit(solution)/shard_map/ppermute | solution.py:45
  56.0 9.9 %collective-permute-start.13 = (bf16[64,4096]{1,0:T(8,128)(2,1)S(1)}, bf16[64,4096]{1,0:T(8,128)(2,1)S(1)}, u32[]{:S(2)}, u32[]{:S(2)}) collective-permute-start(bf16[64,4096]{1,0:T(8,128)(2,1)S(1)} %slice.54), channel_id=1, source_target_pairs={{0,24},{1,25},{2,26},{3,27},{4,28},{5,29},{6,30},{7,31},{8,0},{9,1... | collective-permute-start | bytes 1572872 | tf_op jit(solution)/shard_map/ppermute | solution.py:45
  59.9 9.3 %collective-permute-start.16 = (bf16[2,2,4,64,128]{4,3,2,1,0:T(8,128)(2,1)S(1)}, bf16[2,2,4,64,128]{4,3,2,1,0:T(8,128)(2,1)S(1)}, u32[]{:S(2)}, u32[]{:S(2)}) collective-permute-start(bf16[2,2,4,64,128]{4,3,2,1,0:T(8,128)(2,1)S(1)} %slice.60), channel_id=1, source_target_pairs={{0,8},{1,9},{2,10},{3,11},{4,12},{5,13},{6,14},{7,15},{8,16},{9,17... | collective-permute-start | bytes 786440 | tf_op jit(solution)/shard_map/ppermute | solution.py:45
  60.0 9.2 %collective-permute-start.17 = (bf16[2,2,4,64,128]{4,3,2,1,0:T(8,128)(2,1)S(1)}, bf16[2,2,4,64,128]{4,3,2,1,0:T(8,128)(2,1)S(1)}, u32[]{:S(2)}, u32[]{:S(2)}) collective-permute-start(bf16[2,2,4,64,128]{4,3,2,1,0:T(8,128)(2,1)S(1)} %slice.61), channel_id=1, source_target_pairs={{0,24},{1,25},{2,26},{3,27},{4,28},{5,29},{6,30},{7,31},{8,0},{9,1... | collective-permute-start | bytes 786440 | tf_op jit(solution)/shard_map/ppermute | solution.py:45
  69.2 4.2 %collective-permute-start.18 = (bf16[4,2,4,64,128]{4,3,2,1,0:T(8,128)(2,1)S(1)}, bf16[4,2,4,64,128]{4,3,2,1,0:T(8,128)(2,1)S(1)}, u32[]{:S(2)}, u32[]{:S(2)}) collective-permute-start(bf16[4,2,4,64,128]{4,3,2,1,0:T(8,128)(2,1)S(1)} %bitcast_dynamic-update-slice_fusion.4.refs_0_), channel_id=1, source_target_pairs={{0,32},{1,33},{2,34},{3,35},{4,36},{5,37},{6,38},{7,39},{8,40},{9,... | collective-permute-start | bytes 1572872 | tf_op jit(solution)/shard_map/ppermute | solution.py:45
  69.2 4.2 %collective-permute-start.19 = (bf16[4,2,4,64,128]{4,3,2,1,0:T(8,128)(2,1)S(1)}, bf16[4,2,4,64,128]{4,3,2,1,0:T(8,128)(2,1)S(1)}, u32[]{:S(2)}, u32[]{:S(2)}) collective-permute-start(bf16[4,2,4,64,128]{4,3,2,1,0:T(8,128)(2,1)S(1)} %collective-permute-done.14.refs_1_), channel_id=1, source_target_pairs={{0,32},{1,33},{2,34},{3,35},{4,36},{5,37},{6,38},{7,39},{8,40},{9,... | collective-permute-start | bytes 1572872 | tf_op jit(solution)/shard_map/ppermute | solution.py:45
  69.7 3.7 %collective-permute-start.20 = (bf16[4,2,4,64,128]{4,3,2,1,0:T(8,128)(2,1)S(1)}, bf16[4,2,4,64,128]{4,3,2,1,0:T(8,128)(2,1)S(1)}, u32[]{:S(2)}, u32[]{:S(2)}) collective-permute-start(bf16[4,2,4,64,128]{4,3,2,1,0:T(8,128)(2,1)S(1)} %collective-permute-done.15.refs_2_), channel_id=1, source_target_pairs={{0,32},{1,33},{2,34},{3,35},{4,36},{5,37},{6,38},{7,39},{8,40},{9,... | collective-permute-start | bytes 1572872 | tf_op jit(solution)/shard_map/ppermute | solution.py:45
  70.2 2.8 %collective-permute-start.21 = (bf16[2,2,4,64,128]{4,3,2,1,0:T(8,128)(2,1)S(1)}, bf16[2,2,4,64,128]{4,3,2,1,0:T(8,128)(2,1)S(1)}, u32[]{:S(2)}, u32[]{:S(2)}) collective-permute-start(bf16[2,2,4,64,128]{4,3,2,1,0:T(8,128)(2,1)S(1)} %collective-permute-done.16.refs_3_), channel_id=1, source_target_pairs={{0,32},{1,33},{2,34},{3,35},{4,36},{5,37},{6,38},{7,39},{8,40},{9,... | collective-permute-start | bytes 786440 | tf_op jit(solution)/shard_map/ppermute | solution.py:45
  70.8 2.6 %collective-permute-start.22 = (bf16[2,2,4,64,128]{4,3,2,1,0:T(8,128)(2,1)S(1)}, bf16[2,2,4,64,128]{4,3,2,1,0:T(8,128)(2,1)S(1)}, u32[]{:S(2)}, u32[]{:S(2)}) collective-permute-start(bf16[2,2,4,64,128]{4,3,2,1,0:T(8,128)(2,1)S(1)} %collective-permute-done.17.refs_4_), channel_id=1, source_target_pairs={{0,32},{1,33},{2,34},{3,35},{4,36},{5,37},{6,38},{7,39},{8,40},{9,... | collective-permute-start | bytes 786440 | tf_op jit(solution)/shard_map/ppermute | solution.py:45
  80.9 16.5 %collective-permute-start.26 = (bf16[64,8192]{1,0:T(8,128)(2,1)S(1)}, bf16[64,8192]{1,0:T(8,128)(2,1)S(1)}, u32[]{:S(2)}, u32[]{:S(2)}) collective-permute-start(bf16[64,8192]{1,0:T(8,128)(2,1)S(1)} %get-tuple-element.50), channel_id=1, source_target_pairs={{0,16},{1,17},{2,18},{3,19},{4,20},{5,21},{6,22},{7,23},{8,24},{9,... | collective-permute-start | bytes 3145736 | tf_op jit(solution)/shard_map/ppermute | solution.py:45
  83.3 25.3 %collective-permute-start.27 = (bf16[64,8192]{1,0:T(8,128)(2,1)S(1)}, bf16[64,8192]{1,0:T(8,128)(2,1)S(1)}, u32[]{:S(2)}, u32[]{:S(2)}) collective-permute-start(bf16[64,8192]{1,0:T(8,128)(2,1)S(1)} %get-tuple-element.51), channel_id=1, source_target_pairs={{0,8},{1,9},{2,10},{3,11},{4,12},{5,13},{6,14},{7,15},{8,16},{9,17... | collective-permute-start | bytes 3145736 | tf_op jit(solution)/shard_map/ppermute | solution.py:45
  85.1 24.1 %collective-permute-start.28 = (bf16[64,8192]{1,0:T(8,128)(2,1)S(1)}, bf16[64,8192]{1,0:T(8,128)(2,1)S(1)}, u32[]{:S(2)}, u32[]{:S(2)}) collective-permute-start(bf16[64,8192]{1,0:T(8,128)(2,1)S(1)} %get-tuple-element.52), channel_id=1, source_target_pairs={{0,24},{1,25},{2,26},{3,27},{4,28},{5,29},{6,30},{7,31},{8,0},{9,1... | collective-permute-start | bytes 3145736 | tf_op jit(solution)/shard_map/ppermute | solution.py:45
  110.1 7.7 %collective-permute-start.29 = (bf16[16,8192]{1,0:T(8,128)(2,1)S(1)}, bf16[16,8192]{1,0:T(8,128)(2,1)S(1)}, u32[]{:S(2)}, u32[]{:S(2)}) collective-permute-start(bf16[16,8192]{1,0:T(8,128)(2,1)S(1)} %get-tuple-element.54), channel_id=1, source_target_pairs={{0,1},{1,2},{2,3},{3,0},{4,5},{5,6},{6,7},{7,4},{8,9},{9,10},{10,1... | collective-permute-start | bytes 786440 | tf_op jit(solution)/shard_map/ppermute | solution.py:45
  110.8 10.3 %collective-permute-start.30 = (bf16[16,8192]{1,0:T(8,128)(2,1)S(1)}, bf16[16,8192]{1,0:T(8,128)(2,1)S(1)}, u32[]{:S(2)}, u32[]{:S(2)}) collective-permute-start(bf16[16,8192]{1,0:T(8,128)(2,1)S(1)} %get-tuple-element.55), channel_id=1, source_target_pairs={{0,2},{1,3},{2,0},{3,1},{4,6},{5,7},{6,4},{7,5},{8,10},{9,11},{10,... | collective-permute-start | bytes 786440 | tf_op jit(solution)/shard_map/ppermute | solution.py:45
  114.0 7.5 %collective-permute-start.31 = (bf16[16,8192]{1,0:T(8,128)(2,1)S(1)}, bf16[16,8192]{1,0:T(8,128)(2,1)S(1)}, u32[]{:S(2)}, u32[]{:S(2)}) collective-permute-start(bf16[16,8192]{1,0:T(8,128)(2,1)S(1)} %get-tuple-element.56), channel_id=1, source_target_pairs={{0,3},{1,0},{2,1},{3,2},{4,7},{5,4},{6,5},{7,6},{8,11},{9,8},{10,9... | collective-permute-start | bytes 786440 | tf_op jit(solution)/shard_map/ppermute | solution.py:45
  121.6 5.1 %collective-permute-start.32 = (bf16[8,8192]{1,0:T(8,128)(2,1)S(1)}, bf16[8,8192]{1,0:T(8,128)(2,1)S(1)}, u32[]{:S(2)}, u32[]{:S(2)}) collective-permute-start(bf16[8,8192]{1,0:T(8,128)(2,1)S(1)} %fusion.26), channel_id=1, source_target_pairs={{0,4},{1,5},{2,6},{3,7},{4,0},{5,1},{6,2},{7,3},{8,12},{9,13},{10,... | collective-permute-start | bytes 393224 | tf_op jit(solution)/shard_map/ppermute | solution.py:45
  (7 other events, 92.7 us)
